TPU v7x, 32 devices: a whole 2x2x4 slice. The times are simulated.
32 devices in a mesh: seq: 8 (over z, x), section: 2 (over core), dp: 2 (over y).
Axes of the slice: x: 2, y: 2, z: 4, core: 2. Of those that a mesh axis runs over, the one named last changes fastest.
Arguments:
- queries: bfloat16 [2, 1024, 3584], P('section', 'seq', 'dp'), may hold values from -5 to 5
- key_vectors: bfloat16 [2, 1024, 3584], P('section', 'seq', 'dp'), may hold values from -5 to 5
- value_vectors: bfloat16 [2, 1024, 3584], P('section', 'seq', 'dp'), may hold values from -6 to 6
- out_grad: bfloat16 [2, 1024, 3584], P('section', 'seq', 'dp'), may hold values from -6 to 6
- doc_lengths: int32 [8], replicated, may hold values from 1 to 384, 1024 in all
Outputs:
- query_grad: bfloat16 [2, 1024, 3584], P('section', 'seq', 'dp')
- key_grad: bfloat16 [2, 1024, 3584], P('section', 'seq', 'dp')
- value_grad: bfloat16 [2, 1024, 3584], P('section', 'seq', 'dp')
Inputs may be any that keep to these rules, and one draw needn't show every extreme that they name: `doc_lengths`: the 8 lengths sum to 1024; the longest is exactly 384.
All inputs are finite; a program needn't handle non-finite values.
Results may differ from a plain program's by a relative error of at most 0.024.
Values may be sent and summed in bfloat16 or wider, within the bound.
No kernel may reach another device: no remote copies, remote signals or barrier semaphores. Data moves between devices by JAX's collectives and lax.ppermute only.
A program may use at most 192 MiB of HBM per device.

v0:
```python
import jax
import jax.numpy as jnp
from jax import lax
from jax.sharding import PartitionSpec as P

HEAD = 224


def pick_slot(stacked, slot):
    return lax.dynamic_index_in_dim(stacked, slot, 0, keepdims=False)


def put_slot(stacked, update, slot):
    return lax.dynamic_update_index_in_dim(stacked, update, slot, 0)


def shards(queries, key_vectors, value_vectors, out_grad, doc_lengths):
    local_rows = queries.shape[1]
    local_width = queries.shape[2]
    head_count = local_width // HEAD
    seq_size = lax.axis_size("seq")
    group = seq_size // head_count
    scaling = HEAD ** (-0.5)

    def spread(matrix):
        shaped = matrix.reshape(local_rows, head_count, 1, HEAD)
        copies = jnp.broadcast_to(shaped, (local_rows, head_count, group, HEAD))
        return copies.reshape(local_rows, seq_size * HEAD)

    query_head, key_head, value_head, cot_head = (
        lax.all_to_all(spread(queries), "seq", split_axis=1, concat_axis=0, tiled=True),
        lax.all_to_all(spread(key_vectors), "seq", split_axis=1, concat_axis=0, tiled=True),
        lax.all_to_all(spread(value_vectors), "seq", split_axis=1, concat_axis=0, tiled=True),
        lax.all_to_all(spread(out_grad), "seq", split_axis=1, concat_axis=0, tiled=True),
    )
    length = key_head.shape[0]
    member = lax.axis_index("seq") % group
    blocks = 2 * group
    block = length // blocks
    bounds = jnp.cumsum(doc_lengths)
    positions = jnp.arange(length, dtype=jnp.int32)
    doc_index = jnp.sum((positions[:, None] >= bounds[None, :]).astype(jnp.int32), axis=1)
    row_list = [member, blocks - 1 - member]
    query_list = []
    cot_list = []
    pos_list = []
    for which in range(2):
        offset = row_list[which] * block
        query_list.append(lax.dynamic_slice_in_dim(query_head, offset, block, 0))
        cot_list.append(lax.dynamic_slice_in_dim(cot_head, offset, block, 0))
        pos_list.append(offset + jnp.arange(block, dtype=jnp.int32))
    query_stack = jnp.stack(query_list)
    cot_stack = jnp.stack(cot_list)
    pos_stack = jnp.stack(pos_list)
    doc_stack = jnp.take(doc_index, pos_stack)
    plan = []
    for number in range(blocks + 1):
        first = number <= member
        slot = jnp.where(first, 0, 1).astype(jnp.int32)
        col_block = jnp.where(first, number, number - member - 1)
        flag = None
        plan.append((slot, col_block, flag))
    row_max = jnp.full((2, block), -jnp.inf, jnp.float32)
    row_sum = jnp.zeros((2, block), jnp.float32)
    stored = []
    for slot, col_block, flag in plan:

        def score_tile(carry, slot=slot, col_block=col_block):
            maxima, totals = carry
            query_rows = pick_slot(query_stack, slot)
            key_rows = lax.dynamic_slice_in_dim(key_head, col_block * block, block, 0)
            col_docs = lax.dynamic_slice_in_dim(doc_index, col_block * block, block, 0)
            col_positions = col_block * block + jnp.arange(block, dtype=jnp.int32)
            raw = jnp.dot(query_rows, key_rows.T, preferred_element_type=jnp.float32) * scaling
            allowed = (pick_slot(doc_stack, slot)[:, None] == col_docs[None, :]) & (
                pick_slot(pos_stack, slot)[:, None] >= col_positions[None, :]
            )
            scores = jnp.where(allowed, raw, -jnp.inf)
            before = pick_slot(maxima, slot)
            after = jnp.maximum(before, jnp.max(scores, axis=1))
            safe = jnp.where(jnp.isfinite(after), after, 0.0)
            total = pick_slot(totals, slot) * jnp.exp(before - safe) + jnp.sum(
                jnp.exp(scores - safe[:, None]), axis=1
            )
            return (scores, put_slot(maxima, after, slot), put_slot(totals, total, slot))

        scores, row_max, row_sum = score_tile((row_max, row_sum))
        stored.append(scores)

    def tile_weights(scores, slot):
        return (
            jnp.exp(scores - pick_slot(row_max, slot)[:, None]) / pick_slot(row_sum, slot)[:, None]
        )

    summed = jnp.zeros((2, block, HEAD), jnp.float32)
    for (slot, col_block, flag), scores in zip(plan, stored):

        def add_values(carry, slot=slot, col_block=col_block, scores=scores):
            rounded = tile_weights(scores, slot).astype(jnp.bfloat16)
            value_rows = lax.dynamic_slice_in_dim(value_head, col_block * block, block, 0)
            term = jnp.dot(rounded, value_rows, preferred_element_type=jnp.float32)
            return put_slot(carry, pick_slot(carry, slot) + term, slot)

        summed = add_values(summed)
    attended = summed.astype(jnp.bfloat16)
    row_dot = jnp.sum(cot_stack.astype(jnp.float32) * attended.astype(jnp.float32), axis=2)
    query_acc = jnp.zeros((2, block, HEAD), jnp.float32)
    key_acc = jnp.zeros((length, HEAD), jnp.float32)
    value_acc = jnp.zeros((length, HEAD), jnp.float32)
    for (slot, col_block, flag), scores in zip(plan, stored):

        def backward_tile(carry, slot=slot, col_block=col_block, scores=scores):
            query_sum, key_sum, value_sum = carry
            weights = tile_weights(scores, slot)
            rounded = weights.astype(jnp.bfloat16)
            query_rows = pick_slot(query_stack, slot)
            cot_rows = pick_slot(cot_stack, slot)
            start = col_block * block
            key_rows = lax.dynamic_slice_in_dim(key_head, start, block, 0)
            value_rows = lax.dynamic_slice_in_dim(value_head, start, block, 0)
            value_term = jnp.dot(rounded.T, cot_rows, preferred_element_type=jnp.float32)
            prob_grad = jnp.dot(cot_rows, value_rows.T, preferred_element_type=jnp.float32)
            score_grad = (
                weights * (prob_grad - pick_slot(row_dot, slot)[:, None]) * scaling
            ).astype(jnp.bfloat16)
            query_term = jnp.dot(score_grad, key_rows, preferred_element_type=jnp.float32)
            key_term = jnp.dot(score_grad.T, query_rows, preferred_element_type=jnp.float32)
            query_sum = put_slot(query_sum, pick_slot(query_sum, slot) + query_term, slot)
            key_sum = lax.dynamic_update_slice_in_dim(
                key_sum, lax.dynamic_slice_in_dim(key_sum, start, block, 0) + key_term, start, 0
            )
            value_sum = lax.dynamic_update_slice_in_dim(
                value_sum,
                lax.dynamic_slice_in_dim(value_sum, start, block, 0) + value_term,
                start,
                0,
            )
            return (query_sum, key_sum, value_sum)

        query_acc, key_acc, value_acc = backward_tile((query_acc, key_acc, value_acc))
    query_rounded = query_acc.astype(jnp.bfloat16)
    key_back, value_back = (
        lax.all_to_all(key_acc, "seq", split_axis=0, concat_axis=1, tiled=True),
        lax.all_to_all(value_acc, "seq", split_axis=0, concat_axis=1, tiled=True),
    )

    def settle(received):
        shaped = received.astype(jnp.float32).reshape(local_rows, head_count, group, HEAD)
        return jnp.sum(shaped, axis=2).reshape(1, local_rows, local_width).astype(jnp.bfloat16)

    query_full = jnp.zeros((length, HEAD), jnp.bfloat16)
    for which in range(2):
        query_full = lax.dynamic_update_slice_in_dim(
            query_full, query_rounded[which], row_list[which] * block, 0
        )
    query_back = lax.all_to_all(query_full, "seq", split_axis=0, concat_axis=1, tiled=True)
    query_out = settle(query_back)
    return (query_out, settle(key_back), settle(value_back))


def solution(mesh):
    return jax.shard_map(
        shards,
        mesh=mesh,
        in_specs=(
            P("section", "seq", "dp"),
            P("section", "seq", "dp"),
            P("section", "seq", "dp"),
            P("section", "seq", "dp"),
            P(),
        ),
        out_specs=(P("section", "seq", "dp"), P("section", "seq", "dp"), P("section", "seq", "dp")),
        check_vma=False,
    )
```

profile of v0, /device:TPU:0, one launch (start us, length us, event | category | flops | bytes accessed | tf_op | source)
XLA Modules:
  0.0 136.4 jit_solution(10478994382363630940)
XLA Ops:
  0.6 2.0 %copy.59 = bf16[1,128,1792]{1,2,0:T(8,128)(2,1)} copy(bf16[1,128,1792]{2,1,0:T(8,128)(2,1)} %param.5) | data formatting | bytes 917504 | tf_op args[0]
  2.6 7.4 %all-to-all-start = ((bf16[128,8,224]{0,2,1:T(8,128)(2,1)}), bf16[128,8,224]{0,2,1:T(8,128)(2,1)S(1)}, u32[]{:S(2)}, u32[]{:S(2)}) async-start(bf16[128,8,224]{0,2,1:T(8,128)(2,1)} %bitcast.5), calls=%async_computation | async-start | bytes 917504 | tf_op jit(solution)/shard_map/all_to_all | solution.py:31
  10.0 1.0 copy.61
  11.0 12.1 %all-to-all-done = bf16[128,8,224]{0,2,1:T(8,128)(2,1)S(1)} async-done(((bf16[128,8,224]{0,2,1:T(8,128)(2,1)}), bf16[128,8,224]{0,2,1:T(8,128)(2,1)S(1)}, u32[]{:S(2)}, u32[]{:S(2)}) %all-to-all-start) | async-done | bytes 458784 | tf_op jit(solution)/shard_map/all_to_all | solution.py:31
  23.1 3.8 %all-to-all-start.1 = ((bf16[128,8,224]{0,2,1:T(8,128)(2,1)}), bf16[128,8,224]{0,2,1:T(8,128)(2,1)S(1)}, u32[]{:S(2)}, u32[]{:S(2)}) async-start(bf16[128,8,224]{0,2,1:T(8,128)(2,1)} %bitcast.7), calls=%async_computation.1 | async-start | bytes 917504 | tf_op jit(solution)/shard_map/all_to_all | solution.py:32
  26.9 1.0 copy.65
  28.7 11.3 %all-to-all-done.1 = bf16[128,8,224]{0,2,1:T(8,128)(2,1)S(1)} async-done(((bf16[128,8,224]{0,2,1:T(8,128)(2,1)}), bf16[128,8,224]{0,2,1:T(8,128)(2,1)S(1)}, u32[]{:S(2)}, u32[]{:S(2)}) %all-to-all-start.1) | async-done | bytes 458784 | tf_op jit(solution)/shard_map/all_to_all | solution.py:32
  40.0 3.6 %all-to-all-start.3 = ((bf16[128,8,224]{0,2,1:T(8,128)(2,1)}), bf16[128,8,224]{0,2,1:T(8,128)(2,1)S(1)}, u32[]{:S(2)}, u32[]{:S(2)}) async-start(bf16[128,8,224]{0,2,1:T(8,128)(2,1)} %bitcast.11), calls=%async_computation.3 | async-start | bytes 917504 | tf_op jit(solution)/shard_map/all_to_all | solution.py:33
  43.8 4.5 %gather_fusion = s32[1024]{0:T(1024)S(1)} fusion(s32[1024]{0:T(1024)S(1)} %convert_reduce_fusion, s32[1024]{0:T(1024)S(1)} %broadcast_clamp_fusion), kind=kCustom, calls=%fused_computation | custom fusion | bytes 12288 | tf_op jit(solution)/shard_map/jit(_take)/gather | solution.py:55
  48.3 1.0 copy.63
  49.3 7.6 %all-to-all-done.3 = bf16[128,8,224]{0,2,1:T(8,128)(2,1)S(1)} async-done(((bf16[128,8,224]{0,2,1:T(8,128)(2,1)}), bf16[128,8,224]{0,2,1:T(8,128)(2,1)S(1)}, u32[]{:S(2)}, u32[]{:S(2)}) %all-to-all-start.3) | async-done | bytes 458784 | tf_op jit(solution)/shard_map/all_to_all | solution.py:33
  56.9 3.6 %all-to-all-start.2 = ((bf16[128,8,224]{0,2,1:T(8,128)(2,1)}), bf16[128,8,224]{0,2,1:T(8,128)(2,1)S(1)}, u32[]{:S(2)}, u32[]{:S(2)}) async-start(bf16[128,8,224]{0,2,1:T(8,128)(2,1)} %bitcast.9), calls=%async_computation.2 | async-start | bytes 917504 | tf_op jit(solution)/shard_map/all_to_all | solution.py:34
  61.5 12.4 %all-to-all-done.2 = bf16[128,8,224]{0,2,1:T(8,128)(2,1)S(1)} async-done(((bf16[128,8,224]{0,2,1:T(8,128)(2,1)}), bf16[128,8,224]{0,2,1:T(8,128)(2,1)S(1)}, u32[]{:S(2)}, u32[]{:S(2)}) %all-to-all-start.2) | async-done | bytes 458784 | tf_op jit(solution)/shard_map/all_to_all | solution.py:34
  73.8 0.9 slice_bitcast_fusion.9
  83.0 0.9 copy-done.5
  85.0 4.2 %all-to-all-start.4 = ((bf16[8,128,224]{1,2,0:T(8,128)(2,1)}), bf16[8,128,224]{1,2,0:T(8,128)(2,1)}, u32[]{:S(2)}, u32[]{:S(2)}) async-start(bf16[8,128,224]{1,2,0:T(8,128)(2,1)} %copy_bitcast_fusion.2), calls=%async_computation.4 | async-start | bytes 917504 | tf_op jit(solution)/shard_map/all_to_all | solution.py:156
  91.4 10.8 %all-to-all-done.4 = bf16[8,128,224]{1,2,0:T(8,128)(2,1)} async-done(((bf16[8,128,224]{1,2,0:T(8,128)(2,1)}), bf16[8,128,224]{1,2,0:T(8,128)(2,1)}, u32[]{:S(2)}, u32[]{:S(2)}) %all-to-all-start.4) | async-done | bytes 458784 | tf_op jit(solution)/shard_map/all_to_all | solution.py:156
  102.2 3.6 %all-to-all-start.5 = ((bf16[8,128,224]{1,2,0:T(8,128)(2,1)}), bf16[8,128,224]{1,2,0:T(8,128)(2,1)S(1)}, u32[]{:S(2)}, u32[]{:S(2)}) async-start(bf16[8,128,224]{1,2,0:T(8,128)(2,1)} %copy_bitcast_fusion.1), calls=%async_computation.5 | async-start | bytes 917504 | tf_op jit(solution)/shard_map/all_to_all | solution.py:143
  108.3 10.5 %all-to-all-done.5 = bf16[8,128,224]{1,2,0:T(8,128)(2,1)S(1)} async-done(((bf16[8,128,224]{1,2,0:T(8,128)(2,1)}), bf16[8,128,224]{1,2,0:T(8,128)(2,1)S(1)}, u32[]{:S(2)}, u32[]{:S(2)}) %all-to-all-start.5) | async-done | bytes 458784 | tf_op jit(solution)/shard_map/all_to_all | solution.py:143
  118.8 3.6 %all-to-all-start.6 = ((bf16[8,128,224]{1,2,0:T(8,128)(2,1)}), bf16[8,128,224]{1,2,0:T(8,128)(2,1)S(1)}, u32[]{:S(2)}, u32[]{:S(2)}) async-start(bf16[8,128,224]{1,2,0:T(8,128)(2,1)} %copy_bitcast_fusion), calls=%async_computation.6 | async-start | bytes 917504 | tf_op jit(solution)/shard_map/all_to_all | solution.py:144
  122.4 2.0 %copy.79 = bf16[1,128,1792]{2,1,0:T(8,128)(2,1)} copy(bf16[1,128,1792]{1,2,0:T(8,128)(2,1)} %bitcast.25) | data formatting | bytes 917504
  124.4 1.0 copy.80
  125.4 10.0 %all-to-all-done.6 = bf16[8,128,224]{1,2,0:T(8,128)(2,1)S(1)} async-done(((bf16[8,128,224]{1,2,0:T(8,128)(2,1)}), bf16[8,128,224]{1,2,0:T(8,128)(2,1)S(1)}, u32[]{:S(2)}, u32[]{:S(2)}) %all-to-all-start.6) | async-done | bytes 458784 | tf_op jit(solution)/shard_map/all_to_all | solution.py:144
  135.4 1.0 copy.81
  (83 shorter events, 15.5 us)
Async XLA Ops:
  2.6 7.4 %copy-start.9 = (bf16[1,128,1792]{2,1,0:T(8,128)(2,1)S(1)}, bf16[1,128,1792]{2,1,0:T(8,128)(2,1)}, u32[]{:S(2)}) copy-start(bf16[1,128,1792]{2,1,0:T(8,128)(2,1)} %param.6) | copy-start | bytes 1376260
  2.6 20.5 %all-to-all-start = ((bf16[128,8,224]{0,2,1:T(8,128)(2,1)}), bf16[128,8,224]{0,2,1:T(8,128)(2,1)S(1)}, u32[]{:S(2)}, u32[]{:S(2)}) async-start(bf16[128,8,224]{0,2,1:T(8,128)(2,1)} %bitcast.5), calls=%async_computation | async-start | bytes 917504 | tf_op jit(solution)/shard_map/all_to_all | solution.py:31
  23.1 3.8 %copy-start.10 = (bf16[1,128,1792]{2,1,0:T(8,128)(2,1)S(1)}, bf16[1,128,1792]{2,1,0:T(8,128)(2,1)}, u32[]{:S(2)}) copy-start(bf16[1,128,1792]{2,1,0:T(8,128)(2,1)} %param.7) | copy-start | bytes 1376260
  23.1 16.9 %all-to-all-start.1 = ((bf16[128,8,224]{0,2,1:T(8,128)(2,1)}), bf16[128,8,224]{0,2,1:T(8,128)(2,1)S(1)}, u32[]{:S(2)}, u32[]{:S(2)}) async-start(bf16[128,8,224]{0,2,1:T(8,128)(2,1)} %bitcast.7), calls=%async_computation.1 | async-start | bytes 917504 | tf_op jit(solution)/shard_map/all_to_all | solution.py:32
  27.8 0.7 copy-start.13
  40.0 16.9 %all-to-all-start.3 = ((bf16[128,8,224]{0,2,1:T(8,128)(2,1)}), bf16[128,8,224]{0,2,1:T(8,128)(2,1)S(1)}, u32[]{:S(2)}, u32[]{:S(2)}) async-start(bf16[128,8,224]{0,2,1:T(8,128)(2,1)} %bitcast.11), calls=%async_computation.3 | async-start | bytes 917504 | tf_op jit(solution)/shard_map/all_to_all | solution.py:33
  43.8 4.6 %copy-start.11 = (bf16[1,128,1792]{2,1,0:T(8,128)(2,1)S(1)}, bf16[1,128,1792]{2,1,0:T(8,128)(2,1)}, u32[]{:S(2)}) copy-start(bf16[1,128,1792]{2,1,0:T(8,128)(2,1)} %param.8) | copy-start | bytes 1376260
  56.9 16.9 %all-to-all-start.2 = ((bf16[128,8,224]{0,2,1:T(8,128)(2,1)}), bf16[128,8,224]{0,2,1:T(8,128)(2,1)S(1)}, u32[]{:S(2)}, u32[]{:S(2)}) async-start(bf16[128,8,224]{0,2,1:T(8,128)(2,1)} %bitcast.9), calls=%async_computation.2 | async-start | bytes 917504 | tf_op jit(solution)/shard_map/all_to_all | solution.py:34
  60.6 16.0 %copy-start.2 = (bf16[4,28,8,128]{3,2,1,0:T(8,128)(2,1)}, bf16[4,28,8,128]{3,2,1,0:T(8,128)(2,1)S(1)}, u32[]{:S(2)}) copy-start(bf16[4,28,8,128]{3,2,1,0:T(8,128)(2,1)S(1)} %get-tuple-element.22) | copy-start | bytes 688132
  60.7 14.5 %copy-start.4 = (bf16[4,28,8,128]{3,2,1,0:T(8,128)(2,1)}, bf16[4,28,8,128]{3,2,1,0:T(8,128)(2,1)S(1)}, u32[]{:S(2)}) copy-start(bf16[4,28,8,128]{3,2,1,0:T(8,128)(2,1)S(1)} %get-tuple-element.25) | copy-start | bytes 688132
  75.6 5.0 %copy-start = (f32[512,512]{0,1:T(8,128)}, f32[512,512]{0,1:T(8,128)S(1)}, u32[]{:S(2)}) copy-start(f32[512,512]{0,1:T(8,128)S(1)} %get-tuple-element.36) | copy-start | bytes 3145732
  78.0 0.9 copy-start.12
  79.3 0.9 copy-start.6
  80.7 0.9 copy-start.8
  82.9 0.9 copy-start.5
  85.0 4.3 %copy-start.3 = (bf16[4,28,8,128]{3,2,1,0:T(8,128)(2,1)S(1)}, bf16[4,28,8,128]{3,2,1,0:T(8,128)(2,1)}, u32[]{:S(2)}) copy-start(bf16[4,28,8,128]{3,2,1,0:T(8,128)(2,1)} %copy-done.2) | copy-start | bytes 688132
  85.0 17.2 %all-to-all-start.4 = ((bf16[8,128,224]{1,2,0:T(8,128)(2,1)}), bf16[8,128,224]{1,2,0:T(8,128)(2,1)}, u32[]{:S(2)}, u32[]{:S(2)}) async-start(bf16[8,128,224]{1,2,0:T(8,128)(2,1)} %copy_bitcast_fusion.2), calls=%async_computation.4 | async-start | bytes 917504 | tf_op jit(solution)/shard_map/all_to_all | solution.py:156
  91.4 14.5 %copy-start.7 = (bf16[4,28,8,128]{3,2,1,0:T(8,128)(2,1)S(1)}, bf16[4,28,8,128]{3,2,1,0:T(8,128)(2,1)}, u32[]{:S(2)}) copy-start(bf16[4,28,8,128]{3,2,1,0:T(8,128)(2,1)} %get-tuple-element.17) | copy-start | bytes 688132
  102.2 16.6 %all-to-all-start.5 = ((bf16[8,128,224]{1,2,0:T(8,128)(2,1)}), bf16[8,128,224]{1,2,0:T(8,128)(2,1)S(1)}, u32[]{:S(2)}, u32[]{:S(2)}) async-start(bf16[8,128,224]{1,2,0:T(8,128)(2,1)} %copy_bitcast_fusion.1), calls=%async_computation.5 | async-start | bytes 917504 | tf_op jit(solution)/shard_map/all_to_all | solution.py:143
  105.8 1.2 copy-start.1
  118.8 16.6 %all-to-all-start.6 = ((bf16[8,128,224]{1,2,0:T(8,128)(2,1)}), bf16[8,128,224]{1,2,0:T(8,128)(2,1)S(1)}, u32[]{:S(2)}, u32[]{:S(2)}) async-start(bf16[8,128,224]{1,2,0:T(8,128)(2,1)} %copy_bitcast_fusion), calls=%async_computation.6 | async-start | bytes 917504 | tf_op jit(solution)/shard_map/all_to_all | solution.py:144
where the time goes:
time: 137 us; the launch traced here: 136 us
  waiting for transfers between devices  74.7 us (55%)
  starting transfers between devices  29.9 us (22%)
  local copies, waits for them, and re-layouts  22.1 us (16%)
  matrix products  6.32 us (5%)
  other arithmetic  2.27 us (2%)
    unnamed x39, local copies, waits for them, and re-layouts  15.2 us
    all_to_all x1, waiting for transfers between devices, shards(): lax.all_to_all(spread(out_grad), 'seq', split_axis=1, concat_axis=0, tile...  12.4 us
    all_to_all x1, waiting for transfers between devices, shards(): lax.all_to_all(spread(queries), 'seq', split_axis=1, concat_axis=0, tiled...  12.1 us
    all_to_all x1, waiting for transfers between devices, shards(): lax.all_to_all(spread(key_vectors), 'seq', split_axis=1, concat_axis=0, t...  11.3 us
    all_to_all x1, waiting for transfers between devices, shards(): lax.all_to_all(query_full, 'seq', split_axis=0, concat_axis=1, tiled=True)  10.8 us
    all_to_all x1, waiting for transfers between devices, shards(): lax.all_to_all(key_acc, 'seq', split_axis=0, concat_axis=1, tiled=True)  10.5 us
    all_to_all x1, waiting for transfers between devices, shards(): lax.all_to_all(value_acc, 'seq', split_axis=0, concat_axis=1, tiled=True)  10 us
    all_to_all x1, waiting for transfers between devices, shards(): lax.all_to_all(spread(value_vectors), 'seq', split_axis=1, concat_axis=0,...  7.59 us
  transfers between devices with their start and end apart: 7, of which 7 were waited for; matrix products, arithmetic and copies ran while one was open for 11% of the time, Pallas kernels for 0%

commit v1 on v0

--- a/solution.py
+++ b/solution.py
@@ -1,9 +1,14 @@
+import functools
 import jax
 import jax.numpy as jnp
 from jax import lax
+from jax.experimental import pallas as pl
+from jax.experimental.pallas import tpu as pltpu
 from jax.sharding import PartitionSpec as P
 
 HEAD = 224
+LANES = 128
+FLOOR = -1e30
 
 
 def pick_slot(stacked, slot):
@@ -14,7 +19,7 @@
     return lax.dynamic_update_index_in_dim(stacked, update, slot, 0)
 
 
-def shards(queries, key_vectors, value_vectors, out_grad, doc_lengths):
+def spread_shards(queries, key_vectors, value_vectors, out_grad, doc_lengths):
     local_rows = queries.shape[1]
     local_width = queries.shape[2]
     head_count = local_width // HEAD
@@ -158,6 +163,278 @@
     return (query_out, settle(key_back), settle(value_back))
 
 
+def head_span(head):
+    low = head * HEAD // LANES * LANES
+    high = -(-(head + 1) * HEAD // LANES) * LANES
+    return low, high
+
+
+def head_mask(head):
+    low, high = head_span(head)
+    lane = lax.broadcasted_iota(jnp.int32, (1, high - low), 1) + low
+    inside = (lane >= head * HEAD) & (lane < (head + 1) * HEAD)
+    return inside.astype(jnp.float32).astype(jnp.bfloat16)
+
+
+def matmul(left, right, dims):
+    return lax.dot_general(left, right, (dims, ((), ())), preferred_element_type=jnp.float32)
+
+
+NT = ((1,), (1,))
+NN = ((1,), (0,))
+TN = ((0,), (0,))
+
+
+def tile_masks(place_ref, lengths_ref, rows):
+    me = place_ref[0]
+    odd = lax.rem(me, 2)
+    shape = (rows, rows)
+    row = lax.broadcasted_iota(jnp.int32, shape, 0)
+    col = lax.broadcasted_iota(jnp.int32, shape, 1)
+
+    def first_of(block):
+        position = block * rows + row
+        start = jnp.zeros_like(position)
+        bound = jnp.int32(0)
+        for doc in range(lengths_ref.shape[0]):
+            bound = bound + lengths_ref[doc]
+            start = jnp.where(position >= bound, bound, start)
+        return position, start
+
+    def allowed(query, key_block):
+        position, start = query
+        keys = key_block * rows + col
+        return (keys >= start) & (keys <= position)
+
+    own = first_of(me)
+    mate = first_of(me + 1 - 2 * odd)
+    third = first_of(me + 1)
+    return odd, (
+        allowed(own, me),
+        allowed(own, me - 2),
+        allowed(mate, me - 2 * odd),
+        allowed(third, me - 2),
+    )
+
+
+def scores_of(head, refs, odd, masks, scaling):
+    q_own, q_mate, q_third, o_own, o_mate, o_third, k_own, k_back, v_own, v_back = refs
+    low, high = head_span(head)
+    keep = head_mask(head)
+    is_odd = odd == 1
+
+    def read(ref):
+        return ref[0, :, low:high]
+
+    qs, qm = read(q_own), read(q_mate)
+    os, om = read(o_own), read(o_mate)
+    qt = jnp.where(is_odd, read(q_third), qm)
+    ot = jnp.where(is_odd, read(o_third), om)
+    ks, kb = read(k_own) * keep, read(k_back) * keep
+    vs, vb = read(v_own) * keep, read(v_back) * keep
+    km = jnp.where(is_odd, kb, ks)
+    vm = jnp.where(is_odd, vb, vs)
+    pairs = ((qs, ks, os, vs), (qs, kb, os, vb), (qm, km, om, vm), (qt, kb, ot, vb))
+    scores = [
+        jnp.where(mask, matmul(q, k, NT) * scaling, FLOOR) for (q, k, _, _), mask in zip(pairs, masks)
+    ]
+    grads = [matmul(o, v, NT) for _, _, o, v in pairs]
+    return scores, grads, (qs, qm, qt, os, om, ot, ks, kb, km), keep
+
+
+def stats_kernel(heads, scaling, place_ref, lengths_ref, *refs):
+    inputs, out_ref = refs[:10], refs[10]
+    rows = out_ref.shape[1]
+    odd, masks = tile_masks(place_ref, lengths_ref, rows)
+    lane = lax.broadcasted_iota(jnp.int32, (rows, LANES), 1)
+    result = jnp.zeros((rows, LANES), jnp.float32)
+    for head in range(heads):
+        scores, grads, _, _ = scores_of(head, inputs, odd, masks, scaling)
+        for group, tiles in enumerate(((0, 1), (2,), (3,))):
+            top = functools.reduce(
+                jnp.maximum, [jnp.max(scores[t], axis=1, keepdims=True) for t in tiles]
+            )
+            exps = [jnp.exp(scores[t] - top) for t in tiles]
+            total = sum(jnp.sum(e, axis=1, keepdims=True) for e in exps)
+            dots = sum(jnp.sum(e * grads[t], axis=1, keepdims=True) for e, t in zip(exps, tiles))
+            for kind, value in enumerate((top, total, dots)):
+                result = jnp.where(lane == (group * 3 + kind) * heads + head, value, result)
+    out_ref[0] = result
+
+
+def merge_stats(heads, odd, mine, mate, up, down, zig):
+    width = 3 * heads
+    lane = lax.broadcasted_iota(jnp.int32, mine.shape, 1)
+    is_odd = odd == 1
+
+    def to(value, source, target):
+        shift = (target - source) * width % LANES
+        return value if shift == 0 else pltpu.roll(value, shift, 1)
+
+    def by_group(own, partner, third):
+        return jnp.where(lane < width, own, jnp.where(lane < 2 * width, partner, third))
+
+    parts = (
+        mine,
+        by_group(
+            to(mate, 1, 0), to(mate, 0, 1), jnp.where(is_odd, to(zig, 0, 2), to(mate, 0, 2))
+        ),
+        by_group(
+            jnp.where(is_odd, to(mate, 2, 0), to(zig, 2, 0)),
+            jnp.where(is_odd, to(up, 2, 1), to(mine, 2, 1)),
+            jnp.where(is_odd, to(down, 1, 2), to(mine, 1, 2)),
+        ),
+    )
+    split = []
+    for part in parts:
+        total = pltpu.roll(part, LANES - heads, 1)
+        dots = pltpu.roll(part, LANES - 2 * heads, 1)
+        split.append((jnp.where(total > 0, part, FLOOR), total, dots))
+    top = functools.reduce(jnp.maximum, [s[0] for s in split])
+    scales = [jnp.exp(s[0] - top) for s in split]
+    total = sum(w * s[1] for w, s in zip(scales, split))
+    dots = sum(w * s[2] for w, s in zip(scales, split))
+    safe = jnp.where(total > 0, total, 1.0)
+    return top + jnp.log(safe), dots / safe
+
+
+def grads_kernel(heads, scaling, place_ref, lengths_ref, *refs):
+    inputs, stats, outs = refs[:10], refs[10:15], refs[15:]
+    rows = inputs[0].shape[1]
+    odd, masks = tile_masks(place_ref, lengths_ref, rows)
+    is_odd = odd == 1
+    shift, dots = merge_stats(heads, odd, *[ref[0] for ref in stats])
+    carry = [None] * len(outs)
+
+    def emit(head, values):
+        low, high = head_span(head)
+        last = head == heads - 1
+        for number, value in enumerate(values):
+            start = low
+            if carry[number] is not None:
+                outs[number][0, :, low : low + LANES] = (
+                    value[:, :LANES] + carry[number]
+                ).astype(jnp.bfloat16)
+                start = low + LANES
+            stop = high if last else high - LANES
+            if stop > start:
+                outs[number][0, :, start:stop] = value[:, start - low : stop - low].astype(
+                    jnp.bfloat16
+                )
+            carry[number] = None if last else value[:, high - LANES - low :]
+
+    for head in range(heads):
+        scores, grads, values, keep = scores_of(head, inputs, odd, masks, scaling)
+        qs, qm, qt, os, om, ot, ks, kb, km = values
+        groups = (0, 0, 1, 2)
+        weights, slopes = [], []
+        for tile in range(4):
+            at = groups[tile] * 3 * heads + head
+            weight = jnp.where(masks[tile], jnp.exp(scores[tile] - shift[:, at : at + 1]), 0.0)
+            slope = weight * (grads[tile] - dots[:, at : at + 1]) * scaling
+            weights.append(weight.astype(jnp.bfloat16))
+            slopes.append(slope.astype(jnp.bfloat16))
+        none = jnp.zeros_like(weights[0])
+
+        def to_keys(tiles, own, mate, third):
+            first = [tiles[0], jnp.where(is_odd, none, tiles[2])]
+            second = [tiles[1], tiles[3], jnp.where(is_odd, tiles[2], none)]
+            return (
+                matmul(jnp.concatenate(first, 0), jnp.concatenate([own, mate], 0), TN),
+                matmul(jnp.concatenate(second, 0), jnp.concatenate([own, third, mate], 0), TN),
+            )
+
+        qs, qm, qt = qs * keep, qm * keep, qt * keep
+        os, om, ot = os * keep, om * keep, ot * keep
+        query_own = matmul(
+            jnp.concatenate(slopes[:2], 1), jnp.concatenate([ks, kb], 0), NN
+        )
+        query_third = matmul(slopes[3], kb, NN)
+        query_mate = matmul(slopes[2], km, NN) + jnp.where(is_odd, 0.0, query_third)
+        key_own, key_back = to_keys(slopes, qs, qm, qt)
+        value_own, value_back = to_keys(weights, os, om, ot)
+        emit(
+            head,
+            (query_own, query_mate, query_third, key_own, key_back, value_own, value_back),
+        )
+
+
+def halo_shards(queries, key_vectors, value_vectors, out_grad, doc_lengths):
+    _, rows, width = queries.shape
+    seq_size = lax.axis_size("seq")
+    me = lax.axis_index("seq").astype(jnp.int32)
+    scaling = HEAD ** (-0.5)
+    chunks = 2
+    part = width // chunks
+    heads = part // HEAD
+    devices = range(seq_size)
+    mates = [(s, s ^ 1) for s in devices]
+    ahead = [(s, s + 2) for s in devices if s + 2 < seq_size]
+    behind = [(s, s - 2) for s in devices if s >= 2]
+    odd_behind = [(s, s - 2) for s in devices if s >= 2 and s % 2 == 1]
+    odd_next = [(s, s + 1) for s in devices if s % 2 == 1 and s + 1 < seq_size]
+    zigzag = odd_next + [(t, s) for s, t in odd_next]
+
+    def send(value, pairs):
+        return lax.ppermute(value, "seq", pairs)
+
+    q_mate = send(queries, mates)
+    o_mate = send(out_grad, mates)
+    k_back = send(key_vectors, ahead)
+    v_back = send(value_vectors, ahead)
+    q_third = send(q_mate, odd_behind)
+    o_third = send(o_mate, odd_behind)
+    tensors = (
+        queries, q_mate, q_third, out_grad, o_mate, o_third, key_vectors, k_back, value_vectors, v_back,
+    )
+    place = me[None]
+    smem = pl.BlockSpec(memory_space=pltpu.SMEM)
+    wide = pl.BlockSpec((1, rows, part), lambda step: (0, 0, step))
+    slim = pl.BlockSpec((1, rows, LANES), lambda step: (step, 0, 0))
+    tile_flops = 2 * 4 * rows * rows * chunks * heads * 320
+    stats = pl.pallas_call(
+        functools.partial(stats_kernel, heads, scaling),
+        grid=(chunks,),
+        in_specs=[smem, smem] + [wide] * 10,
+        out_specs=slim,
+        out_shape=jax.ShapeDtypeStruct((chunks, rows, LANES), jnp.float32),
+        cost_estimate=pl.CostEstimate(
+            flops=2 * tile_flops, bytes_accessed=20 * rows * width, transcendentals=0
+        ),
+    )(place, doc_lengths, *tensors)
+    others = (send(stats, mates), send(stats, ahead), send(stats, behind), send(stats, zigzag))
+    query_own, query_mate, query_third, key_own, key_back, value_own, value_back = pl.pallas_call(
+        functools.partial(grads_kernel, heads, scaling),
+        grid=(chunks,),
+        in_specs=[smem, smem] + [wide] * 10 + [slim] * 5,
+        out_specs=[wide] * 7,
+        out_shape=[jax.ShapeDtypeStruct((1, rows, width), jnp.bfloat16)] * 7,
+        cost_estimate=pl.CostEstimate(
+            flops=7 * tile_flops, bytes_accessed=34 * rows * width, transcendentals=0
+        ),
+    )(place, doc_lengths, *tensors, stats, *others)
+
+    def total(first, *rest):
+        value = first.astype(jnp.float32)
+        for term in rest:
+            value = value + term.astype(jnp.float32)
+        return value.astype(jnp.bfloat16)
+
+    value_ready = total(value_own, send(value_back, behind))
+    key_ready = total(key_own, send(key_back, behind))
+    query_ready = total(query_own, send(query_mate, mates), send(query_third, odd_next))
+    return query_ready, key_ready, value_ready
+
+
+def shards(queries, key_vectors, value_vectors, out_grad, doc_lengths):
+    _, rows, width = queries.shape
+    length = rows * lax.axis_size("seq")
+    longest = length * 3 // 8
+    fits = longest <= 3 * rows and lax.axis_size("seq") % 2 == 0 and width % (2 * LANES) == 0
+    plan = halo_shards if fits and width % (2 * HEAD) == 0 else spread_shards
+    return plan(queries, key_vectors, value_vectors, out_grad, doc_lengths)
+
+
 def solution(mesh):
     return jax.shard_map(
         shards,

time: 137 us -> 89.9 us (0.66)
  waiting for transfers between devices: 74.7 us -> 33.9 us
  local copies, waits for them, and re-layouts: 22.1 us -> 1.87 us
  Pallas kernels: 0 us -> 13.7 us
  matrix products: 6.32 us -> 0 us
  starting transfers between devices: 29.9 us -> 35.5 us
  other arithmetic: 2.27 us -> 3.75 us
    all_to_all x7 -> x0, waiting for transfers between devices: 74.7 us -> none  [the longest x1 12.4 us: shards(): lax.all_to_all(spread(out_grad), 'seq', split_axis=1, concat_axis=0, tile...]
    ppermute x0 -> x14, starting transfers between devices: none -> 35.5 us  [send(): return lax.ppermute(value, 'seq', pairs)]
    ppermute x0 -> x14, waiting for transfers between devices: none -> 33.9 us  [send(): return lax.ppermute(value, 'seq', pairs)]
    all_to_all x7 -> x0, starting transfers between devices: 29.9 us -> none  [the longest x1 7.38 us: shards(): lax.all_to_all(spread(queries), 'seq', split_axis=1, concat_axis=0, tiled...]
    pallas_call x0 -> x2, Pallas kernels: none -> 13.7 us  [the longest x1 8.48 us: halo_shards(): pl.pallas_call(functools.partial(grads_kernel, heads, scaling), grid=(chu...]
    unnamed x39 -> x24, local copies, waits for them, and re-layouts: 15.2 us -> 1.87 us
    dot_general x18 -> x0, matrix products: 6.32 us -> none  [the longest x3 1.3 us: score_tile(): jnp.dot(query_rows, key_rows.T, preferred_element_type=jnp.float32)]
    gather x2 -> x0, local copies, waits for them, and re-layouts: 4.54 us -> none  [shards(): doc_stack = jnp.take(doc_index, pos_stack)]
  transfers between devices with their start and end apart: 7 -> 14, of which waited for: 7 -> 8; matrix products, arithmetic and copies ran while one was open for 11% -> 3% of each run, Pallas kernels for 0% -> 0%
where the time goes in v1:
time: 89.9 us; the launch traced here: 89.5 us
  starting transfers between devices  35.5 us (39%)
  waiting for transfers between devices  33.9 us (38%)
  Pallas kernels  13.7 us (15%)
  other arithmetic  3.75 us (4%)
  local copies, waits for them, and re-layouts  1.87 us (2%)
    ppermute x14, starting transfers between devices, send(): return lax.ppermute(value, 'seq', pairs)  35.5 us
    ppermute x14, waiting for transfers between devices, send(): return lax.ppermute(value, 'seq', pairs)  33.9 us
    pallas_call x1, Pallas kernels, halo_shards(): pl.pallas_call(functools.partial(grads_kernel, heads, scaling), grid=(chu...  8.48 us
    pallas_call x1, Pallas kernels, halo_shards(): pl.pallas_call(functools.partial(stats_kernel, heads, scaling), grid=(chu...  5.17 us
    convert_element_type x3, other arithmetic, total(): return value.astype(jnp.bfloat16)  3.75 us
    unnamed x24, local copies, waits for them, and re-layouts  1.87 us
  transfers between devices with their start and end apart: 14, of which 8 were waited for; matrix products, arithmetic and copies ran while one was open for 3% of the time, Pallas kernels for 0%

profile of v1, /device:TPU:0, one launch (start us, length us, event | category | flops | bytes accessed | tf_op | source)
XLA Modules:
  0.0 89.5 jit_solution(4934566495671386043)
XLA Ops:
  0.6 3.0 %collective-permute-start = (bf16[1,128,1792]{2,1,0:T(8,128)(2,1)}, bf16[1,128,1792]{2,1,0:T(8,128)(2,1)S(1)}, u32[]{:S(2)}, u32[]{:S(2)}) collective-permute-start(bf16[1,128,1792]{2,1,0:T(8,128)(2,1)} %refs_0_.3), channel_id=1, source_target_pairs={{0,4},{4,0},{8,12},{12,8},{16,20},{20,16},{24,28},{28,24},{1,5},{5... | collective-permute-start | bytes 1376264 | tf_op jit(solution)/shard_map/ppermute | solution.py:379
  3.7 4.0 %collective-permute-start.4 = (bf16[1,128,1792]{2,1,0:T(8,128)(2,1)}, bf16[1,128,1792]{2,1,0:T(8,128)(2,1)S(1)}, u32[]{:S(2)}, u32[]{:S(2)}) collective-permute-start(bf16[1,128,1792]{2,1,0:T(8,128)(2,1)} %refs_6_.3), channel_id=1, source_target_pairs={{0,8},{4,12},{8,16},{12,20},{16,24},{20,28},{1,9},{5,13},{9,17},{1... | collective-permute-start | bytes 1376264 | tf_op jit(solution)/shard_map/ppermute | solution.py:379
  7.7 3.5 %collective-permute-start.5 = (bf16[1,128,1792]{2,1,0:T(8,128)(2,1)}, bf16[1,128,1792]{2,1,0:T(8,128)(2,1)S(1)}, u32[]{:S(2)}, u32[]{:S(2)}) collective-permute-start(bf16[1,128,1792]{2,1,0:T(8,128)(2,1)} %refs_8_.3), channel_id=1, source_target_pairs={{0,8},{4,12},{8,16},{12,20},{16,24},{20,28},{1,9},{5,13},{9,17},{1... | collective-permute-start | bytes 1376264 | tf_op jit(solution)/shard_map/ppermute | solution.py:379
  11.2 4.0 %collective-permute-done.refs_1_ = bf16[1,128,1792]{2,1,0:T(8,128)(2,1)S(1)} collective-permute-done((bf16[1,128,1792]{2,1,0:T(8,128)(2,1)}, bf16[1,128,1792]{2,1,0:T(8,128)(2,1)S(1)}, u32[]{:S(2)}, u32[]{:S(2)}) %collective-permute-start) | collective-permute-done | bytes 458784 | tf_op jit(solution)/shard_map/ppermute | solution.py:379
  15.2 0.7 collective-permute-start.1
  15.9 8.3 %collective-permute-done.2.refs_4_ = bf16[1,128,1792]{2,1,0:T(8,128)(2,1)S(1)} collective-permute-done((bf16[1,128,1792]{2,1,0:T(8,128)(2,1)}, bf16[1,128,1792]{2,1,0:T(8,128)(2,1)S(1)}, u32[]{:S(2)}, u32[]{:S(2)}) %collective-permute-start.2) | collective-permute-done | bytes 458784 | tf_op jit(solution)/shard_map/ppermute | solution.py:379
  24.2 0.7 collective-permute-start.3
  24.9 2.1 %collective-permute-done.5.refs_9_ = bf16[1,128,1792]{2,1,0:T(8,128)(2,1)S(1)} collective-permute-done((bf16[1,128,1792]{2,1,0:T(8,128)(2,1)}, bf16[1,128,1792]{2,1,0:T(8,128)(2,1)S(1)}, u32[]{:S(2)}, u32[]{:S(2)}) %collective-permute-start.5) | collective-permute-done | bytes 458784 | tf_op jit(solution)/shard_map/ppermute | solution.py:379
  27.0 0.8 copy-done.3
  28.1 5.2 %shard_map.76.refs_10_ = f32[2,128,128]{2,1,0:T(8,128)} custom-call(s32[1]{0:T(128)} %bitcast.place_ref, s32[8]{0:T(128)} %lengths_ref.3, bf16[1,128,1792]{2,1,0:T(8,128)(2,1)} %refs_0_.3, bf16[1,128,1792]{2,1,0:T(8,128)(2,1)} %copy-done, bf16[1,128,1792]{2,1,0:T(8,128)(2,1)} %copy-done.4, bf16[1,128,1792]{2,1,0:T(8,128)(2,1)} %refs_3_.3, ...), custom_call_target="tpu_custom_call" | custom-call | flops 671088640 | bytes 4587520 | tf_op jit(solution)/shard_map/pallas_call | solution.py:395
  33.3 0.7 collective-permute-start.9
  33.9 1.3 %collective-permute-start.8 = (f32[2,128,128]{2,1,0:T(8,128)}, f32[2,128,128]{2,1,0:T(8,128)S(1)}, u32[]{:S(2)}, u32[]{:S(2)}) collective-permute-start(f32[2,128,128]{2,1,0:T(8,128)} %shard_map.76.refs_10_), channel_id=1, source_target_pairs={{8,0},{12,4},{16,8},{20,12},{24,16},{28,20},{9,1},{13,5},{17,9},{2... | collective-permute-start | bytes 393224 | tf_op jit(solution)/shard_map/ppermute | solution.py:379
  35.2 17.2 %collective-permute-start.7 = (f32[2,128,128]{2,1,0:T(8,128)}, f32[2,128,128]{2,1,0:T(8,128)S(1)}, u32[]{:S(2)}, u32[]{:S(2)}) collective-permute-start(f32[2,128,128]{2,1,0:T(8,128)} %shard_map.76.refs_10_), channel_id=1, source_target_pairs={{0,8},{4,12},{8,16},{12,20},{16,24},{20,28},{1,9},{5,13},{9,17},{1... | collective-permute-start | bytes 393224 | tf_op jit(solution)/shard_map/ppermute | solution.py:379
  53.6 1.6 %collective-permute-done.7.refs_12_ = f32[2,128,128]{2,1,0:T(8,128)S(1)} collective-permute-done((f32[2,128,128]{2,1,0:T(8,128)}, f32[2,128,128]{2,1,0:T(8,128)S(1)}, u32[]{:S(2)}, u32[]{:S(2)}) %collective-permute-start.7) | collective-permute-done | bytes 131104 | tf_op jit(solution)/shard_map/ppermute | solution.py:379
  55.2 2.4 %collective-permute-done.6.refs_11_ = f32[2,128,128]{2,1,0:T(8,128)S(1)} collective-permute-done((f32[2,128,128]{2,1,0:T(8,128)}, f32[2,128,128]{2,1,0:T(8,128)S(1)}, u32[]{:S(2)}, u32[]{:S(2)}) %collective-permute-start.6) | collective-permute-done | bytes 131104 | tf_op jit(solution)/shard_map/ppermute | solution.py:379
  58.3 8.5 %shard_map.77 = (bf16[1,128,1792]{2,1,0:T(8,128)(2,1)}, bf16[1,128,1792]{2,1,0:T(8,128)(2,1)}, bf16[1,128,1792]{2,1,0:T(8,128)(2,1)}, bf16[1,128,1792]{2,1,0:T(8...) custom-call(s32[1]{0:T(128)} %bitcast.place_ref, ...), custom_call_target="tpu_custom_call" | custom-call | flops 2348810240 | bytes 7798784 | tf_op jit(solution)/shard_map/pallas_call | solution.py:406
  66.8 1.3 %collective-permute-start.12 = (bf16[1,128,1792]{2,1,0:T(8,128)(2,1)}, bf16[1,128,1792]{2,1,0:T(8,128)(2,1)S(1)}, u32[]{:S(2)}, u32[]{:S(2)}) collective-permute-start(bf16[1,128,1792]{2,1,0:T(8,128)(2,1)} %get-tuple-element.14), channel_id=1, source_target_pairs={{8,0},{12,4},{16,8},{20,12},{24,16},{28,20},{9,1},{13,5},{17,9},{2... | collective-permute-start | bytes 1376264 | tf_op jit(solution)/shard_map/ppermute | solution.py:379
  68.7 0.7 collective-permute-start.11
  69.4 1.3 %collective-permute-start.13 = (bf16[1,128,1792]{2,1,0:T(8,128)(2,1)}, bf16[1,128,1792]{2,1,0:T(8,128)(2,1)S(1)}, u32[]{:S(2)}, u32[]{:S(2)}) collective-permute-start(bf16[1,128,1792]{2,1,0:T(8,128)(2,1)} %get-tuple-element.16), channel_id=1, source_target_pairs={{8,0},{12,4},{16,8},{20,12},{24,16},{28,20},{9,1},{13,5},{17,9},{2... | collective-permute-start | bytes 1376264 | tf_op jit(solution)/shard_map/ppermute | solution.py:379
  70.7 11.6 %collective-permute-done.12 = bf16[1,128,1792]{2,1,0:T(8,128)(2,1)S(1)} collective-permute-done((bf16[1,128,1792]{2,1,0:T(8,128)(2,1)}, bf16[1,128,1792]{2,1,0:T(8,128)(2,1)S(1)}, u32[]{:S(2)}, u32[]{:S(2)}) %collective-permute-start.12) | collective-permute-done | bytes 458784 | tf_op jit(solution)/shard_map/ppermute | solution.py:379
  82.3 1.9 %add_convert_fusion.1 = bf16[1,128,1792]{2,1,0:T(8,128)(2,1)} fusion(bf16[1,128,1792]{2,1,0:T(8,128)(2,1)S(1)} %collective-permute-done.12, bf16[1,128,1792]{2,1,0:T(8,128)(2,1)} %get-tuple-element.13), kind=kLoop, calls=%fused_computation.1 | loop fusion | flops 917504 | bytes 1376256 | tf_op jit(solution)/shard_map/convert_element_type | solution.py:421
  84.3 3.2 %collective-permute-done.13 = bf16[1,128,1792]{2,1,0:T(8,128)(2,1)S(1)} collective-permute-done((bf16[1,128,1792]{2,1,0:T(8,128)(2,1)}, bf16[1,128,1792]{2,1,0:T(8,128)(2,1)S(1)}, u32[]{:S(2)}, u32[]{:S(2)}) %collective-permute-start.13) | collective-permute-done | bytes 458784 | tf_op jit(solution)/shard_map/ppermute | solution.py:379
  87.5 0.9 add_convert_fusion
  88.5 0.9 %add_convert_fusion.2 = bf16[1,128,1792]{2,1,0:T(8,128)(2,1)} fusion(bf16[1,128,1792]{2,1,0:T(8,128)(2,1)S(1)} %collective-permute-done.11, bf16[1,128,1792]{2,1,0:T(8,128)(2,1)S(1)} %collective-permute-done.10, bf16[1,128,1792]{2,1,0:T(8,128)(2,1)S(1)} %copy-done.6), kind=kLoop, calls=%fused_computation.2 | loop fusion | flops 1376256 | bytes 1835008 | tf_op jit(solution)/shard_map/convert_element_type | solution.py:421
  (33 shorter events, 3.0 us)
Async XLA Ops:
  0.6 14.6 %collective-permute-start = (bf16[1,128,1792]{2,1,0:T(8,128)(2,1)}, bf16[1,128,1792]{2,1,0:T(8,128)(2,1)S(1)}, u32[]{:S(2)}, u32[]{:S(2)}) collective-permute-start(bf16[1,128,1792]{2,1,0:T(8,128)(2,1)} %refs_0_.3), channel_id=1, source_target_pairs={{0,4},{4,0},{8,12},{12,8},{16,20},{20,16},{24,28},{28,24},{1,5},{5... | collective-permute-start | bytes 1376264 | tf_op jit(solution)/shard_map/ppermute | solution.py:379
  3.6 20.6 %collective-permute-start.2 = (bf16[1,128,1792]{2,1,0:T(8,128)(2,1)}, bf16[1,128,1792]{2,1,0:T(8,128)(2,1)S(1)}, u32[]{:S(2)}, u32[]{:S(2)}) collective-permute-start(bf16[1,128,1792]{2,1,0:T(8,128)(2,1)} %refs_3_.3), channel_id=1, source_target_pairs={{0,4},{4,0},{8,12},{12,8},{16,20},{20,16},{24,28},{28,24},{1,5},{5... | collective-permute-start | bytes 1376264 | tf_op jit(solution)/shard_map/ppermute | solution.py:379
  3.7 21.2 %collective-permute-start.4 = (bf16[1,128,1792]{2,1,0:T(8,128)(2,1)}, bf16[1,128,1792]{2,1,0:T(8,128)(2,1)S(1)}, u32[]{:S(2)}, u32[]{:S(2)}) collective-permute-start(bf16[1,128,1792]{2,1,0:T(8,128)(2,1)} %refs_6_.3), channel_id=1, source_target_pairs={{0,8},{4,12},{8,16},{12,20},{16,24},{20,28},{1,9},{5,13},{9,17},{1... | collective-permute-start | bytes 1376264 | tf_op jit(solution)/shard_map/ppermute | solution.py:379
  7.7 19.3 %collective-permute-start.5 = (bf16[1,128,1792]{2,1,0:T(8,128)(2,1)}, bf16[1,128,1792]{2,1,0:T(8,128)(2,1)S(1)}, u32[]{:S(2)}, u32[]{:S(2)}) collective-permute-start(bf16[1,128,1792]{2,1,0:T(8,128)(2,1)} %refs_8_.3), channel_id=1, source_target_pairs={{0,8},{4,12},{8,16},{12,20},{16,24},{20,28},{1,9},{5,13},{9,17},{1... | collective-permute-start | bytes 1376264 | tf_op jit(solution)/shard_map/ppermute | solution.py:379
  15.2 11.8 %copy-start = (bf16[1,128,1792]{2,1,0:T(8,128)(2,1)}, bf16[1,128,1792]{2,1,0:T(8,128)(2,1)S(1)}, u32[]{:S(2)}) copy-start(bf16[1,128,1792]{2,1,0:T(8,128)(2,1)S(1)} %collective-permute-done.refs_1_) | copy-start | bytes 1376260
  15.2 11.8 %collective-permute-start.1 = (bf16[1,128,1792]{2,1,0:T(8,128)(2,1)S(1)}, bf16[1,128,1792]{2,1,0:T(8,128)(2,1)S(1)}, u32[]{:S(2)}, u32[]{:S(2)}) collective-permute-start(bf16[1,128,1792]{2,1,0:T(8,128)(2,1)S(1)} %collective-permute-done.refs_1_), channel_id=1, source_target_pairs={{12,4},{20,12},{28,20},{13,5},{21,13},{29,21},{14,6},{22,14},{30,2... | collective-permute-start | bytes 1376264 | tf_op jit(solution)/shard_map/ppermute | solution.py:379
  24.2 2.8 %copy-start.1 = (bf16[1,128,1792]{2,1,0:T(8,128)(2,1)}, bf16[1,128,1792]{2,1,0:T(8,128)(2,1)S(1)}, u32[]{:S(2)}) copy-start(bf16[1,128,1792]{2,1,0:T(8,128)(2,1)S(1)} %collective-permute-done.2.refs_4_) | copy-start | bytes 1376260
  24.2 2.8 %collective-permute-start.3 = (bf16[1,128,1792]{2,1,0:T(8,128)(2,1)S(1)}, bf16[1,128,1792]{2,1,0:T(8,128)(2,1)S(1)}, u32[]{:S(2)}, u32[]{:S(2)}) collective-permute-start(bf16[1,128,1792]{2,1,0:T(8,128)(2,1)S(1)} %collective-permute-done.2.refs_4_), channel_id=1, source_target_pairs={{12,4},{20,12},{28,20},{13,5},{21,13},{29,21},{14,6},{22,14},{30,2... | collective-permute-start | bytes 1376264 | tf_op jit(solution)/shard_map/ppermute | solution.py:379
  24.9 2.1 %copy-start.2 = (bf16[1,128,1792]{2,1,0:T(8,128)(2,1)}, bf16[1,128,1792]{2,1,0:T(8,128)(2,1)S(1)}, u32[]{:S(2)}) copy-start(bf16[1,128,1792]{2,1,0:T(8,128)(2,1)S(1)} %collective-permute-done.4.refs_7_) | copy-start | bytes 1376260
  27.0 0.9 %copy-start.4 = (bf16[1,128,1792]{2,1,0:T(8,128)(2,1)}, bf16[1,128,1792]{2,1,0:T(8,128)(2,1)S(1)}, u32[]{:S(2)}) copy-start(bf16[1,128,1792]{2,1,0:T(8,128)(2,1)S(1)} %collective-permute-done.1.refs_2_) | copy-start | bytes 1376260
  27.0 1.1 %copy-start.5 = (bf16[1,128,1792]{2,1,0:T(8,128)(2,1)}, bf16[1,128,1792]{2,1,0:T(8,128)(2,1)S(1)}, u32[]{:S(2)}) copy-start(bf16[1,128,1792]{2,1,0:T(8,128)(2,1)S(1)} %collective-permute-done.3.refs_5_) | copy-start | bytes 1376260
  33.3 19.8 %collective-permute-start.9 = (f32[2,128,128]{2,1,0:T(8,128)}, f32[2,128,128]{2,1,0:T(8,128)S(1)}, u32[]{:S(2)}, u32[]{:S(2)}) collective-permute-start(f32[2,128,128]{2,1,0:T(8,128)} %shard_map.76.refs_10_), channel_id=1, source_target_pairs={{4,8},{12,16},{20,24},{8,4},{16,12},{24,20},{5,9},{13,17},{21,25},... | collective-permute-start | bytes 393224 | tf_op jit(solution)/shard_map/ppermute | solution.py:379
  33.9 19.7 %collective-permute-start.8 = (f32[2,128,128]{2,1,0:T(8,128)}, f32[2,128,128]{2,1,0:T(8,128)S(1)}, u32[]{:S(2)}, u32[]{:S(2)}) collective-permute-start(f32[2,128,128]{2,1,0:T(8,128)} %shard_map.76.refs_10_), channel_id=1, source_target_pairs={{8,0},{12,4},{16,8},{20,12},{24,16},{28,20},{9,1},{13,5},{17,9},{2... | collective-permute-start | bytes 393224 | tf_op jit(solution)/shard_map/ppermute | solution.py:379
  35.2 20.0 %collective-permute-start.7 = (f32[2,128,128]{2,1,0:T(8,128)}, f32[2,128,128]{2,1,0:T(8,128)S(1)}, u32[]{:S(2)}, u32[]{:S(2)}) collective-permute-start(f32[2,128,128]{2,1,0:T(8,128)} %shard_map.76.refs_10_), channel_id=1, source_target_pairs={{0,8},{4,12},{8,16},{12,20},{16,24},{20,28},{1,9},{5,13},{9,17},{1... | collective-permute-start | bytes 393224 | tf_op jit(solution)/shard_map/ppermute | solution.py:379
  52.4 5.2 %collective-permute-start.6 = (f32[2,128,128]{2,1,0:T(8,128)}, f32[2,128,128]{2,1,0:T(8,128)S(1)}, u32[]{:S(2)}, u32[]{:S(2)}) collective-permute-start(f32[2,128,128]{2,1,0:T(8,128)} %shard_map.76.refs_10_), channel_id=1, source_target_pairs={{0,4},{4,0},{8,12},{12,8},{16,20},{20,16},{24,28},{28,24},{1,5},{5... | collective-permute-start | bytes 393224 | tf_op jit(solution)/shard_map/ppermute | solution.py:379
  53.0 4.6 %copy-start.8 = (f32[2,128,128]{2,1,0:T(8,128)}, f32[2,128,128]{2,1,0:T(8,128)S(1)}, u32[]{:S(2)}) copy-start(f32[2,128,128]{2,1,0:T(8,128)S(1)} %collective-permute-done.9.refs_14_) | copy-start | bytes 393220
  53.6 4.0 %copy-start.9 = (f32[2,128,128]{2,1,0:T(8,128)}, f32[2,128,128]{2,1,0:T(8,128)S(1)}, u32[]{:S(2)}) copy-start(f32[2,128,128]{2,1,0:T(8,128)S(1)} %collective-permute-done.8.refs_13_) | copy-start | bytes 393220
  55.2 2.4 %copy-start.10 = (f32[2,128,128]{2,1,0:T(8,128)}, f32[2,128,128]{2,1,0:T(8,128)S(1)}, u32[]{:S(2)}) copy-start(f32[2,128,128]{2,1,0:T(8,128)S(1)} %collective-permute-done.7.refs_12_) | copy-start | bytes 393220
  66.8 15.6 %collective-permute-start.12 = (bf16[1,128,1792]{2,1,0:T(8,128)(2,1)}, bf16[1,128,1792]{2,1,0:T(8,128)(2,1)S(1)}, u32[]{:S(2)}, u32[]{:S(2)}) collective-permute-start(bf16[1,128,1792]{2,1,0:T(8,128)(2,1)} %get-tuple-element.14), channel_id=1, source_target_pairs={{8,0},{12,4},{16,8},{20,12},{24,16},{28,20},{9,1},{13,5},{17,9},{2... | collective-permute-start | bytes 1376264 | tf_op jit(solution)/shard_map/ppermute | solution.py:379
  68.1 20.3 %collective-permute-start.10 = (bf16[1,128,1792]{2,1,0:T(8,128)(2,1)}, bf16[1,128,1792]{2,1,0:T(8,128)(2,1)S(1)}, u32[]{:S(2)}, u32[]{:S(2)}) collective-permute-start(bf16[1,128,1792]{2,1,0:T(8,128)(2,1)} %get-tuple-element.11), channel_id=1, source_target_pairs={{0,4},{4,0},{8,12},{12,8},{16,20},{20,16},{24,28},{28,24},{1,5},{5... | collective-permute-start | bytes 1376264 | tf_op jit(solution)/shard_map/ppermute | solution.py:379
  68.7 19.7 %collective-permute-start.11 = (bf16[1,128,1792]{2,1,0:T(8,128)(2,1)}, bf16[1,128,1792]{2,1,0:T(8,128)(2,1)S(1)}, u32[]{:S(2)}, u32[]{:S(2)}) collective-permute-start(bf16[1,128,1792]{2,1,0:T(8,128)(2,1)} %get-tuple-element.12), channel_id=1, source_target_pairs={{4,8},{12,16},{20,24},{5,9},{13,17},{21,25},{6,10},{14,18},{22,26}... | collective-permute-start | bytes 1376264 | tf_op jit(solution)/shard_map/ppermute | solution.py:379
  69.4 18.1 %collective-permute-start.13 = (bf16[1,128,1792]{2,1,0:T(8,128)(2,1)}, bf16[1,128,1792]{2,1,0:T(8,128)(2,1)S(1)}, u32[]{:S(2)}, u32[]{:S(2)}) collective-permute-start(bf16[1,128,1792]{2,1,0:T(8,128)(2,1)} %get-tuple-element.16), channel_id=1, source_target_pairs={{8,0},{12,4},{16,8},{20,12},{24,16},{28,20},{9,1},{13,5},{17,9},{2... | collective-permute-start | bytes 1376264 | tf_op jit(solution)/shard_map/ppermute | solution.py:379
  82.3 5.2 %copy-start.7 = (bf16[1,128,1792]{2,1,0:T(8,128)(2,1)S(1)}, bf16[1,128,1792]{2,1,0:T(8,128)(2,1)}, u32[]{:S(2)}) copy-start(bf16[1,128,1792]{2,1,0:T(8,128)(2,1)} %get-tuple-element.15) | copy-start | bytes 1376260
  87.5 1.0 %copy-start.6 = (bf16[1,128,1792]{2,1,0:T(8,128)(2,1)S(1)}, bf16[1,128,1792]{2,1,0:T(8,128)(2,1)}, u32[]{:S(2)}) copy-start(bf16[1,128,1792]{2,1,0:T(8,128)(2,1)} %get-tuple-element.10) | copy-start | bytes 1376260
  (2 other events, 1.5 us)

commit v2 on v0

--- a/solution.py
+++ b/solution.py
@@ -1,9 +1,14 @@
+import functools
 import jax
 import jax.numpy as jnp
 from jax import lax
+from jax.experimental import pallas as pl
+from jax.experimental.pallas import tpu as pltpu
 from jax.sharding import PartitionSpec as P
 
 HEAD = 224
+LANES = 128
+FLOOR = -1e30
 
 
 def pick_slot(stacked, slot):
@@ -14,7 +19,7 @@
     return lax.dynamic_update_index_in_dim(stacked, update, slot, 0)
 
 
-def shards(queries, key_vectors, value_vectors, out_grad, doc_lengths):
+def spread_shards(queries, key_vectors, value_vectors, out_grad, doc_lengths):
     local_rows = queries.shape[1]
     local_width = queries.shape[2]
     head_count = local_width // HEAD
@@ -158,6 +163,335 @@
     return (query_out, settle(key_back), settle(value_back))
 
 
+NT = ((1,), (1,))
+NN = ((1,), (0,))
+TN = ((0,), (0,))
+KINDS = 3
+SLOT = 16
+
+
+def head_span(head):
+    low = head * HEAD // LANES * LANES
+    high = -(-(head + 1) * HEAD // LANES) * LANES
+    return low, high
+
+
+def head_mask(head):
+    low, high = head_span(head)
+    lane = lax.broadcasted_iota(jnp.int32, (1, high - low), 1) + low
+    inside = (lane >= head * HEAD) & (lane < (head + 1) * HEAD)
+    return inside.astype(jnp.float32).astype(jnp.bfloat16)
+
+
+def matmul(left, right, dims):
+    return lax.dot_general(left, right, (dims, ((), ())), preferred_element_type=jnp.float32)
+
+
+def stack_rows(*values):
+    return jnp.concatenate(values, axis=0)
+
+
+def allowed(lengths_ref, rows, query_block, key_block):
+    shape = (rows, rows)
+    position = query_block * rows + lax.broadcasted_iota(jnp.int32, shape, 0)
+    keys = key_block * rows + lax.broadcasted_iota(jnp.int32, shape, 1)
+    start = jnp.zeros_like(position)
+    bound = jnp.int32(0)
+    for doc in range(lengths_ref.shape[0]):
+        bound = bound + lengths_ref[doc]
+        start = jnp.where(position >= bound, bound, start)
+    return (keys >= start) & (keys <= position)
+
+
+def even_plan(lengths_ref, rows, me):
+    def pair(query, key):
+        return allowed(lengths_ref, rows, query, key)
+
+    mask = stack_rows(
+        jnp.concatenate([pair(me, me), pair(me, me - 2)], axis=1),
+        jnp.concatenate([pair(me + 1, me), pair(me + 1, me - 2)], axis=1),
+    )
+    return (((0, 1), (0, 1), mask),)
+
+
+def odd_plan(lengths_ref, rows, me):
+    def pair(query, key):
+        return allowed(lengths_ref, rows, query, key)
+
+    mask = stack_rows(pair(me, me - 2), pair(me - 1, me - 2), pair(me + 1, me - 2))
+    return (((0,), (0,), pair(me, me)), ((0, 1, 2), (1,), mask))
+
+
+def gather_head(ref, number, slots, low, high):
+    return stack_rows(*[ref[slot][number, :, low:high] for slot in slots])
+
+
+def tile_values(plan, head, queries, keys, scaling):
+    low, high = head_span(head)
+    keep = head_mask(head)
+    out = []
+    for query_slots, key_slots, mask in plan:
+        q = gather_head(queries, 0, query_slots, low, high)
+        o = gather_head(queries, 1, query_slots, low, high)
+        k = gather_head(keys, 0, key_slots, low, high) * keep
+        v = gather_head(keys, 1, key_slots, low, high) * keep
+        scores = jnp.where(mask, matmul(q, k, NT) * scaling, FLOOR)
+        out.append((q, o, k, scores, matmul(o, v, NT)))
+    return out, keep
+
+
+def row_part(value, slot, rows):
+    return value[slot * rows : (slot + 1) * rows]
+
+
+def stats_kernel(heads, scaling, place_ref, lengths_ref, own, mate, third, key_own, key_back, out_ref):
+    rows = own.shape[1]
+    me = place_ref[0]
+    total = out_ref.shape[0]
+    lane = lax.broadcasted_iota(jnp.int32, (rows, LANES), 1)
+    queries, keys = (own, mate, third), (key_own, key_back)
+    out_ref[...] = jnp.zeros_like(out_ref)
+
+    def collect(plan, groups):
+        results = [jnp.zeros((rows, LANES), jnp.float32) for _ in range(groups)]
+        for head in range(heads):
+            tiles, _ = tile_values(plan, head, queries, keys, scaling)
+            parts = [[] for _ in range(groups)]
+            for (slots, _, _), (_, _, _, scores, grads) in zip(plan, tiles):
+                for number, slot in enumerate(slots):
+                    parts[slot].append((row_part(scores, number, rows), row_part(grads, number, rows)))
+            for group, pieces in enumerate(parts):
+                top = functools.reduce(
+                    jnp.maximum, [jnp.max(s, axis=1, keepdims=True) for s, _ in pieces]
+                )
+                exps = [jnp.exp(s - top) for s, _ in pieces]
+                sums = sum(jnp.sum(e, axis=1, keepdims=True) for e in exps)
+                dots = sum(
+                    jnp.sum(e * g, axis=1, keepdims=True) for e, (_, g) in zip(exps, pieces)
+                )
+                for kind, value in enumerate((top, sums, dots)):
+                    results[group] = jnp.where(lane == kind * heads + head, value, results[group])
+        return [result.T[:SLOT] for result in results]
+
+    @pl.when(lax.rem(me, 2) == 0)
+    def _():
+        own_stats, mate_stats = collect(even_plan(lengths_ref, rows, me), 2)
+        out_ref[me + 1, :SLOT] = own_stats
+        out_ref[me + 1, SLOT:] = mate_stats
+
+        @pl.when(me > 0)
+        def _():
+            out_ref[me - 1, :SLOT] = own_stats
+
+        out_ref[me, :SLOT] = own_stats
+        out_ref[me, SLOT:] = mate_stats
+
+    @pl.when(lax.rem(me, 2) == 1)
+    def _():
+        own_stats, mate_stats, third_stats = collect(odd_plan(lengths_ref, rows, me), 3)
+        out_ref[me - 1, :SLOT] = own_stats
+        out_ref[me - 1, SLOT:] = mate_stats
+
+        @pl.when(me >= 2)
+        def _():
+            out_ref[me - 2, :SLOT] = mate_stats
+
+        @pl.when(me + 1 < total)
+        def _():
+            out_ref[me + 1, :SLOT] = third_stats
+            out_ref[me + 2, :SLOT] = third_stats
+
+        out_ref[me, :SLOT] = own_stats
+        out_ref[me, SLOT:] = mate_stats
+
+    return None
+
+
+def merge_stats(heads, parts):
+    split = []
+    for part in parts:
+        top, total, dots = (part[kind * heads : (kind + 1) * heads] for kind in range(KINDS))
+        split.append((jnp.where(total > 0, top, FLOOR), total, dots))
+    top = functools.reduce(jnp.maximum, [s[0] for s in split])
+    scales = [jnp.exp(s[0] - top) for s in split]
+    total = sum(w * s[1] for w, s in zip(scales, split))
+    dots = sum(w * s[2] for w, s in zip(scales, split))
+    safe = jnp.where(total > 0, total, 1.0)
+    return stack_rows(top + jnp.log(safe), dots / safe)
+
+
+def grads_kernel(
+    heads, scaling, place_ref, lengths_ref, own, mate, third, key_own, key_back, mine_ref, stats_ref,
+    query_own, query_mate, query_third, key_out, back_out,
+):
+    rows = own.shape[1]
+    me = place_ref[0]
+    total = stats_ref.shape[0]
+    queries, keys = (own, mate, third), (key_own, key_back)
+
+    def slot(index, second):
+        part = stats_ref[jnp.clip(index, 0, total - 1)][SLOT * second : SLOT * (second + 1)]
+        return jnp.where((index >= 0) & (index < total), part, 0.0)
+
+    def columns(groups):
+        merged = [merge_stats(heads, parts) for parts in groups]
+        used = sum(m.shape[0] for m in merged)
+        return stack_rows(*merged, jnp.zeros((LANES - used, rows), jnp.float32)).T
+
+    def run(plan, stats, outs):
+        carry = {}
+
+        def emit(head, name, value):
+            ref, number = outs[name]
+            low, high = head_span(head)
+            last = head == heads - 1
+            start = low
+            if name in carry:
+                ref[number, :, low : low + LANES] = (
+                    value[:, :LANES] + carry.pop(name)
+                ).astype(jnp.bfloat16)
+                start = low + LANES
+            stop = high if last else high - LANES
+            if stop > start:
+                ref[number, :, start:stop] = value[:, start - low : stop - low].astype(jnp.bfloat16)
+            if not last:
+                carry[name] = value[:, high - LANES - low :]
+
+        for head in range(heads):
+            tiles, keep = tile_values(plan, head, queries, keys, scaling)
+            sums = {}
+
+            def add(name, value):
+                sums[name] = sums[name] + value if name in sums else value
+
+            for (query_slots, key_slots, mask), (q, o, k, scores, grads) in zip(plan, tiles):
+                def column(kind):
+                    at = [2 * heads * s + kind * heads + head for s in query_slots]
+                    return stack_rows(*[stats[:, c : c + 1] for c in at])
+
+                weight = jnp.where(mask, jnp.exp(scores - column(0)), 0.0)
+                slope = (weight * (grads - column(1)) * scaling).astype(jnp.bfloat16)
+                weight = weight.astype(jnp.bfloat16)
+                from_keys = matmul(slope, k, NN)
+                for number, s in enumerate(query_slots):
+                    add(("q", s), row_part(from_keys, number, rows))
+                to_keys = matmul(slope, q * keep, TN)
+                to_values = matmul(weight, o * keep, TN)
+                for number, s in enumerate(key_slots):
+                    add(("k", s), row_part(to_keys, number, rows))
+                    add(("v", s), row_part(to_values, number, rows))
+            for name, value in sums.items():
+                emit(head, name, value)
+
+    outs = {
+        ("q", 0): (query_own, 0),
+        ("q", 1): (query_mate, 0),
+        ("q", 2): (query_third, 0),
+        ("k", 0): (key_out, 0),
+        ("v", 0): (key_out, 1),
+        ("k", 1): (back_out, 0),
+        ("v", 1): (back_out, 1),
+    }
+    mine_own, mine_mate = mine_ref[me][:SLOT], mine_ref[me][SLOT:]
+
+    @pl.when(lax.rem(me, 2) == 0)
+    def _():
+        groups = (
+            (mine_own, slot(me + 1, 1), slot(me - 1, 0)),
+            (mine_mate, slot(me + 1, 0)),
+        )
+        run(even_plan(lengths_ref, rows, me), columns(groups), outs)
+
+    @pl.when(lax.rem(me, 2) == 1)
+    def _():
+        mine_third = jnp.where(me + 1 < total, mine_ref[jnp.minimum(me + 1, total - 1)][:SLOT], 0.0)
+        groups = (
+            (mine_own, slot(me - 1, 1)),
+            (mine_mate, slot(me - 1, 0), slot(me - 2, 0)),
+            (mine_third, slot(me + 1, 0), slot(me + 2, 0)),
+        )
+        run(odd_plan(lengths_ref, rows, me), columns(groups), outs)
+
+
+def halo_shards(queries, key_vectors, value_vectors, out_grad, doc_lengths):
+    _, rows, width = queries.shape
+    seq_size = lax.axis_size("seq")
+    me = lax.axis_index("seq").astype(jnp.int32)
+    scaling = HEAD ** (-0.5)
+    chunks = 2
+    part = width // chunks
+    heads = part // HEAD
+    devices = range(seq_size)
+    mates = [(s, s ^ 1) for s in devices]
+    ahead = [(s, s + 2) for s in devices if s + 2 < seq_size]
+    behind = [(s, s - 2) for s in devices if s >= 2]
+    odd_behind = [(s, s - 2) for s in devices if s >= 2 and s % 2 == 1]
+    odd_next = [(s, s + 1) for s in devices if s % 2 == 1 and s + 1 < seq_size]
+
+    def send(value, pairs):
+        return lax.ppermute(value, "seq", pairs)
+
+    def pack(first, second, chunk):
+        cut = [lax.slice_in_dim(a, chunk * part, (chunk + 1) * part, axis=2) for a in (first, second)]
+        return jnp.concatenate(cut, axis=0)
+
+    place = me[None]
+    smem = pl.BlockSpec(memory_space=pltpu.SMEM)
+    vmem = pl.BlockSpec(memory_space=pltpu.VMEM)
+    tile_flops = 2 * 4 * rows * rows * heads * 320
+    moved = []
+    for chunk in range(chunks):
+        query_own = pack(queries, out_grad, chunk)
+        key_own = pack(key_vectors, value_vectors, chunk)
+        query_mate = send(query_own, mates)
+        key_back = send(key_own, ahead)
+        query_third = send(query_mate, odd_behind)
+        moved.append((query_own, query_mate, query_third, key_own, key_back))
+    parts = []
+    for tensors in moved:
+        stats = pl.pallas_call(
+            functools.partial(stats_kernel, heads, scaling),
+            in_specs=[smem, smem] + [vmem] * 5,
+            out_specs=vmem,
+            out_shape=jax.ShapeDtypeStruct((seq_size, 2 * SLOT, rows), jnp.float32),
+            cost_estimate=pl.CostEstimate(
+                flops=2 * tile_flops, bytes_accessed=20 * rows * part, transcendentals=0
+            ),
+        )(place, doc_lengths, *tensors)
+        others = lax.all_to_all(stats, "seq", split_axis=0, concat_axis=0, tiled=True)
+        single = jax.ShapeDtypeStruct((1, rows, part), jnp.bfloat16)
+        double = jax.ShapeDtypeStruct((2, rows, part), jnp.bfloat16)
+        query_own, query_mate, query_third, key_own, key_back = pl.pallas_call(
+            functools.partial(grads_kernel, heads, scaling),
+            in_specs=[smem, smem] + [vmem] * 7,
+            out_specs=[vmem] * 5,
+            out_shape=[single, single, single, double, double],
+            cost_estimate=pl.CostEstimate(
+                flops=7 * tile_flops, bytes_accessed=34 * rows * part, transcendentals=0
+            ),
+        )(place, doc_lengths, *tensors, stats, others)
+        key_sent = send(key_back, behind)
+        query_sent = send(query_mate, mates)
+        third_sent = send(query_third, odd_next)
+
+        def total(*terms):
+            return sum(term.astype(jnp.float32) for term in terms).astype(jnp.bfloat16)
+
+        key_sum = total(key_own, key_sent)
+        parts.append((total(query_own, query_sent, third_sent), key_sum[:1], key_sum[1:]))
+    return tuple(jnp.concatenate(pieces, axis=2) for pieces in zip(*parts))
+
+
+def shards(queries, key_vectors, value_vectors, out_grad, doc_lengths):
+    _, rows, width = queries.shape
+    seq_size = lax.axis_size("seq")
+    longest = rows * seq_size * 3 // 8
+    fits = longest <= 3 * rows and seq_size % 2 == 0 and rows == LANES
+    aligned = width % (2 * HEAD) == 0 and (width // 2) % LANES == 0
+    plan = halo_shards if fits and aligned else spread_shards
+    return plan(queries, key_vectors, value_vectors, out_grad, doc_lengths)
+
+
 def solution(mesh):
     return jax.shard_map(
         shards,

time: 137 us -> 94.1 us (0.69)
  waiting for transfers between devices: 74.7 us -> 29.2 us
  local copies, waits for them, and re-layouts: 22.1 us -> 5.82 us
  Pallas kernels: 0 us -> 16.2 us
  starting transfers between devices: 29.9 us -> 38.3 us
  matrix products: 6.32 us -> 0 us
    all_to_all x7 -> x2, waiting for transfers between devices: 74.7 us -> 2.6 us  [halo_shards(): lax.all_to_all(stats, 'seq', split_axis=0, concat_axis=0, tiled=True)]
    ppermute x0 -> x12, waiting for transfers between devices: none -> 26.6 us  [send(): return lax.ppermute(value, 'seq', pairs)]
    ppermute x0 -> x12, starting transfers between devices: none -> 26.2 us  [send(): return lax.ppermute(value, 'seq', pairs)]
    all_to_all x7 -> x2, starting transfers between devices: 29.9 us -> 12 us  [halo_shards(): lax.all_to_all(stats, 'seq', split_axis=0, concat_axis=0, tiled=True)]
    pallas_call x0 -> x4, Pallas kernels: none -> 16.2 us  [the longest x2 9.91 us: halo_shards(): pl.pallas_call(functools.partial(grads_kernel, heads, scaling), in_specs=...]
    unnamed x39 -> x36, local copies, waits for them, and re-layouts: 15.2 us -> 4.31 us
    dot_general x18 -> x0, matrix products: 6.32 us -> none  [the longest x3 1.3 us: score_tile(): jnp.dot(query_rows, key_rows.T, preferred_element_type=jnp.float32)]
    gather x2 -> x0, local copies, waits for them, and re-layouts: 4.54 us -> none  [shards(): doc_stack = jnp.take(doc_index, pos_stack)]
  transfers between devices with their start and end apart: 7 -> 14, of which waited for: 7 -> 6; matrix products, arithmetic and copies ran while one was open for 11% -> 1% of each run, Pallas kernels for 0% -> 17%
where the time goes in v2:
time: 94.1 us; the launch traced here: 93.5 us
  starting transfers between devices  38.3 us (41%)
  waiting for transfers between devices  29.2 us (31%)
  Pallas kernels  16.2 us (17%)
  local copies, waits for them, and re-layouts  5.82 us (6%)
  other arithmetic  3 us (3%)
  between operations  0.96 us (1%)
    ppermute x12, waiting for transfers between devices, send(): return lax.ppermute(value, 'seq', pairs)  26.6 us
    ppermute x12, starting transfers between devices, send(): return lax.ppermute(value, 'seq', pairs)  26.2 us
    all_to_all x2, starting transfers between devices, halo_shards(): lax.all_to_all(stats, 'seq', split_axis=0, concat_axis=0, tiled=True)  12 us
    pallas_call x2, Pallas kernels, halo_shards(): pl.pallas_call(functools.partial(grads_kernel, heads, scaling), in_specs=...  9.91 us
    pallas_call x2, Pallas kernels, halo_shards(): pl.pallas_call(functools.partial(stats_kernel, heads, scaling), in_specs=...  6.27 us
    unnamed x36, local copies, waits for them, and re-layouts  4.31 us
    all_to_all x2, waiting for transfers between devices, halo_shards(): lax.all_to_all(stats, 'seq', split_axis=0, concat_axis=0, tiled=True)  2.6 us
    concatenate x3, other arithmetic, halo_shards(): return tuple((jnp.concatenate(pieces, axis=2) for pieces in zip(*parts)))  2.41 us
  transfers between devices with their start and end apart: 14, of which 6 were waited for; matrix products, arithmetic and copies ran while one was open for 1% of the time, Pallas kernels for 17%

profile of v2, /device:TPU:0, one launch (start us, length us, event | category | flops | bytes accessed | tf_op | source)
XLA Modules:
  0.0 93.5 jit_solution(16733679081782026856)
XLA Ops:
  0.6 1.4 %fusion.4 = (bf16[1,128,896]{2,1,0:T(8,128)(2,1)S(1)}, bf16[1,128,896]{2,1,0:T(8,128)(2,1)S(1)}, bf16[1,128,896]{2,1,0:T(8,128)(2,1)S(1)}, bf16[1,128,896]{2,1,0:T(8,128)(2,1)S(1)}) fusion(bf16[1,128,1792]{2,1,0:T(8,128)(2,1)} %param.5, bf16[1,128,1792]{2,1,0:T(8,128)(2,1)} %param.8), kind=kLoop, calls=%fused_computation.15 | loop fusion | bytes 1835008 | tf_op jit(solution)/shard_map/slice | solution.py:435
  2.1 3.0 %collective-permute-start.5 = (bf16[2,128,896]{2,1,0:T(8,128)(2,1)S(1)}, bf16[2,128,896]{2,1,0:T(8,128)(2,1)S(1)}, u32[]{:S(2)}, u32[]{:S(2)}) collective-permute-start(bf16[2,128,896]{2,1,0:T(8,128)(2,1)S(1)} %pad_maximum_fusion.2.own), channel_id=1, source_target_pairs={{0,4},{4,0},{8,12},{12,8},{16,20},{20,16},{24,28},{28,24},{1,5},{5... | collective-permute-start | bytes 1376264 | tf_op jit(solution)/shard_map/ppermute | solution.py:432
  6.6 3.5 %collective-permute-start.7 = (bf16[2,128,896]{2,1,0:T(8,128)(2,1)S(1)}, bf16[2,128,896]{2,1,0:T(8,128)(2,1)S(1)}, u32[]{:S(2)}, u32[]{:S(2)}) collective-permute-start(bf16[2,128,896]{2,1,0:T(8,128)(2,1)S(1)} %pad_maximum_fusion.3.key_own), channel_id=1, source_target_pairs={{0,8},{4,12},{8,16},{12,20},{16,24},{20,28},{1,9},{5,13},{9,17},{1... | collective-permute-start | bytes 1376264 | tf_op jit(solution)/shard_map/ppermute | solution.py:432
  10.1 6.3 %collective-permute-done.5.mate = bf16[2,128,896]{2,1,0:T(8,128)(2,1)S(1)} collective-permute-done((bf16[2,128,896]{2,1,0:T(8,128)(2,1)S(1)}, bf16[2,128,896]{2,1,0:T(8,128)(2,1)S(1)}, u32[]{:S(2)}, u32[]{:S(2)}) %collective-permute-start.5) | collective-permute-done | bytes 458784 | tf_op jit(solution)/shard_map/ppermute | solution.py:432
  16.4 1.4 %collective-permute-start.6 = (bf16[2,128,896]{2,1,0:T(8,128)(2,1)S(1)}, bf16[2,128,896]{2,1,0:T(8,128)(2,1)}, u32[]{:S(2)}, u32[]{:S(2)}) collective-permute-start(bf16[2,128,896]{2,1,0:T(8,128)(2,1)S(1)} %collective-permute-done.5.mate), channel_id=1, source_target_pairs={{12,4},{20,12},{28,20},{13,5},{21,13},{29,21},{14,6},{22,14},{30,2... | collective-permute-start | bytes 1376264 | tf_op jit(solution)/shard_map/ppermute | solution.py:432
  17.9 4.1 %collective-permute-start.2 = (bf16[2,128,896]{2,1,0:T(8,128)(2,1)S(1)}, bf16[2,128,896]{2,1,0:T(8,128)(2,1)S(1)}, u32[]{:S(2)}, u32[]{:S(2)}) collective-permute-start(bf16[2,128,896]{2,1,0:T(8,128)(2,1)S(1)} %pad_maximum_fusion.1.key_own), channel_id=1, source_target_pairs={{0,8},{4,12},{8,16},{12,20},{16,24},{20,28},{1,9},{5,13},{9,17},{1... | collective-permute-start | bytes 1376264 | tf_op jit(solution)/shard_map/ppermute | solution.py:432
  22.0 3.4 %collective-permute-done.mate = bf16[2,128,896]{2,1,0:T(8,128)(2,1)S(1)} collective-permute-done((bf16[2,128,896]{2,1,0:T(8,128)(2,1)S(1)}, bf16[2,128,896]{2,1,0:T(8,128)(2,1)S(1)}, u32[]{:S(2)}, u32[]{:S(2)}) %collective-permute-start) | collective-permute-done | bytes 458784 | tf_op jit(solution)/shard_map/ppermute | solution.py:432
  26.9 3.1 %shard_map.78.mine_ref = f32[8,32,128]{2,1,0:T(8,128)} custom-call(s32[1]{0:T(128)} %bitcast.place_ref, s32[8]{0:T(128)} %lengths_ref.7, bf16[2,128,896]{2,1,0:T(8,128)(2,1)} %copy-done.1, bf16[2,128,896]{2,1,0:T(8,128)(2,1)} %copy-done.7, bf16[2,128,896]{2,1,0:T(8,128)(2,1)} %collective-permute-done.6.third, bf16[2,128,896]{2,1,0:T(8,128)(2,1)} %copy-done.3, ...), custom_call_target="tpu_custom_call" | custom-call | flops 335544320 | bytes 2293760 | tf_op jit(solution)/shard_map/pallas_call | solution.py:452
  30.0 8.2 %all-to-all-start.1 = ((f32[8,32,128]{2,1,0:T(8,128)}), f32[8,32,128]{2,1,0:T(8,128)S(1)}, u32[]{:S(2)}, u32[]{:S(2)}) async-start(f32[8,32,128]{2,1,0:T(8,128)} %shard_map.78.mine_ref), calls=%async_computation.1 | async-start | bytes 262144 | tf_op jit(solution)/shard_map/all_to_all | solution.py:461
  39.8 3.1 %shard_map.76.mine_ref = f32[8,32,128]{2,1,0:T(8,128)} custom-call(s32[1]{0:T(128)} %bitcast.place_ref, s32[8]{0:T(128)} %lengths_ref.7, bf16[2,128,896]{2,1,0:T(8,128)(2,1)} %copy-done, bf16[2,128,896]{2,1,0:T(8,128)(2,1)} %copy-done.6, bf16[2,128,896]{2,1,0:T(8,128)(2,1)} %copy-done.10, bf16[2,128,896]{2,1,0:T(8,128)(2,1)} %copy-done.2, ...), custom_call_target="tpu_custom_call" | custom-call | flops 335544320 | bytes 2293760 | tf_op jit(solution)/shard_map/pallas_call | solution.py:452
  43.0 2.6 %all-to-all-done.1.stats_ref = f32[8,32,128]{2,1,0:T(8,128)S(1)} async-done(((f32[8,32,128]{2,1,0:T(8,128)}), f32[8,32,128]{2,1,0:T(8,128)S(1)}, u32[]{:S(2)}, u32[]{:S(2)}) %all-to-all-start.1) | async-done | bytes 131104 | tf_op jit(solution)/shard_map/all_to_all | solution.py:461
  46.2 3.8 %all-to-all-start = ((f32[8,32,128]{2,1,0:T(8,128)}), f32[8,32,128]{2,1,0:T(8,128)S(1)}, u32[]{:S(2)}, u32[]{:S(2)}) async-start(f32[8,32,128]{2,1,0:T(8,128)} %shard_map.76.mine_ref), calls=%async_computation | async-start | bytes 262144 | tf_op jit(solution)/shard_map/all_to_all | solution.py:461
  50.1 4.9 %shard_map.79 = (bf16[1,128,896]{2,1,0:T(8,128)(2,1)}, bf16[1,128,896]{2,1,0:T(8,128)(2,1)}, bf16[1,128,896]{2,1,0:T(8,128)(2,1)}, bf16[2,128,896]{2,1,0:T(8,128)(2,1)}, bf16[2,128,896]{2,1,0:T(8,128)(2,1)}) custom-call(s32[1]{0:T(128)} %bitcast.place_ref, s32[8]{0:T(128)} %lengths_ref.7, bf16[2,128,896]{2,1,0:T(8,128)(2,1)} %copy-done.1, ...), custom_call_target="tpu_custom_call" | custom-call | flops 1174405120 | bytes 3899392 | tf_op jit(solution)/shard_map/pallas_call | solution.py:464
  55.6 4.8 %collective-permute-start.8 = (bf16[1,128,896]{2,1,0:T(8,128)(2,1)}, bf16[1,128,896]{2,1,0:T(8,128)(2,1)S(1)}, u32[]{:S(2)}, u32[]{:S(2)}) collective-permute-start(bf16[1,128,896]{2,1,0:T(8,128)(2,1)} %get-tuple-element.17), channel_id=1, source_target_pairs={{0,4},{4,0},{8,12},{12,8},{16,20},{20,16},{24,28},{28,24},{1,5},{5... | collective-permute-start | bytes 688136 | tf_op jit(solution)/shard_map/ppermute | solution.py:432
  61.1 5.0 %shard_map.77 = (bf16[1,128,896]{2,1,0:T(8,128)(2,1)}, bf16[1,128,896]{2,1,0:T(8,128)(2,1)}, bf16[1,128,896]{2,1,0:T(8,128)(2,1)}, bf16[2,128,896]{2,1,0:T(8,128)(2,1)}, bf16[2,128,896]{2,1,0:T(8,128)(2,1)}) custom-call(s32[1]{0:T(128)} %bitcast.place_ref, s32[8]{0:T(128)} %lengths_ref.7, bf16[2,128,896]{2,1,0:T(8,128)(2,1)} %copy-done, ...), custom_call_target="tpu_custom_call" | custom-call | flops 1174405120 | bytes 3899392 | tf_op jit(solution)/shard_map/pallas_call | solution.py:464
  66.8 4.2 %collective-permute-start.3 = (bf16[1,128,896]{2,1,0:T(8,128)(2,1)}, bf16[1,128,896]{2,1,0:T(8,128)(2,1)S(1)}, u32[]{:S(2)}, u32[]{:S(2)}) collective-permute-start(bf16[1,128,896]{2,1,0:T(8,128)(2,1)} %get-tuple-element.14), channel_id=1, source_target_pairs={{0,4},{4,0},{8,12},{12,8},{16,20},{20,16},{24,28},{28,24},{1,5},{5... | collective-permute-start | bytes 688136 | tf_op jit(solution)/shard_map/ppermute | solution.py:432
  71.0 1.3 %collective-permute-start.11 = (bf16[2,128,896]{2,1,0:T(8,128)(2,1)S(1)}, bf16[2,128,896]{2,1,0:T(8,128)(2,1)S(1)}, u32[]{:S(2)}, u32[]{:S(2)}) collective-permute-start(bf16[2,128,896]{2,1,0:T(8,128)(2,1)S(1)} %copy-done.17), channel_id=1, source_target_pairs={{8,0},{12,4},{16,8},{20,12},{24,16},{28,20},{9,1},{13,5},{17,9},{2... | collective-permute-start | bytes 1376264 | tf_op jit(solution)/shard_map/ppermute | solution.py:432
  72.3 1.3 %collective-permute-start.10 = (bf16[2,128,896]{2,1,0:T(8,128)(2,1)}, bf16[2,128,896]{2,1,0:T(8,128)(2,1)S(1)}, u32[]{:S(2)}, u32[]{:S(2)}) collective-permute-start(bf16[2,128,896]{2,1,0:T(8,128)(2,1)} %get-tuple-element.20), channel_id=1, source_target_pairs={{8,0},{12,4},{16,8},{20,12},{24,16},{28,20},{9,1},{13,5},{17,9},{2... | collective-permute-start | bytes 1376264 | tf_op jit(solution)/shard_map/ppermute | solution.py:432
  73.7 1.5 %collective-permute-done.3 = bf16[1,128,896]{2,1,0:T(8,128)(2,1)S(1)} collective-permute-done((bf16[1,128,896]{2,1,0:T(8,128)(2,1)}, bf16[1,128,896]{2,1,0:T(8,128)(2,1)S(1)}, u32[]{:S(2)}, u32[]{:S(2)}) %collective-permute-start.3) | collective-permute-done | bytes 229408 | tf_op jit(solution)/shard_map/ppermute | solution.py:432
  75.3 0.8 pad_maximum_fusion.4
  76.1 10.2 %collective-permute-done.11 = bf16[2,128,896]{2,1,0:T(8,128)(2,1)S(1)} collective-permute-done((bf16[2,128,896]{2,1,0:T(8,128)(2,1)S(1)}, bf16[2,128,896]{2,1,0:T(8,128)(2,1)S(1)}, u32[]{:S(2)}, u32[]{:S(2)}) %collective-permute-start.11) | collective-permute-done | bytes 458784 | tf_op jit(solution)/shard_map/ppermute | solution.py:432
  86.5 5.2 %collective-permute-done.10 = bf16[2,128,896]{2,1,0:T(8,128)(2,1)S(1)} collective-permute-done((bf16[2,128,896]{2,1,0:T(8,128)(2,1)}, bf16[2,128,896]{2,1,0:T(8,128)(2,1)S(1)}, u32[]{:S(2)}, u32[]{:S(2)}) %collective-permute-start.10) | collective-permute-done | bytes 458784 | tf_op jit(solution)/shard_map/ppermute | solution.py:432
  91.9 0.8 pad_maximum_fusion.5
  92.7 0.8 pad_maximum_fusion.6
  (59 shorter events, 7.7 us)
Async XLA Ops:
  2.0 3.1 %copy-start.1 = (bf16[2,128,896]{2,1,0:T(8,128)(2,1)}, bf16[2,128,896]{2,1,0:T(8,128)(2,1)S(1)}, u32[]{:S(2)}) copy-start(bf16[2,128,896]{2,1,0:T(8,128)(2,1)S(1)} %pad_maximum_fusion.2.own) | copy-start | bytes 1376260
  2.1 14.4 %collective-permute-start.5 = (bf16[2,128,896]{2,1,0:T(8,128)(2,1)S(1)}, bf16[2,128,896]{2,1,0:T(8,128)(2,1)S(1)}, u32[]{:S(2)}, u32[]{:S(2)}) collective-permute-start(bf16[2,128,896]{2,1,0:T(8,128)(2,1)S(1)} %pad_maximum_fusion.2.own), channel_id=1, source_target_pairs={{0,4},{4,0},{8,12},{12,8},{16,20},{20,16},{24,28},{28,24},{1,5},{5... | collective-permute-start | bytes 1376264 | tf_op jit(solution)/shard_map/ppermute | solution.py:432
  5.1 20.3 %collective-permute-start = (bf16[2,128,896]{2,1,0:T(8,128)(2,1)S(1)}, bf16[2,128,896]{2,1,0:T(8,128)(2,1)S(1)}, u32[]{:S(2)}, u32[]{:S(2)}) collective-permute-start(bf16[2,128,896]{2,1,0:T(8,128)(2,1)S(1)} %pad_maximum_fusion.own), channel_id=1, source_target_pairs={{0,4},{4,0},{8,12},{12,8},{16,20},{20,16},{24,28},{28,24},{1,5},{5... | collective-permute-start | bytes 1376264 | tf_op jit(solution)/shard_map/ppermute | solution.py:432
  6.5 11.3 %copy-start.3 = (bf16[2,128,896]{2,1,0:T(8,128)(2,1)}, bf16[2,128,896]{2,1,0:T(8,128)(2,1)S(1)}, u32[]{:S(2)}) copy-start(bf16[2,128,896]{2,1,0:T(8,128)(2,1)S(1)} %pad_maximum_fusion.3.key_own) | copy-start | bytes 1376260
  6.6 19.6 %collective-permute-start.7 = (bf16[2,128,896]{2,1,0:T(8,128)(2,1)S(1)}, bf16[2,128,896]{2,1,0:T(8,128)(2,1)S(1)}, u32[]{:S(2)}, u32[]{:S(2)}) collective-permute-start(bf16[2,128,896]{2,1,0:T(8,128)(2,1)S(1)} %pad_maximum_fusion.3.key_own), channel_id=1, source_target_pairs={{0,8},{4,12},{8,16},{12,20},{16,24},{20,28},{1,9},{5,13},{9,17},{1... | collective-permute-start | bytes 1376264 | tf_op jit(solution)/shard_map/ppermute | solution.py:432
  16.4 1.5 %copy-start.7 = (bf16[2,128,896]{2,1,0:T(8,128)(2,1)}, bf16[2,128,896]{2,1,0:T(8,128)(2,1)S(1)}, u32[]{:S(2)}) copy-start(bf16[2,128,896]{2,1,0:T(8,128)(2,1)S(1)} %collective-permute-done.5.mate) | copy-start | bytes 1376260
  16.4 9.7 %collective-permute-start.6 = (bf16[2,128,896]{2,1,0:T(8,128)(2,1)S(1)}, bf16[2,128,896]{2,1,0:T(8,128)(2,1)}, u32[]{:S(2)}, u32[]{:S(2)}) collective-permute-start(bf16[2,128,896]{2,1,0:T(8,128)(2,1)S(1)} %collective-permute-done.5.mate), channel_id=1, source_target_pairs={{12,4},{20,12},{28,20},{13,5},{21,13},{29,21},{14,6},{22,14},{30,2... | collective-permute-start | bytes 1376264 | tf_op jit(solution)/shard_map/ppermute | solution.py:432
  17.9 12.1 %copy-start.2 = (bf16[2,128,896]{2,1,0:T(8,128)(2,1)}, bf16[2,128,896]{2,1,0:T(8,128)(2,1)S(1)}, u32[]{:S(2)}) copy-start(bf16[2,128,896]{2,1,0:T(8,128)(2,1)S(1)} %pad_maximum_fusion.1.key_own) | copy-start | bytes 1376260
  17.9 20.3 %collective-permute-start.2 = (bf16[2,128,896]{2,1,0:T(8,128)(2,1)S(1)}, bf16[2,128,896]{2,1,0:T(8,128)(2,1)S(1)}, u32[]{:S(2)}, u32[]{:S(2)}) collective-permute-start(bf16[2,128,896]{2,1,0:T(8,128)(2,1)S(1)} %pad_maximum_fusion.1.key_own), channel_id=1, source_target_pairs={{0,8},{4,12},{8,16},{12,20},{16,24},{20,28},{1,9},{5,13},{9,17},{1... | collective-permute-start | bytes 1376264 | tf_op jit(solution)/shard_map/ppermute | solution.py:432
  25.4 4.6 %copy-start.6 = (bf16[2,128,896]{2,1,0:T(8,128)(2,1)}, bf16[2,128,896]{2,1,0:T(8,128)(2,1)S(1)}, u32[]{:S(2)}) copy-start(bf16[2,128,896]{2,1,0:T(8,128)(2,1)S(1)} %collective-permute-done.mate) | copy-start | bytes 1376260
  25.4 12.8 %collective-permute-start.1 = (bf16[2,128,896]{2,1,0:T(8,128)(2,1)S(1)}, bf16[2,128,896]{2,1,0:T(8,128)(2,1)S(1)}, u32[]{:S(2)}, u32[]{:S(2)}) collective-permute-start(bf16[2,128,896]{2,1,0:T(8,128)(2,1)S(1)} %collective-permute-done.mate), channel_id=1, source_target_pairs={{12,4},{20,12},{28,20},{13,5},{21,13},{29,21},{14,6},{22,14},{30,2... | collective-permute-start | bytes 1376264 | tf_op jit(solution)/shard_map/ppermute | solution.py:432
  30.0 15.5 %all-to-all-start.1 = ((f32[8,32,128]{2,1,0:T(8,128)}), f32[8,32,128]{2,1,0:T(8,128)S(1)}, u32[]{:S(2)}, u32[]{:S(2)}) async-start(f32[8,32,128]{2,1,0:T(8,128)} %shard_map.78.mine_ref), calls=%async_computation.1 | async-start | bytes 262144 | tf_op jit(solution)/shard_map/all_to_all | solution.py:461
  46.2 14.2 %all-to-all-start = ((f32[8,32,128]{2,1,0:T(8,128)}), f32[8,32,128]{2,1,0:T(8,128)S(1)}, u32[]{:S(2)}, u32[]{:S(2)}) async-start(f32[8,32,128]{2,1,0:T(8,128)} %shard_map.76.mine_ref), calls=%async_computation | async-start | bytes 262144 | tf_op jit(solution)/shard_map/all_to_all | solution.py:461
  54.9 17.4 %collective-permute-start.9 = (bf16[1,128,896]{2,1,0:T(8,128)(2,1)}, bf16[1,128,896]{2,1,0:T(8,128)(2,1)S(1)}, u32[]{:S(2)}, u32[]{:S(2)}) collective-permute-start(bf16[1,128,896]{2,1,0:T(8,128)(2,1)} %get-tuple-element.18), channel_id=1, source_target_pairs={{4,8},{12,16},{20,24},{5,9},{13,17},{21,25},{6,10},{14,18},{22,26}... | collective-permute-start | bytes 688136 | tf_op jit(solution)/shard_map/ppermute | solution.py:432
  55.6 15.4 %copy-start.17 = (bf16[2,128,896]{2,1,0:T(8,128)(2,1)S(1)}, bf16[2,128,896]{2,1,0:T(8,128)(2,1)}, u32[]{:S(2)}) copy-start(bf16[2,128,896]{2,1,0:T(8,128)(2,1)} %get-tuple-element.22) | copy-start | bytes 1376260
  55.6 18.0 %copy-start.13 = (bf16[1,128,896]{2,1,0:T(8,128)(2,1)S(1)}, bf16[1,128,896]{2,1,0:T(8,128)(2,1)}, u32[]{:S(2)}) copy-start(bf16[1,128,896]{2,1,0:T(8,128)(2,1)} %get-tuple-element.16) | copy-start | bytes 688132
  55.6 18.0 %collective-permute-start.8 = (bf16[1,128,896]{2,1,0:T(8,128)(2,1)}, bf16[1,128,896]{2,1,0:T(8,128)(2,1)S(1)}, u32[]{:S(2)}, u32[]{:S(2)}) collective-permute-start(bf16[1,128,896]{2,1,0:T(8,128)(2,1)} %get-tuple-element.17), channel_id=1, source_target_pairs={{0,4},{4,0},{8,12},{12,8},{16,20},{20,16},{24,28},{28,24},{1,5},{5... | collective-permute-start | bytes 688136 | tf_op jit(solution)/shard_map/ppermute | solution.py:432
  66.1 7.6 %collective-permute-start.4 = (bf16[1,128,896]{2,1,0:T(8,128)(2,1)}, bf16[1,128,896]{2,1,0:T(8,128)(2,1)S(1)}, u32[]{:S(2)}, u32[]{:S(2)}) collective-permute-start(bf16[1,128,896]{2,1,0:T(8,128)(2,1)} %get-tuple-element.15), channel_id=1, source_target_pairs={{4,8},{12,16},{20,24},{5,9},{13,17},{21,25},{6,10},{14,18},{22,26}... | collective-permute-start | bytes 688136 | tf_op jit(solution)/shard_map/ppermute | solution.py:432
  66.8 8.4 %collective-permute-start.3 = (bf16[1,128,896]{2,1,0:T(8,128)(2,1)}, bf16[1,128,896]{2,1,0:T(8,128)(2,1)S(1)}, u32[]{:S(2)}, u32[]{:S(2)}) collective-permute-start(bf16[1,128,896]{2,1,0:T(8,128)(2,1)} %get-tuple-element.14), channel_id=1, source_target_pairs={{0,4},{4,0},{8,12},{12,8},{16,20},{20,16},{24,28},{28,24},{1,5},{5... | collective-permute-start | bytes 688136 | tf_op jit(solution)/shard_map/ppermute | solution.py:432
  71.0 15.3 %collective-permute-start.11 = (bf16[2,128,896]{2,1,0:T(8,128)(2,1)S(1)}, bf16[2,128,896]{2,1,0:T(8,128)(2,1)S(1)}, u32[]{:S(2)}, u32[]{:S(2)}) collective-permute-start(bf16[2,128,896]{2,1,0:T(8,128)(2,1)S(1)} %copy-done.17), channel_id=1, source_target_pairs={{8,0},{12,4},{16,8},{20,12},{24,16},{28,20},{9,1},{13,5},{17,9},{2... | collective-permute-start | bytes 1376264 | tf_op jit(solution)/shard_map/ppermute | solution.py:432
  72.3 19.4 %collective-permute-start.10 = (bf16[2,128,896]{2,1,0:T(8,128)(2,1)}, bf16[2,128,896]{2,1,0:T(8,128)(2,1)S(1)}, u32[]{:S(2)}, u32[]{:S(2)}) collective-permute-start(bf16[2,128,896]{2,1,0:T(8,128)(2,1)} %get-tuple-element.20), channel_id=1, source_target_pairs={{8,0},{12,4},{16,8},{20,12},{24,16},{28,20},{9,1},{13,5},{17,9},{2... | collective-permute-start | bytes 1376264 | tf_op jit(solution)/shard_map/ppermute | solution.py:432
  73.6 1.6 %copy-start.14 = (bf16[1,128,896]{2,1,0:T(8,128)(2,1)S(1)}, bf16[1,128,896]{2,1,0:T(8,128)(2,1)}, u32[]{:S(2)}) copy-start(bf16[1,128,896]{2,1,0:T(8,128)(2,1)} %get-tuple-element.13) | copy-start | bytes 688132
  75.3 11.0 %copy-start.8 = (bf16[2,128,896]{2,1,0:T(8,128)(2,1)S(1)}, bf16[2,128,896]{2,1,0:T(8,128)(2,1)}, u32[]{:S(2)}) copy-start(bf16[2,128,896]{2,1,0:T(8,128)(2,1)} %get-tuple-element.21) | copy-start | bytes 1376260
  86.5 5.2 %copy-start.11 = (bf16[2,128,896]{2,1,0:T(8,128)(2,1)S(1)}, bf16[2,128,896]{2,1,0:T(8,128)(2,1)}, u32[]{:S(2)}) copy-start(bf16[2,128,896]{2,1,0:T(8,128)(2,1)} %get-tuple-element.19) | copy-start | bytes 1376260
  (8 other events, 7.5 us)

commit v3 on v0

--- a/solution.py
+++ b/solution.py
@@ -1,9 +1,15 @@
+import functools
+import math
 import jax
 import jax.numpy as jnp
 from jax import lax
+from jax.experimental import pallas as pl
+from jax.experimental.pallas import tpu as pltpu
 from jax.sharding import PartitionSpec as P
 
 HEAD = 224
+LANES = 128
+FLOOR = -1e30
 
 
 def pick_slot(stacked, slot):
@@ -14,7 +20,7 @@
     return lax.dynamic_update_index_in_dim(stacked, update, slot, 0)
 
 
-def shards(queries, key_vectors, value_vectors, out_grad, doc_lengths):
+def spread_shards(queries, key_vectors, value_vectors, out_grad, doc_lengths):
     local_rows = queries.shape[1]
     local_width = queries.shape[2]
     head_count = local_width // HEAD
@@ -158,6 +164,378 @@
     return (query_out, settle(key_back), settle(value_back))
 
 
+NT = ((1,), (1,))
+NN = ((1,), (0,))
+TN = ((0,), (0,))
+KINDS = 3
+GROUP = 8
+SLOT = KINDS * GROUP
+
+
+def head_span(head):
+    low = head * HEAD // LANES * LANES
+    high = -(-(head + 1) * HEAD // LANES) * LANES
+    return low, high
+
+
+def head_mask(head):
+    low, high = head_span(head)
+    lane = lax.broadcasted_iota(jnp.int32, (1, high - low), 1) + low
+    inside = (lane >= head * HEAD) & (lane < (head + 1) * HEAD)
+    return inside.astype(jnp.float32).astype(jnp.bfloat16)
+
+
+def matmul(left, right, dims):
+    return lax.dot_general(left, right, (dims, ((), ())), preferred_element_type=jnp.float32)
+
+
+def stack(values, axis):
+    return values[0] if len(values) == 1 else jnp.concatenate(values, axis=axis)
+
+
+def allowed(lengths_ref, rows, query_block, key_block):
+    shape = (rows, rows)
+    position = query_block * rows + lax.broadcasted_iota(jnp.int32, shape, 1)
+    keys = key_block * rows + lax.broadcasted_iota(jnp.int32, shape, 0)
+    start = jnp.zeros_like(position)
+    bound = jnp.int32(0)
+    for doc in range(lengths_ref.shape[0]):
+        bound = bound + lengths_ref[doc]
+        start = jnp.where(position >= bound, bound, start)
+    return (keys >= start) & (keys <= position)
+
+
+def make_tile(lengths_ref, rows, queries, keys):
+    mask = stack(
+        [stack([allowed(lengths_ref, rows, q, k) for _, q in queries], 1) for _, k in keys], 0
+    )
+    return [slot for slot, _ in queries], [slot for slot, _ in keys], mask
+
+
+def tile_values(plan, head, queries, keys):
+    low, high = head_span(head)
+    keep = head_mask(head)
+
+    def gather(refs, number, slots):
+        return stack([refs[slot][number][0, :, low:high] for slot in slots], 0)
+
+    out = []
+    for query_slots, key_slots, mask in plan:
+        q, o = (gather(queries, number, query_slots) for number in range(2))
+        k, v = (gather(keys, number, key_slots) * keep for number in range(2))
+        out.append((q, o, k, matmul(k, q, NT), matmul(v, o, NT)))
+    return out, keep
+
+
+def collect_stats(heads, power, step, plan, queries, keys, rows, out_ref, slots):
+    for head in range(heads):
+        tiles, _ = tile_values(plan, head, queries, keys)
+        parts = {}
+        for (query_slots, _, mask), (_, _, _, raw, grads) in zip(plan, tiles):
+            raw = jnp.where(mask, raw, FLOOR)
+            for number, slot in enumerate(query_slots):
+                cut = slice(number * rows, (number + 1) * rows)
+                parts.setdefault(slot, []).append((raw[:, cut], grads[:, cut]))
+        for slot, pieces in parts.items():
+            top = functools.reduce(
+                jnp.maximum, [jnp.max(s, axis=0, keepdims=True) for s, _ in pieces]
+            )
+            exps = [jnp.exp2((s - top) * power) for s, _ in pieces]
+            sums = sum(jnp.sum(e, axis=0, keepdims=True) for e in exps)
+            dots = sum(jnp.sum(e * g, axis=0, keepdims=True) for e, (_, g) in zip(exps, pieces))
+            for kind, value in enumerate((top, sums, dots)):
+                row = slots[slot] * SLOT + kind * GROUP + step * heads + head
+                out_ref[pl.ds(row, 1), :] = value
+
+
+def merge_stats(scaling, parts):
+    split = []
+    for part in parts:
+        top, total, dots = (part[kind * GROUP : (kind + 1) * GROUP] for kind in range(KINDS))
+        split.append((jnp.where(total > 0, top, FLOOR), total, dots))
+    top = functools.reduce(jnp.maximum, [s[0] for s in split])
+    scales = [jnp.exp((s[0] - top) * scaling) for s in split]
+    total = sum(w * s[1] for w, s in zip(scales, split))
+    dots = sum(w * s[2] for w, s in zip(scales, split))
+    safe = jnp.where(total > 0, total, 1.0)
+    return top + jnp.log(safe) / scaling, dots / safe
+
+
+def collect_grads(heads, scaling, power, step, plan, queries, keys, rows, merged, outs, base):
+    carry = {}
+
+    def emit(head, name, value):
+        ref, number = outs[name]
+        low, high = head_span(head)
+        first, last = head * HEAD % LANES == 0, (head + 1) * HEAD % LANES == 0
+
+        def put(start, stop, piece):
+            if name in base:
+                old, at = base[name]
+                piece = piece + old[at, :, start:stop].astype(jnp.float32)
+            ref[number, :, start:stop] = piece.astype(jnp.bfloat16)
+
+        start, stop = low, high
+        if not first:
+            put(low, low + LANES, value[:, :LANES] + carry.pop(name))
+            start = low + LANES
+        if not last:
+            carry[name] = value[:, high - LANES - low :]
+            stop = high - LANES
+        if stop > start:
+            put(start, stop, value[:, start - low : stop - low])
+
+    for head in range(heads):
+        tiles, keep = tile_values(plan, head, queries, keys)
+        sums = {}
+
+        def add(name, value):
+            sums[name] = sums[name] + value if name in sums else value
+
+        for (query_slots, key_slots, mask), (q, o, k, raw, grads) in zip(plan, tiles):
+            def row(kind):
+                at = step * heads + head + kind * GROUP
+                return stack([merged[slot][pl.ds(at, 1), :] for slot in query_slots], 1)
+
+            weight = jnp.where(mask, jnp.exp2((raw - row(0)) * power), 0.0)
+            slope = (weight * (grads - row(1)) * scaling).astype(jnp.bfloat16)
+            weight = weight.astype(jnp.bfloat16)
+            to_queries = matmul(slope, k, TN)
+            to_keys = matmul(slope, q * keep, NN)
+            to_values = matmul(weight, o * keep, NN)
+            for number, slot in enumerate(query_slots):
+                add(("q", slot), to_queries[number * rows : (number + 1) * rows])
+            for number, slot in enumerate(key_slots):
+                cut = slice(number * rows, (number + 1) * rows)
+                add(("k", slot), to_keys[cut])
+                add(("v", slot), to_values[cut])
+        for name, value in sums.items():
+            emit(head, name, value)
+
+
+def by_parity(me, even, odd):
+    pl.when(lax.rem(me, 2) == 0)(even)
+    pl.when(lax.rem(me, 2) == 1)(odd)
+
+
+def first_stats(heads, power, place_ref, lengths_ref, qo, oo, qm, om, ko, vo, kb, vb, out_ref):
+    rows, me, step = qo.shape[1], place_ref[0], pl.program_id(0)
+    queries, keys = ((qo, oo), (qm, om)), ((ko, vo), (kb, vb))
+
+    def even():
+        plan = [
+            make_tile(lengths_ref, rows, ((0, me), (1, me + 1)), ((0, me), (1, me - 2)))
+        ]
+        collect_stats(heads, power, step, plan, queries, keys, rows, out_ref, (1, 0))
+
+    def odd():
+        plan = [
+            make_tile(lengths_ref, rows, ((0, me),), ((0, me),)),
+            make_tile(lengths_ref, rows, ((0, me), (1, me - 1)), ((1, me - 2),)),
+        ]
+        collect_stats(heads, power, step, plan, queries, keys, rows, out_ref, (0, 1))
+
+    by_parity(me, even, odd)
+
+
+def third_stats(heads, power, place_ref, lengths_ref, qt, ot, kb, vb, first_ref, out_ref):
+    rows, me, step = qt.shape[1], place_ref[0], pl.program_id(0)
+
+    def even():
+        out_ref[...] = first_ref[SLOT : 2 * SLOT]
+
+    def odd():
+        plan = [make_tile(lengths_ref, rows, ((0, me + 1),), ((0, me - 2),))]
+        collect_stats(heads, power, step, plan, ((qt, ot),), ((kb, vb),), rows, out_ref, (0,))
+
+    by_parity(me, even, odd)
+
+
+def odd_block_grads(
+    heads, scaling, power, place_ref, lengths_ref, qo, oo, qm, om, ko, vo, kb, vb, mine, mate,
+    query_out, own_out, back_out, merged,
+):
+    rows, me, step = qo.shape[1], place_ref[0], pl.program_id(0)
+    keys = ((ko, vo), (kb, vb))
+    shift, dots = merge_stats(scaling, (mine[:SLOT], mate[:SLOT]))
+    merged[:GROUP], merged[GROUP:] = shift, dots
+    outs = {
+        ("q", 0): (query_out, 0),
+        ("k", 0): (own_out, 0),
+        ("v", 0): (own_out, 1),
+        ("k", 1): (back_out, 0),
+        ("v", 1): (back_out, 1),
+    }
+
+    def run(block, queries):
+        own = me
+        plan = [make_tile(lengths_ref, rows, ((0, block),), ((0, own), (1, own - 2)))]
+        collect_grads(
+            heads, scaling, power, step, plan, queries, keys, rows, (merged,), outs, {}
+        )
+
+    by_parity(me, lambda: run(me + 1, ((qm, om),)), lambda: run(me, ((qo, oo),)))
+
+
+def even_block_grads(
+    heads, scaling, power, place_ref, lengths_ref, qo, oo, qm, om, qt, ot, ko, vo, kb, vb, mine, mate, up,
+    third, zig, down, own_part, back_part, query_out, third_out, own_out, back_out, merged, merged_third,
+):
+    rows, me, step = qo.shape[1], place_ref[0], pl.program_id(0)
+
+    def even():
+        shift, dots = merge_stats(scaling, (mine[SLOT:], mate[SLOT:], zig[...]))
+        merged[:GROUP], merged[GROUP:] = shift, dots
+        plan = [make_tile(lengths_ref, rows, ((0, me),), ((0, me), (1, me - 2)))]
+        outs = {
+            ("q", 0): (query_out, 0),
+            ("k", 0): (own_out, 0),
+            ("v", 0): (own_out, 1),
+            ("k", 1): (back_out, 0),
+            ("v", 1): (back_out, 1),
+        }
+        base = {
+            ("k", 0): (own_part, 0),
+            ("v", 0): (own_part, 1),
+            ("k", 1): (back_part, 0),
+            ("v", 1): (back_part, 1),
+        }
+        collect_grads(
+            heads, scaling, power, step, plan, ((qo, oo),), ((ko, vo), (kb, vb)), rows, (merged,), outs, base
+        )
+        third_out[...] = jnp.zeros_like(third_out)
+
+    def odd():
+        shift, dots = merge_stats(scaling, (mine[SLOT:], mate[SLOT:], up[...]))
+        merged[:GROUP], merged[GROUP:] = shift, dots
+        shift, dots = merge_stats(scaling, (third[...], zig[...], down[SLOT:]))
+        merged_third[:GROUP], merged_third[GROUP:] = shift, dots
+        plan = [make_tile(lengths_ref, rows, ((0, me - 1), (1, me + 1)), ((0, me - 2),))]
+        outs = {
+            ("q", 0): (query_out, 0),
+            ("q", 1): (third_out, 0),
+            ("k", 0): (back_out, 0),
+            ("v", 0): (back_out, 1),
+        }
+        base = {("k", 0): (back_part, 0), ("v", 0): (back_part, 1)}
+        collect_grads(
+            heads, scaling, power, step, plan, ((qm, om), (qt, ot)), ((kb, vb),), rows,
+            (merged, merged_third), outs, base,
+        )
+        own_out[...] = own_part[...]
+
+    by_parity(me, even, odd)
+
+
+def halo_shards(queries, key_vectors, value_vectors, out_grad, doc_lengths):
+    _, rows, width = queries.shape
+    seq_size = lax.axis_size("seq")
+    me = lax.axis_index("seq").astype(jnp.int32)
+    scaling = HEAD ** (-0.5)
+    power = scaling * math.log2(math.e)
+    steps = width // HEAD // 4
+    part = width // steps
+    heads = part // HEAD
+    devices = range(seq_size)
+    odds = [s for s in devices if s % 2]
+    mates = [(s, s ^ 1) for s in devices]
+    ahead = [(s, s + 2) for s in devices if s + 2 < seq_size]
+    behind = [(s, s - 2) for s in devices if s >= 2]
+    odd_ahead = [(s, s + 2) for s in odds if s + 2 < seq_size]
+    odd_behind = [(s, s - 2) for s in odds if s >= 2]
+    odd_next = [(s, s + 1) for s in odds if s + 1 < seq_size]
+    zigzag = odd_next + [(t, s) for s, t in odd_next]
+    even_to_odd = [(s - 1, s) for s in odds]
+    odd_to_even = [(s, s - 1) for s in odds]
+
+    def send(value, pairs):
+        return lax.ppermute(value, "seq", pairs)
+
+    smem = pl.BlockSpec(memory_space=pltpu.SMEM)
+    wide = pl.BlockSpec((1, rows, part), lambda step: (0, 0, step))
+    pair = pl.BlockSpec((2, rows, part), lambda step: (0, 0, step))
+
+    def slim(count):
+        return pl.BlockSpec((count * SLOT, rows), lambda step: (0, 0))
+
+    def stats_shape(count):
+        return jax.ShapeDtypeStruct((count * SLOT, rows), jnp.float32)
+
+    def shape(count):
+        return jax.ShapeDtypeStruct((count, rows, width), jnp.bfloat16)
+
+    def call(kernel, tiles, products, arguments, in_specs, out_specs, out_shape, scratch=0):
+        flops = 2 * products * tiles * rows * rows * width * 3 // 2
+        return pl.pallas_call(
+            kernel,
+            grid=(steps,),
+            in_specs=[smem, smem] + in_specs,
+            out_specs=out_specs,
+            out_shape=out_shape,
+            scratch_shapes=[pltpu.VMEM((2 * GROUP, rows), jnp.float32)] * scratch,
+            cost_estimate=pl.CostEstimate(
+                flops=flops, bytes_accessed=20 * rows * width, transcendentals=0
+            ),
+        )(me[None], doc_lengths, *arguments)
+
+    query_mate = send(queries, mates)
+    grad_mate = send(out_grad, mates)
+    key_back = send(key_vectors, ahead)
+    value_back = send(value_vectors, ahead)
+    query_third = send(query_mate, odd_behind)
+    grad_third = send(grad_mate, odd_behind)
+    rows_here = (queries, out_grad, query_mate, grad_mate)
+    rows_third = (query_third, grad_third)
+    back = (key_back, value_back)
+    cols = (key_vectors, value_vectors) + back
+
+    mine = call(
+        functools.partial(first_stats, heads, power), 4, 2, (*rows_here, *cols), [wide] * 8, slim(2),
+        stats_shape(2),
+    )
+    mate = send(mine, mates)
+    down = send(mine, odd_behind)
+    query_a, own_part, back_part = call(
+        functools.partial(odd_block_grads, heads, scaling, power), 2, 5, (*rows_here, *cols, mine, mate),
+        [wide] * 8 + [slim(2)] * 2, [wide, pair, pair], [shape(1), shape(2), shape(2)], 1,
+    )
+    from_even = send(query_a, even_to_odd)
+    third = call(
+        functools.partial(third_stats, heads, power), 1, 2, (*rows_third, *back, mine),
+        [wide] * 4 + [slim(2)], slim(1), stats_shape(1),
+    )
+    zig = send(third, zigzag)
+    up = send(third, odd_ahead)
+    query_b, query_c, key_own, key_sent = call(
+        functools.partial(even_block_grads, heads, scaling, power), 2, 5,
+        (*rows_here, *rows_third, *cols, mine, mate, up, third, zig, down, own_part, back_part),
+        [wide] * 10 + [slim(2)] * 2 + [slim(1)] * 3 + [slim(2)] + [pair] * 2,
+        [wide, wide, pair, pair], [shape(1), shape(1), shape(2), shape(2)], 2,
+    )
+    key_back_sum = send(key_sent, behind)
+    from_odd = send(query_b, odd_to_even)
+    from_third = send(query_c, odd_next)
+
+    def total(*terms):
+        return sum(term.astype(jnp.float32) for term in terms).astype(jnp.bfloat16)
+
+    query_own = jnp.where(lax.rem(me, 2) == 0, query_b, query_a)
+    query_ready = total(query_own, from_even, from_odd, from_third)
+    key_ready = total(key_own[:1], key_back_sum[:1])
+    value_ready = total(key_own[1:], key_back_sum[1:])
+    return query_ready, key_ready, value_ready
+
+
+def shards(queries, key_vectors, value_vectors, out_grad, doc_lengths):
+    _, rows, width = queries.shape
+    seq_size = lax.axis_size("seq")
+    longest = rows * seq_size * 3 // 8
+    fits = longest <= 3 * rows and seq_size % 2 == 0 and rows == LANES
+    heads = width // HEAD
+    plan = halo_shards if fits and heads % 4 == 0 and heads <= GROUP else spread_shards
+    return plan(queries, key_vectors, value_vectors, out_grad, doc_lengths)
+
+
 def solution(mesh):
     return jax.shard_map(
         shards,

time: 137 us -> 91 us (0.66)
  waiting for transfers between devices: 74.7 us -> 33.1 us
  Pallas kernels: 0 us -> 19 us
  local copies, waits for them, and re-layouts: 22.1 us -> 3.49 us
  matrix products: 6.32 us -> 0 us
    all_to_all x7 -> x0, waiting for transfers between devices: 74.7 us -> none  [the longest x1 12.4 us: shards(): lax.all_to_all(spread(out_grad), 'seq', split_axis=1, concat_axis=0, tile...]
    ppermute x0 -> x14, waiting for transfers between devices: none -> 33.1 us  [send(): return lax.ppermute(value, 'seq', pairs)]
    ppermute x0 -> x14, starting transfers between devices: none -> 30.3 us  [send(): return lax.ppermute(value, 'seq', pairs)]
    all_to_all x7 -> x0, starting transfers between devices: 29.9 us -> none  [the longest x1 7.38 us: shards(): lax.all_to_all(spread(queries), 'seq', split_axis=1, concat_axis=0, tiled...]
    pallas_call x0 -> x4, Pallas kernels: none -> 19 us  [call(): pl.pallas_call(kernel, grid=(steps,), in_specs=[smem, smem] + in_specs, o...]
    unnamed x39 -> x24, local copies, waits for them, and re-layouts: 15.2 us -> 3.49 us
    dot_general x18 -> x0, matrix products: 6.32 us -> none  [the longest x3 1.3 us: score_tile(): jnp.dot(query_rows, key_rows.T, preferred_element_type=jnp.float32)]
    gather x2 -> x0, local copies, waits for them, and re-layouts: 4.54 us -> none  [shards(): doc_stack = jnp.take(doc_index, pos_stack)]
  transfers between devices with their start and end apart: 7 -> 14, of which waited for: 7 -> 5; matrix products, arithmetic and copies ran while one was open for 11% -> 2% of each run, Pallas kernels for 0% -> 21%
where the time goes in v3:
time: 91 us; the launch traced here: 90 us
  waiting for transfers between devices  33.1 us (36%)
  starting transfers between devices  30.3 us (33%)
  Pallas kernels  19 us (21%)
  local copies, waits for them, and re-layouts  3.49 us (4%)
  other arithmetic  3.22 us (4%)
    ppermute x14, waiting for transfers between devices, send(): return lax.ppermute(value, 'seq', pairs)  33.1 us
    ppermute x14, starting transfers between devices, send(): return lax.ppermute(value, 'seq', pairs)  30.3 us
    pallas_call x4, Pallas kernels, call(): pl.pallas_call(kernel, grid=(steps,), in_specs=[smem, smem] + in_specs, o...  19 us
    unnamed x24, local copies, waits for them, and re-layouts  3.49 us
    convert_element_type x2, other arithmetic, total(): sum((term.astype(jnp.float32) for term in terms)).astype(jnp.bfloat16)  3.22 us
  transfers between devices with their start and end apart: 14, of which 5 were waited for; matrix products, arithmetic and copies ran while one was open for 2% of the time, Pallas kernels for 21%

profile of v3, /device:TPU:0, one launch (start us, length us, event | category | flops | bytes accessed | tf_op | source)
XLA Modules:
  0.0 90.0 jit_solution(13293483967012446420)
XLA Ops:
  0.6 3.0 %collective-permute-start = (bf16[1,128,1792]{2,1,0:T(8,128)(2,1)}, bf16[1,128,1792]{2,1,0:T(8,128)(2,1)S(1)}, u32[]{:S(2)}, u32[]{:S(2)}) collective-permute-start(bf16[1,128,1792]{2,1,0:T(8,128)(2,1)} %qo.5), channel_id=1, source_target_pairs={{0,4},{4,0},{8,12},{12,8},{16,20},{20,16},{24,28},{28,24},{1,5},{5... | collective-permute-start | bytes 1376264 | tf_op jit(solution)/shard_map/ppermute | solution.py:452
  3.7 4.0 %collective-permute-start.4 = (bf16[1,128,1792]{2,1,0:T(8,128)(2,1)}, bf16[1,128,1792]{2,1,0:T(8,128)(2,1)S(1)}, u32[]{:S(2)}, u32[]{:S(2)}) collective-permute-start(bf16[1,128,1792]{2,1,0:T(8,128)(2,1)} %ko.5), channel_id=1, source_target_pairs={{0,8},{4,12},{8,16},{12,20},{16,24},{20,28},{1,9},{5,13},{9,17},{1... | collective-permute-start | bytes 1376264 | tf_op jit(solution)/shard_map/ppermute | solution.py:452
  7.7 3.5 %collective-permute-start.5 = (bf16[1,128,1792]{2,1,0:T(8,128)(2,1)}, bf16[1,128,1792]{2,1,0:T(8,128)(2,1)S(1)}, u32[]{:S(2)}, u32[]{:S(2)}) collective-permute-start(bf16[1,128,1792]{2,1,0:T(8,128)(2,1)} %vo.5), channel_id=1, source_target_pairs={{0,8},{4,12},{8,16},{12,20},{16,24},{20,28},{1,9},{5,13},{9,17},{1... | collective-permute-start | bytes 1376264 | tf_op jit(solution)/shard_map/ppermute | solution.py:452
  11.2 4.0 %collective-permute-done.qm = bf16[1,128,1792]{2,1,0:T(8,128)(2,1)S(1)} collective-permute-done((bf16[1,128,1792]{2,1,0:T(8,128)(2,1)}, bf16[1,128,1792]{2,1,0:T(8,128)(2,1)S(1)}, u32[]{:S(2)}, u32[]{:S(2)}) %collective-permute-start) | collective-permute-done | bytes 458784 | tf_op jit(solution)/shard_map/ppermute | solution.py:452
  15.2 0.7 collective-permute-start.2
  15.9 8.3 %collective-permute-done.1.om = bf16[1,128,1792]{2,1,0:T(8,128)(2,1)S(1)} collective-permute-done((bf16[1,128,1792]{2,1,0:T(8,128)(2,1)}, bf16[1,128,1792]{2,1,0:T(8,128)(2,1)S(1)}, u32[]{:S(2)}, u32[]{:S(2)}) %collective-permute-start.1) | collective-permute-done | bytes 458784 | tf_op jit(solution)/shard_map/ppermute | solution.py:452
  24.2 0.7 collective-permute-start.3
  24.9 2.1 %collective-permute-done.5.vb = bf16[1,128,1792]{2,1,0:T(8,128)(2,1)S(1)} collective-permute-done((bf16[1,128,1792]{2,1,0:T(8,128)(2,1)}, bf16[1,128,1792]{2,1,0:T(8,128)(2,1)S(1)}, u32[]{:S(2)}, u32[]{:S(2)}) %collective-permute-start.5) | collective-permute-done | bytes 458784 | tf_op jit(solution)/shard_map/ppermute | solution.py:452
  27.0 0.7 copy-done.1
  27.8 3.7 %shard_map.76.first_ref.mine = f32[48,128]{1,0:T(8,128)} custom-call(s32[1]{0:T(128)} %bitcast.place_ref, s32[8]{0:T(128)} %lengths_ref.7, bf16[1,128,1792]{2,1,0:T(8,128)(2,1)} %qo.5, bf16[1,128,1792]{2,1,0:T(8,128)(2,1)} %oo.5, bf16[1,128,1792]{2,1,0:T(8,128)(2,1)} %copy-done.2, bf16[1,128,1792]{2,1,0:T(8,128)(2,1)} %copy-done.3, ...), custom_call_target="tpu_custom_call" | custom-call | flops 704643072 | bytes 4587520 | tf_op jit(solution)/shard_map/pallas_call | solution.py:469
  31.4 1.8 %collective-permute-start.6 = (f32[48,128]{1,0:T(8,128)}, f32[48,128]{1,0:T(8,128)S(1)}, u32[]{:S(2)}, u32[]{:S(2)}) collective-permute-start(f32[48,128]{1,0:T(8,128)} %shard_map.76.first_ref.mine), channel_id=1, source_target_pairs={{0,4},{4,0},{8,12},{12,8},{16,20},{20,16},{24,28},{28,24},{1,5},{5... | collective-permute-start | bytes 73736 | tf_op jit(solution)/shard_map/ppermute | solution.py:452
  33.9 0.7 copy-done.4
  34.7 0.8 copy-done.5
  35.5 2.2 %shard_map.77.third = f32[24,128]{1,0:T(8,128)} custom-call(s32[1]{0:T(128)} %bitcast.place_ref, s32[8]{0:T(128)} %lengths_ref.7, bf16[1,128,1792]{2,1,0:T(8,128)(2,1)} %copy-done.4, bf16[1,128,1792]{2,1,0:T(8,128)(2,1)} %copy-done.5, bf16[1,128,1792]{2,1,0:T(8,128)(2,1)} %copy-done, bf16[1,128,1792]{2,1,0:T(8,128)(2,1)} %copy-done.1, ...), custom_call_target="tpu_custom_call" | custom-call | flops 176160768 | bytes 4587520 | tf_op jit(solution)/shard_map/pallas_call | solution.py:469
  39.6 6.2 %shard_map.78 = (bf16[1,128,1792]{2,1,0:T(8,128)(2,1)}, bf16[2,128,1792]{2,1,0:T(8,128)(2,1)}, bf16[2,128,1792]{2,1,0:T(8,128)(2,1)}) custom-call(s32[1]{0:T(128)} %bitcast.place_ref, s32[8]{0:T(128)} %lengths_ref.7, bf16[1,128,1792]{2,1,0:T(8,128)(2,1)} %qo.5, bf16[1,128,1792]{2,1,0:T(8,128)(2,1)} %oo.5, bf16[1,128,1792]{2,1,0:T(8,128)(2,1)} %copy-done.2, ...), custom_call_target="tpu_custom_call" | custom-call | flops 880803840 | bytes 4587520 | tf_op jit(solution)/shard_map/pallas_call | solution.py:469
  45.8 11.4 %collective-permute-start.10 = (bf16[1,128,1792]{2,1,0:T(8,128)(2,1)}, bf16[1,128,1792]{2,1,0:T(8,128)(2,1)S(1)}, u32[]{:S(2)}, u32[]{:S(2)}) collective-permute-start(bf16[1,128,1792]{2,1,0:T(8,128)(2,1)} %get-tuple-element.13), channel_id=1, source_target_pairs={{0,4},{8,12},{16,20},{24,28},{1,5},{9,13},{17,21},{25,29},{2,6},{1... | collective-permute-start | bytes 1376264 | tf_op jit(solution)/shard_map/ppermute | solution.py:452
  57.9 6.9 %shard_map.79 = (bf16[1,128,1792]{2,1,0:T(8,128)(2,1)}, bf16[1,128,1792]{2,1,0:T(8,128)(2,1)}, bf16[2,128,1792]{2,1,0:T(8,128)(2,1)}, bf16[2,128,1792]{2,1,0:T(8,128)(2,1)}) custom-call(s32[1]{0:T(128)} %bitcast.place_ref, s32[8]{0:T(128)} %lengths_ref.7, bf16[1,128,1792]{2,1,0:T(8,128)(2,1)} %qo.5, bf16[1,128,1792]{2,1,0:T(8,128)(2,1)} %oo.5, ...), custom_call_target="tpu_custom_call" | custom-call | flops 880803840 | bytes 4587520 | tf_op jit(solution)/shard_map/pallas_call | solution.py:469
  64.8 1.3 %collective-permute-start.11 = (bf16[1,128,1792]{2,1,0:T(8,128)(2,1)}, bf16[1,128,1792]{2,1,0:T(8,128)(2,1)S(1)}, u32[]{:S(2)}, u32[]{:S(2)}) collective-permute-start(bf16[1,128,1792]{2,1,0:T(8,128)(2,1)} %get-tuple-element.12), channel_id=1, source_target_pairs={{4,0},{12,8},{20,16},{28,24},{5,1},{13,9},{21,17},{29,25},{6,2},{1... | collective-permute-start | bytes 1376264 | tf_op jit(solution)/shard_map/ppermute | solution.py:452
  66.1 0.7 collective-permute-start.12
  66.8 1.3 %collective-permute-start.13 = (bf16[2,128,1792]{2,1,0:T(8,128)(2,1)}, bf16[2,128,1792]{2,1,0:T(8,128)(2,1)S(1)}, u32[]{:S(2)}, u32[]{:S(2)}) collective-permute-start(bf16[2,128,1792]{2,1,0:T(8,128)(2,1)} %get-tuple-element.16), channel_id=1, source_target_pairs={{8,0},{12,4},{16,8},{20,12},{24,16},{28,20},{9,1},{13,5},{17,9},{2... | collective-permute-start | bytes 2752520 | tf_op jit(solution)/shard_map/ppermute | solution.py:452
  68.1 8.4 %collective-permute-done.11 = bf16[1,128,1792]{2,1,0:T(8,128)(2,1)S(1)} collective-permute-done((bf16[1,128,1792]{2,1,0:T(8,128)(2,1)}, bf16[1,128,1792]{2,1,0:T(8,128)(2,1)S(1)}, u32[]{:S(2)}, u32[]{:S(2)}) %collective-permute-start.11) | collective-permute-done | bytes 458784 | tf_op jit(solution)/shard_map/ppermute | solution.py:452
  76.5 2.1 %add_convert_fusion.2 = bf16[1,128,1792]{2,1,0:T(8,128)(2,1)} fusion(bf16[1,128,1792]{2,1,0:T(8,128)(2,1)S(1)} %collective-permute-done.12, bf16[1,128,1792]{2,1,0:T(8,128)(2,1)S(1)} %collective-permute-done.11, bf16[1,128,1792]{2,1,0:T(8,128)(2,1)S(1)} %collective-permute-done.10, bf16[1,128,1792]{2,1,0:T(8,128)(2,1)} %get-tuple-element.12, ...), kind=kLoop, calls=%fused_computation.2 | loop fusion | flops 2064384 | bytes 2752513 | tf_op jit(solution)/shard_map/convert_element_type | solution.py:520
  78.6 10.2 %collective-permute-done.13 = bf16[2,128,1792]{2,1,0:T(8,128)(2,1)S(1)} collective-permute-done((bf16[2,128,1792]{2,1,0:T(8,128)(2,1)}, bf16[2,128,1792]{2,1,0:T(8,128)(2,1)S(1)}, u32[]{:S(2)}, u32[]{:S(2)}) %collective-permute-start.13) | collective-permute-done | bytes 917536 | tf_op jit(solution)/shard_map/ppermute | solution.py:452
  88.8 1.1 %add_convert_fusion = (bf16[1,128,1792]{2,1,0:T(8,128)(2,1)}, bf16[1,128,1792]{2,1,0:T(8,128)(2,1)}) fusion(bf16[2,128,1792]{2,1,0:T(8,128)(2,1)S(1)} %collective-permute-done.13, bf16[2,128,1792]{2,1,0:T(8,128)(2,1)S(1)} %copy-done.6), kind=kLoop, calls=%fused_computation | loop fusion | flops 1835008 | bytes 2752512 | tf_op jit(solution)/shard_map/convert_element_type | solution.py:520
  (34 shorter events, 3.3 us)
Async XLA Ops:
  0.6 14.6 %collective-permute-start = (bf16[1,128,1792]{2,1,0:T(8,128)(2,1)}, bf16[1,128,1792]{2,1,0:T(8,128)(2,1)S(1)}, u32[]{:S(2)}, u32[]{:S(2)}) collective-permute-start(bf16[1,128,1792]{2,1,0:T(8,128)(2,1)} %qo.5), channel_id=1, source_target_pairs={{0,4},{4,0},{8,12},{12,8},{16,20},{20,16},{24,28},{28,24},{1,5},{5... | collective-permute-start | bytes 1376264 | tf_op jit(solution)/shard_map/ppermute | solution.py:452
  3.6 20.6 %collective-permute-start.1 = (bf16[1,128,1792]{2,1,0:T(8,128)(2,1)}, bf16[1,128,1792]{2,1,0:T(8,128)(2,1)S(1)}, u32[]{:S(2)}, u32[]{:S(2)}) collective-permute-start(bf16[1,128,1792]{2,1,0:T(8,128)(2,1)} %oo.5), channel_id=1, source_target_pairs={{0,4},{4,0},{8,12},{12,8},{16,20},{20,16},{24,28},{28,24},{1,5},{5... | collective-permute-start | bytes 1376264 | tf_op jit(solution)/shard_map/ppermute | solution.py:452
  3.7 21.2 %collective-permute-start.4 = (bf16[1,128,1792]{2,1,0:T(8,128)(2,1)}, bf16[1,128,1792]{2,1,0:T(8,128)(2,1)S(1)}, u32[]{:S(2)}, u32[]{:S(2)}) collective-permute-start(bf16[1,128,1792]{2,1,0:T(8,128)(2,1)} %ko.5), channel_id=1, source_target_pairs={{0,8},{4,12},{8,16},{12,20},{16,24},{20,28},{1,9},{5,13},{9,17},{1... | collective-permute-start | bytes 1376264 | tf_op jit(solution)/shard_map/ppermute | solution.py:452
  7.7 19.3 %collective-permute-start.5 = (bf16[1,128,1792]{2,1,0:T(8,128)(2,1)}, bf16[1,128,1792]{2,1,0:T(8,128)(2,1)S(1)}, u32[]{:S(2)}, u32[]{:S(2)}) collective-permute-start(bf16[1,128,1792]{2,1,0:T(8,128)(2,1)} %vo.5), channel_id=1, source_target_pairs={{0,8},{4,12},{8,16},{12,20},{16,24},{20,28},{1,9},{5,13},{9,17},{1... | collective-permute-start | bytes 1376264 | tf_op jit(solution)/shard_map/ppermute | solution.py:452
  15.2 11.8 %copy-start.2 = (bf16[1,128,1792]{2,1,0:T(8,128)(2,1)}, bf16[1,128,1792]{2,1,0:T(8,128)(2,1)S(1)}, u32[]{:S(2)}) copy-start(bf16[1,128,1792]{2,1,0:T(8,128)(2,1)S(1)} %collective-permute-done.qm) | copy-start | bytes 1376260
  15.2 18.7 %collective-permute-start.2 = (bf16[1,128,1792]{2,1,0:T(8,128)(2,1)S(1)}, bf16[1,128,1792]{2,1,0:T(8,128)(2,1)S(1)}, u32[]{:S(2)}, u32[]{:S(2)}) collective-permute-start(bf16[1,128,1792]{2,1,0:T(8,128)(2,1)S(1)} %collective-permute-done.qm), channel_id=1, source_target_pairs={{12,4},{20,12},{28,20},{13,5},{21,13},{29,21},{14,6},{22,14},{30,2... | collective-permute-start | bytes 1376264 | tf_op jit(solution)/shard_map/ppermute | solution.py:452
  24.2 2.8 %copy-start.3 = (bf16[1,128,1792]{2,1,0:T(8,128)(2,1)}, bf16[1,128,1792]{2,1,0:T(8,128)(2,1)S(1)}, u32[]{:S(2)}) copy-start(bf16[1,128,1792]{2,1,0:T(8,128)(2,1)S(1)} %collective-permute-done.1.om) | copy-start | bytes 1376260
  24.2 9.7 %collective-permute-start.3 = (bf16[1,128,1792]{2,1,0:T(8,128)(2,1)S(1)}, bf16[1,128,1792]{2,1,0:T(8,128)(2,1)S(1)}, u32[]{:S(2)}, u32[]{:S(2)}) collective-permute-start(bf16[1,128,1792]{2,1,0:T(8,128)(2,1)S(1)} %collective-permute-done.1.om), channel_id=1, source_target_pairs={{12,4},{20,12},{28,20},{13,5},{21,13},{29,21},{14,6},{22,14},{30,2... | collective-permute-start | bytes 1376264 | tf_op jit(solution)/shard_map/ppermute | solution.py:452
  24.9 2.1 %copy-start = (bf16[1,128,1792]{2,1,0:T(8,128)(2,1)}, bf16[1,128,1792]{2,1,0:T(8,128)(2,1)S(1)}, u32[]{:S(2)}) copy-start(bf16[1,128,1792]{2,1,0:T(8,128)(2,1)S(1)} %collective-permute-done.4.kb) | copy-start | bytes 1376260
  27.0 0.8 copy-start.1
  31.4 7.6 %collective-permute-start.6 = (f32[48,128]{1,0:T(8,128)}, f32[48,128]{1,0:T(8,128)S(1)}, u32[]{:S(2)}, u32[]{:S(2)}) collective-permute-start(f32[48,128]{1,0:T(8,128)} %shard_map.76.first_ref.mine), channel_id=1, source_target_pairs={{0,4},{4,0},{8,12},{12,8},{16,20},{20,16},{24,28},{28,24},{1,5},{5... | collective-permute-start | bytes 73736 | tf_op jit(solution)/shard_map/ppermute | solution.py:452
  33.3 24.0 %collective-permute-start.9 = (f32[48,128]{1,0:T(8,128)}, f32[48,128]{1,0:T(8,128)S(1)}, u32[]{:S(2)}, u32[]{:S(2)}) collective-permute-start(f32[48,128]{1,0:T(8,128)} %shard_map.76.first_ref.mine), channel_id=1, source_target_pairs={{12,4},{20,12},{28,20},{13,5},{21,13},{29,21},{14,6},{22,14},{30,2... | collective-permute-start | bytes 73736 | tf_op jit(solution)/shard_map/ppermute | solution.py:452
  33.9 0.8 copy-start.4
  34.7 0.8 copy-start.5
  37.7 19.6 %collective-permute-start.7 = (f32[24,128]{1,0:T(8,128)}, f32[24,128]{1,0:T(8,128)S(1)}, u32[]{:S(2)}, u32[]{:S(2)}) collective-permute-start(f32[24,128]{1,0:T(8,128)} %shard_map.77.third), channel_id=1, source_target_pairs={{4,12},{12,20},{20,28},{5,13},{13,21},{21,29},{6,14},{14,22},{22,3... | collective-permute-start | bytes 36872 | tf_op jit(solution)/shard_map/ppermute | solution.py:452
  38.3 18.9 %collective-permute-start.8 = (f32[24,128]{1,0:T(8,128)}, f32[24,128]{1,0:T(8,128)S(1)}, u32[]{:S(2)}, u32[]{:S(2)}) collective-permute-start(f32[24,128]{1,0:T(8,128)} %shard_map.77.third), channel_id=1, source_target_pairs={{4,8},{12,16},{20,24},{8,4},{16,12},{24,20},{5,9},{13,17},{21,25},... | collective-permute-start | bytes 36872 | tf_op jit(solution)/shard_map/ppermute | solution.py:452
  39.0 0.6 copy-start.8
  45.8 22.3 %collective-permute-start.10 = (bf16[1,128,1792]{2,1,0:T(8,128)(2,1)}, bf16[1,128,1792]{2,1,0:T(8,128)(2,1)S(1)}, u32[]{:S(2)}, u32[]{:S(2)}) collective-permute-start(bf16[1,128,1792]{2,1,0:T(8,128)(2,1)} %get-tuple-element.13), channel_id=1, source_target_pairs={{0,4},{8,12},{16,20},{24,28},{1,5},{9,13},{17,21},{25,29},{2,6},{1... | collective-permute-start | bytes 1376264 | tf_op jit(solution)/shard_map/ppermute | solution.py:452
  57.2 0.6 copy-start.9
  57.9 18.7 %copy-start.7 = (bf16[1,128,1792]{2,1,0:T(8,128)(2,1)S(1)}, bf16[1,128,1792]{2,1,0:T(8,128)(2,1)}, u32[]{:S(2)}) copy-start(bf16[1,128,1792]{2,1,0:T(8,128)(2,1)} %get-tuple-element.13) | copy-start | bytes 1376260
  64.8 11.7 %collective-permute-start.11 = (bf16[1,128,1792]{2,1,0:T(8,128)(2,1)}, bf16[1,128,1792]{2,1,0:T(8,128)(2,1)S(1)}, u32[]{:S(2)}, u32[]{:S(2)}) collective-permute-start(bf16[1,128,1792]{2,1,0:T(8,128)(2,1)} %get-tuple-element.12), channel_id=1, source_target_pairs={{4,0},{12,8},{20,16},{28,24},{5,1},{13,9},{21,17},{29,25},{6,2},{1... | collective-permute-start | bytes 1376264 | tf_op jit(solution)/shard_map/ppermute | solution.py:452
  66.1 10.4 %collective-permute-start.12 = (bf16[1,128,1792]{2,1,0:T(8,128)(2,1)}, bf16[1,128,1792]{2,1,0:T(8,128)(2,1)S(1)}, u32[]{:S(2)}, u32[]{:S(2)}) collective-permute-start(bf16[1,128,1792]{2,1,0:T(8,128)(2,1)} %get-tuple-element.14), channel_id=1, source_target_pairs={{4,8},{12,16},{20,24},{5,9},{13,17},{21,25},{6,10},{14,18},{22,26}... | collective-permute-start | bytes 1376264 | tf_op jit(solution)/shard_map/ppermute | solution.py:452
  66.8 22.0 %collective-permute-start.13 = (bf16[2,128,1792]{2,1,0:T(8,128)(2,1)}, bf16[2,128,1792]{2,1,0:T(8,128)(2,1)S(1)}, u32[]{:S(2)}, u32[]{:S(2)}) collective-permute-start(bf16[2,128,1792]{2,1,0:T(8,128)(2,1)} %get-tuple-element.16), channel_id=1, source_target_pairs={{8,0},{12,4},{16,8},{20,12},{24,16},{28,20},{9,1},{13,5},{17,9},{2... | collective-permute-start | bytes 2752520 | tf_op jit(solution)/shard_map/ppermute | solution.py:452
  68.1 20.7 %copy-start.6 = (bf16[2,128,1792]{2,1,0:T(8,128)(2,1)S(1)}, bf16[2,128,1792]{2,1,0:T(8,128)(2,1)}, u32[]{:S(2)}) copy-start(bf16[2,128,1792]{2,1,0:T(8,128)(2,1)} %get-tuple-element.15) | copy-start | bytes 2752516
  (2 other events, 1.2 us)

commit v4 on v3

--- a/solution.py
+++ b/solution.py
@@ -227,9 +227,17 @@
     return out, keep
 
 
+def tiles_ahead(heads, plan, queries, keys):
+    ready = tile_values(plan, 0, queries, keys)
+    for head in range(heads):
+        now = ready
+        if head + 1 < heads:
+            ready = tile_values(plan, head + 1, queries, keys)
+        yield head, now
+
+
 def collect_stats(heads, power, step, plan, queries, keys, rows, out_ref, slots):
-    for head in range(heads):
-        tiles, _ = tile_values(plan, head, queries, keys)
+    for head, (tiles, _) in tiles_ahead(heads, plan, queries, keys):
         parts = {}
         for (query_slots, _, mask), (_, _, _, raw, grads) in zip(plan, tiles):
             raw = jnp.where(mask, raw, FLOOR)
@@ -285,8 +293,7 @@
         if stop > start:
             put(start, stop, value[:, start - low : stop - low])
 
-    for head in range(heads):
-        tiles, keep = tile_values(plan, head, queries, keys)
+    for head, (tiles, keep) in tiles_ahead(heads, plan, queries, keys):
         sums = {}
 
         def add(name, value):
@@ -338,7 +345,7 @@
     by_parity(me, even, odd)
 
 
-def third_stats(heads, power, place_ref, lengths_ref, qt, ot, kb, vb, first_ref, out_ref):
+def third_stats(heads, power, place_ref, lengths_ref, qt, ot, kb, vb, first_ref, after, out_ref):
     rows, me, step = qt.shape[1], place_ref[0], pl.program_id(0)
 
     def even():
@@ -473,6 +480,7 @@
             out_specs=out_specs,
             out_shape=out_shape,
             scratch_shapes=[pltpu.VMEM((2 * GROUP, rows), jnp.float32)] * scratch,
+            compiler_params=pltpu.CompilerParams(vmem_limit_bytes=20 * 1024 * 1024),
             cost_estimate=pl.CostEstimate(
                 flops=flops, bytes_accessed=20 * rows * width, transcendentals=0
             ),
@@ -501,8 +509,8 @@
     )
     from_even = send(query_a, even_to_odd)
     third = call(
-        functools.partial(third_stats, heads, power), 1, 2, (*rows_third, *back, mine),
-        [wide] * 4 + [slim(2)], slim(1), stats_shape(1),
+        functools.partial(third_stats, heads, power), 1, 2, (*rows_third, *back, mine, query_a),
+        [wide] * 4 + [slim(2), pl.BlockSpec(memory_space=pl.ANY)], slim(1), stats_shape(1),
     )
     zig = send(third, zigzag)
     up = send(third, odd_ahead)
@@ -519,10 +527,11 @@
     def total(*terms):
         return sum(term.astype(jnp.float32) for term in terms).astype(jnp.bfloat16)
 
-    query_own = jnp.where(lax.rem(me, 2) == 0, query_b, query_a)
-    query_ready = total(query_own, from_even, from_odd, from_third)
     key_ready = total(key_own[:1], key_back_sum[:1])
     value_ready = total(key_own[1:], key_back_sum[1:])
+    query_own = jnp.where(lax.rem(me, 2) == 0, query_b, query_a)
+    query_own, key_ready, value_ready = lax.optimization_barrier((query_own, key_ready, value_ready))
+    query_ready = total(query_own, from_even, from_odd, from_third)
     return query_ready, key_ready, value_ready
 
 

time: 91 us -> 85.4 us (0.938)
  the two profiles are of different devices: /device:TPU:0 before, /device:TPU:20 now
where the time goes in v4:
time: 85.4 us; the launch traced here: 84.9 us
  waiting for transfers between devices  34.9 us (41%)
  starting transfers between devices  29.1 us (34%)
  Pallas kernels  10.2 us (12%)
  local copies, waits for them, and re-layouts  6.58 us (8%)
  other arithmetic  3.24 us (4%)
    ppermute x14, waiting for transfers between devices, send(): return lax.ppermute(value, 'seq', pairs)  34.9 us
    ppermute x14, starting transfers between devices, send(): return lax.ppermute(value, 'seq', pairs)  29.1 us
    pallas_call x4, Pallas kernels, call(): pl.pallas_call(kernel, grid=(steps,), in_specs=[smem, smem] + in_specs, o...  10.2 us
    unnamed x22, local copies, waits for them, and re-layouts  6.58 us
    convert_element_type x2, other arithmetic, total(): sum((term.astype(jnp.float32) for term in terms)).astype(jnp.bfloat16)  2.17 us
  transfers between devices with their start and end apart: 14, of which 7 were waited for; matrix products, arithmetic and copies ran while one was open for 3% of the time, Pallas kernels for 7%

profile of v4, /device:TPU:20, one launch (start us, length us, event | category | flops | bytes accessed | tf_op | source)
XLA Modules:
  0.0 84.9 jit_solution(5332022905980225323)
XLA Ops:
  0.6 1.6 %collective-permute-start = (bf16[1,128,1792]{2,1,0:T(8,128)(2,1)}, bf16[1,128,1792]{2,1,0:T(8,128)(2,1)S(1)}, u32[]{:S(2)}, u32[]{:S(2)}) collective-permute-start(bf16[1,128,1792]{2,1,0:T(8,128)(2,1)} %qo.5), channel_id=1, source_target_pairs={{0,4},{4,0},{8,12},{12,8},{16,20},{20,16},{24,28},{28,24},{1,5},{5... | collective-permute-start | bytes 1376264 | tf_op jit(solution)/shard_map/ppermute | solution.py:459
  2.7 3.5 %collective-permute-start.4 = (bf16[1,128,1792]{2,1,0:T(8,128)(2,1)}, bf16[1,128,1792]{2,1,0:T(8,128)(2,1)S(1)}, u32[]{:S(2)}, u32[]{:S(2)}) collective-permute-start(bf16[1,128,1792]{2,1,0:T(8,128)(2,1)} %ko.5), channel_id=1, source_target_pairs={{0,8},{4,12},{8,16},{12,20},{16,24},{20,28},{1,9},{5,13},{9,17},{1... | collective-permute-start | bytes 1376264 | tf_op jit(solution)/shard_map/ppermute | solution.py:459
  6.2 1.9 %collective-permute-start.5 = (bf16[1,128,1792]{2,1,0:T(8,128)(2,1)}, bf16[1,128,1792]{2,1,0:T(8,128)(2,1)S(1)}, u32[]{:S(2)}, u32[]{:S(2)}) collective-permute-start(bf16[1,128,1792]{2,1,0:T(8,128)(2,1)} %vo.5), channel_id=1, source_target_pairs={{0,8},{4,12},{8,16},{12,20},{16,24},{20,28},{1,9},{5,13},{9,17},{1... | collective-permute-start | bytes 1376264 | tf_op jit(solution)/shard_map/ppermute | solution.py:459
  8.1 6.2 %collective-permute-done.qm = bf16[1,128,1792]{2,1,0:T(8,128)(2,1)S(1)} collective-permute-done((bf16[1,128,1792]{2,1,0:T(8,128)(2,1)}, bf16[1,128,1792]{2,1,0:T(8,128)(2,1)S(1)}, u32[]{:S(2)}, u32[]{:S(2)}) %collective-permute-start) | collective-permute-done | bytes 458784 | tf_op jit(solution)/shard_map/ppermute | solution.py:459
  15.0 8.0 %collective-permute-done.1.om = bf16[1,128,1792]{2,1,0:T(8,128)(2,1)S(1)} collective-permute-done((bf16[1,128,1792]{2,1,0:T(8,128)(2,1)}, bf16[1,128,1792]{2,1,0:T(8,128)(2,1)S(1)}, u32[]{:S(2)}, u32[]{:S(2)}) %collective-permute-start.1) | collective-permute-done | bytes 458784 | tf_op jit(solution)/shard_map/ppermute | solution.py:459
  23.7 2.6 %collective-permute-done.5.vb = bf16[1,128,1792]{2,1,0:T(8,128)(2,1)S(1)} collective-permute-done((bf16[1,128,1792]{2,1,0:T(8,128)(2,1)}, bf16[1,128,1792]{2,1,0:T(8,128)(2,1)S(1)}, u32[]{:S(2)}, u32[]{:S(2)}) %collective-permute-start.5) | collective-permute-done | bytes 458784 | tf_op jit(solution)/shard_map/ppermute | solution.py:459
  26.4 1.0 %copy-done = bf16[1,128,1792]{2,1,0:T(8,128)(2,1)S(1)} copy-done((bf16[1,128,1792]{2,1,0:T(8,128)(2,1)S(1)}, bf16[1,128,1792]{2,1,0:T(8,128)(2,1)}, u32[]{:S(2)}) %copy-start) | copy-done | bytes 458776
  27.4 1.0 %copy-done.1 = bf16[1,128,1792]{2,1,0:T(8,128)(2,1)S(1)} copy-done((bf16[1,128,1792]{2,1,0:T(8,128)(2,1)S(1)}, bf16[1,128,1792]{2,1,0:T(8,128)(2,1)}, u32[]{:S(2)}) %copy-start.1) | copy-done | bytes 458776
  30.4 2.2 %shard_map.76.mine.first_ref = f32[48,128]{1,0:T(8,128)S(1)} custom-call(s32[1]{0:T(128)} %bitcast.place_ref, s32[8]{0:T(128)S(1)} %copy-done.9, bf16[1,128,1792]{2,1,0:T(8,128)(2,1)S(1)} %copy-done, bf16[1,128,1792]{2,1,0:T(8,128)(2,1)S(1)} %copy-done.1, bf16[1,128,1792]{2,1,0:T(8,128)(2,1)S(1)} %collective-permute-done.qm, ...), custom_call_target="tpu_custom_call" | custom-call | flops 704643072 | bytes 4587520 | tf_op jit(solution)/shard_map/pallas_call | solution.py:476
  32.7 1.9 %collective-permute-start.6 = (f32[48,128]{1,0:T(8,128)S(1)}, f32[48,128]{1,0:T(8,128)S(1)}, u32[]{:S(2)}, u32[]{:S(2)}) collective-permute-start(f32[48,128]{1,0:T(8,128)S(1)} %shard_map.76.mine.first_ref), channel_id=1, source_target_pairs={{0,4},{4,0},{8,12},{12,8},{16,20},{20,16},{24,28},{28,24},{1,5},{5... | collective-permute-start | bytes 73736 | tf_op jit(solution)/shard_map/ppermute | solution.py:459
  35.2 1.4 %collective-permute-done.6.mate = f32[48,128]{1,0:T(8,128)S(1)} collective-permute-done((f32[48,128]{1,0:T(8,128)S(1)}, f32[48,128]{1,0:T(8,128)S(1)}, u32[]{:S(2)}, u32[]{:S(2)}) %collective-permute-start.6) | collective-permute-done | bytes 24608 | tf_op jit(solution)/shard_map/ppermute | solution.py:459
  36.5 3.2 %shard_map.77 = (bf16[1,128,1792]{2,1,0:T(8,128)(2,1)S(1)}, bf16[2,128,1792]{2,1,0:T(8,128)(2,1)S(1)}, bf16[2,128,1792]{2,1,0:T(8,128)(2,1)S(1)}) custom-call(s32[1]{0:T(128)} %bitcast.place_ref, s32[8]{0:T(128)S(1)} %copy-done.9, bf16[1,128,1792]{2,1,0:T(8,128)(2,1)S(1)} %copy-done, bf16[1,128,1792]{2,1,0:T(8,128)(2,1)S(1)} %copy-done.1, ...), custom_call_target="tpu_custom_call" | custom-call | flops 880803840 | bytes 4587520 | tf_op jit(solution)/shard_map/pallas_call | solution.py:476
  41.2 7.2 %collective-permute-start.8 = (f32[24,128]{1,0:T(8,128)S(1)}, f32[24,128]{1,0:T(8,128)S(1)}, u32[]{:S(2)}, u32[]{:S(2)}) collective-permute-start(f32[24,128]{1,0:T(8,128)S(1)} %shard_map.78.third), channel_id=1, source_target_pairs={{4,8},{12,16},{20,24},{8,4},{16,12},{24,20},{5,9},{13,17},{21,25},... | collective-permute-start | bytes 36872 | tf_op jit(solution)/shard_map/ppermute | solution.py:459
  48.4 1.6 %collective-permute-done.8.zig = f32[24,128]{1,0:T(8,128)S(1)} collective-permute-done((f32[24,128]{1,0:T(8,128)S(1)}, f32[24,128]{1,0:T(8,128)S(1)}, u32[]{:S(2)}, u32[]{:S(2)}) %collective-permute-start.8) | collective-permute-done | bytes 12320 | tf_op jit(solution)/shard_map/ppermute | solution.py:459
  50.1 4.1 %shard_map.79 = (bf16[1,128,1792]{2,1,0:T(8,128)(2,1)S(1)}, bf16[1,128,1792]{2,1,0:T(8,128)(2,1)S(1)}, bf16[2,128,1792]{2,1,0:T(8,128)(2,1)S(1)}, bf16[2,128,1792]{2,1,0:T(8,128)(2,1)}) custom-call(s32[1]{0:T(128)} %bitcast.place_ref, s32[8]{0:T(128)S(1)} %copy-done.9, bf16[1,128,1792]{2,1,0:T(8,128)(2,1)S(1)} %copy-done, ...), custom_call_target="tpu_custom_call" | custom-call | flops 880803840 | bytes 4587520 | tf_op jit(solution)/shard_map/pallas_call | solution.py:476
  56.7 2.5 %collective-permute-start.10 = (bf16[2,128,1792]{2,1,0:T(8,128)(2,1)}, bf16[2,128,1792]{2,1,0:T(8,128)(2,1)S(1)}, u32[]{:S(2)}, u32[]{:S(2)}) collective-permute-start(bf16[2,128,1792]{2,1,0:T(8,128)(2,1)} %get-tuple-element.18), channel_id=1, source_target_pairs={{8,0},{12,4},{16,8},{20,12},{24,16},{28,20},{9,1},{13,5},{17,9},{2... | collective-permute-start | bytes 2752520 | tf_op jit(solution)/shard_map/ppermute | solution.py:459
  59.2 4.8 %collective-permute-start.11 = (bf16[1,128,1792]{2,1,0:T(8,128)(2,1)S(1)}, bf16[1,128,1792]{2,1,0:T(8,128)(2,1)S(1)}, u32[]{:S(2)}, u32[]{:S(2)}) collective-permute-start(bf16[1,128,1792]{2,1,0:T(8,128)(2,1)S(1)} %get-tuple-element.13.after), channel_id=1, source_target_pairs={{0,4},{8,12},{16,20},{24,28},{1,5},{9,13},{17,21},{25,29},{2,6},{1... | collective-permute-start | bytes 1376264 | tf_op jit(solution)/shard_map/ppermute | solution.py:459
  63.9 1.3 %collective-permute-start.12 = (bf16[1,128,1792]{2,1,0:T(8,128)(2,1)}, bf16[1,128,1792]{2,1,0:T(8,128)(2,1)S(1)}, u32[]{:S(2)}, u32[]{:S(2)}) collective-permute-start(bf16[1,128,1792]{2,1,0:T(8,128)(2,1)} %copy-done.8), channel_id=1, source_target_pairs={{4,0},{12,8},{20,16},{28,24},{5,1},{13,9},{21,17},{29,25},{6,2},{1... | collective-permute-start | bytes 1376264 | tf_op jit(solution)/shard_map/ppermute | solution.py:459
  65.2 1.3 %collective-permute-start.13 = (bf16[1,128,1792]{2,1,0:T(8,128)(2,1)}, bf16[1,128,1792]{2,1,0:T(8,128)(2,1)S(1)}, u32[]{:S(2)}, u32[]{:S(2)}) collective-permute-start(bf16[1,128,1792]{2,1,0:T(8,128)(2,1)} %copy-done.10), channel_id=1, source_target_pairs={{4,8},{12,16},{20,24},{5,9},{13,17},{21,25},{6,10},{14,18},{22,26}... | collective-permute-start | bytes 1376264 | tf_op jit(solution)/shard_map/ppermute | solution.py:459
  66.5 1.1 %broadcast_select_fusion = bf16[1,128,1792]{2,1,0:T(8,128)(2,1)S(1)} fusion(bf16[1,128,1792]{2,1,0:T(8,128)(2,1)} %copy-done.8, bf16[1,128,1792]{2,1,0:T(8,128)(2,1)S(1)} %get-tuple-element.13.after, pred[]{:T(512)S(6)} %eq.3), kind=kLoop, calls=%fused_computation.3 | loop fusion | flops 229376 | bytes 1376257 | tf_op jit(solution)/shard_map/jit(_where)/select_n | solution.py:532
  67.6 9.9 %collective-permute-done.10 = bf16[2,128,1792]{2,1,0:T(8,128)(2,1)S(1)} collective-permute-done((bf16[2,128,1792]{2,1,0:T(8,128)(2,1)}, bf16[2,128,1792]{2,1,0:T(8,128)(2,1)S(1)}, u32[]{:S(2)}, u32[]{:S(2)}) %collective-permute-start.10) | collective-permute-done | bytes 917536 | tf_op jit(solution)/shard_map/ppermute | solution.py:459
  77.5 1.1 %add_convert_fusion.1 = (bf16[1,128,1792]{2,1,0:T(8,128)(2,1)}, bf16[1,128,1792]{2,1,0:T(8,128)(2,1)}) fusion(bf16[2,128,1792]{2,1,0:T(8,128)(2,1)S(1)} %collective-permute-done.10, bf16[2,128,1792]{2,1,0:T(8,128)(2,1)S(1)} %copy-done.7), kind=kLoop, calls=%fused_computation.1 | loop fusion | flops 1835008 | bytes 2752512 | tf_op jit(solution)/shard_map/convert_element_type | solution.py:528
  78.6 5.2 %collective-permute-done.12 = bf16[1,128,1792]{2,1,0:T(8,128)(2,1)S(1)} collective-permute-done((bf16[1,128,1792]{2,1,0:T(8,128)(2,1)}, bf16[1,128,1792]{2,1,0:T(8,128)(2,1)S(1)}, u32[]{:S(2)}, u32[]{:S(2)}) %collective-permute-start.12) | collective-permute-done | bytes 458784 | tf_op jit(solution)/shard_map/ppermute | solution.py:459
  83.8 1.0 %add_convert_fusion = bf16[1,128,1792]{2,1,0:T(8,128)(2,1)} fusion(bf16[1,128,1792]{2,1,0:T(8,128)(2,1)S(1)} %collective-permute-done.13, bf16[1,128,1792]{2,1,0:T(8,128)(2,1)S(1)} %collective-permute-done.12, bf16[1,128,1792]{2,1,0:T(8,128)(2,1)S(1)} %collective-permute-done.11, bf16[1,128,1792]{2,1,0:T(8,128)(2,1)S(1)} %broadcast_select_fusion), kind=kLoop, calls=%fused_computation | loop fusion | flops 1835008 | bytes 2293760 | tf_op jit(solution)/shard_map/convert_element_type | solution.py:528
  (33 shorter events, 8.5 us)
Async XLA Ops:
  0.6 13.7 %collective-permute-start = (bf16[1,128,1792]{2,1,0:T(8,128)(2,1)}, bf16[1,128,1792]{2,1,0:T(8,128)(2,1)S(1)}, u32[]{:S(2)}, u32[]{:S(2)}) collective-permute-start(bf16[1,128,1792]{2,1,0:T(8,128)(2,1)} %qo.5), channel_id=1, source_target_pairs={{0,4},{4,0},{8,12},{12,8},{16,20},{20,16},{24,28},{28,24},{1,5},{5... | collective-permute-start | bytes 1376264 | tf_op jit(solution)/shard_map/ppermute | solution.py:459
  2.2 20.8 %collective-permute-start.1 = (bf16[1,128,1792]{2,1,0:T(8,128)(2,1)}, bf16[1,128,1792]{2,1,0:T(8,128)(2,1)S(1)}, u32[]{:S(2)}, u32[]{:S(2)}) collective-permute-start(bf16[1,128,1792]{2,1,0:T(8,128)(2,1)} %oo.5), channel_id=1, source_target_pairs={{0,4},{4,0},{8,12},{12,8},{16,20},{20,16},{24,28},{28,24},{1,5},{5... | collective-permute-start | bytes 1376264 | tf_op jit(solution)/shard_map/ppermute | solution.py:459
  2.7 21.0 %collective-permute-start.4 = (bf16[1,128,1792]{2,1,0:T(8,128)(2,1)}, bf16[1,128,1792]{2,1,0:T(8,128)(2,1)S(1)}, u32[]{:S(2)}, u32[]{:S(2)}) collective-permute-start(bf16[1,128,1792]{2,1,0:T(8,128)(2,1)} %ko.5), channel_id=1, source_target_pairs={{0,8},{4,12},{8,16},{12,20},{16,24},{20,28},{1,9},{5,13},{9,17},{1... | collective-permute-start | bytes 1376264 | tf_op jit(solution)/shard_map/ppermute | solution.py:459
  6.2 20.1 %collective-permute-start.5 = (bf16[1,128,1792]{2,1,0:T(8,128)(2,1)}, bf16[1,128,1792]{2,1,0:T(8,128)(2,1)S(1)}, u32[]{:S(2)}, u32[]{:S(2)}) collective-permute-start(bf16[1,128,1792]{2,1,0:T(8,128)(2,1)} %vo.5), channel_id=1, source_target_pairs={{0,8},{4,12},{8,16},{12,20},{16,24},{20,28},{1,9},{5,13},{9,17},{1... | collective-permute-start | bytes 1376264 | tf_op jit(solution)/shard_map/ppermute | solution.py:459
  14.3 25.4 %collective-permute-start.2 = (bf16[1,128,1792]{2,1,0:T(8,128)(2,1)S(1)}, bf16[1,128,1792]{2,1,0:T(8,128)(2,1)S(1)}, u32[]{:S(2)}, u32[]{:S(2)}) collective-permute-start(bf16[1,128,1792]{2,1,0:T(8,128)(2,1)S(1)} %collective-permute-done.qm), channel_id=1, source_target_pairs={{12,4},{20,12},{28,20},{13,5},{21,13},{29,21},{14,6},{22,14},{30,2... | collective-permute-start | bytes 1376264 | tf_op jit(solution)/shard_map/ppermute | solution.py:459
  23.0 16.7 %collective-permute-start.3 = (bf16[1,128,1792]{2,1,0:T(8,128)(2,1)S(1)}, bf16[1,128,1792]{2,1,0:T(8,128)(2,1)S(1)}, u32[]{:S(2)}, u32[]{:S(2)}) collective-permute-start(bf16[1,128,1792]{2,1,0:T(8,128)(2,1)S(1)} %collective-permute-done.1.om), channel_id=1, source_target_pairs={{12,4},{20,12},{28,20},{13,5},{21,13},{29,21},{14,6},{22,14},{30,2... | collective-permute-start | bytes 1376264 | tf_op jit(solution)/shard_map/ppermute | solution.py:459
  23.7 2.7 %copy-start.9 = (s32[8]{0:T(128)S(1)}, s32[8]{0:T(128)}, u32[]{:S(2)}) copy-start(s32[8]{0:T(128)} %lengths_ref.7) | copy-start | bytes 100
  26.3 1.0 %copy-start = (bf16[1,128,1792]{2,1,0:T(8,128)(2,1)S(1)}, bf16[1,128,1792]{2,1,0:T(8,128)(2,1)}, u32[]{:S(2)}) copy-start(bf16[1,128,1792]{2,1,0:T(8,128)(2,1)} %qo.5) | copy-start | bytes 1376260
  27.4 1.0 %copy-start.1 = (bf16[1,128,1792]{2,1,0:T(8,128)(2,1)S(1)}, bf16[1,128,1792]{2,1,0:T(8,128)(2,1)}, u32[]{:S(2)}) copy-start(bf16[1,128,1792]{2,1,0:T(8,128)(2,1)} %oo.5) | copy-start | bytes 1376260
  28.4 1.0 %copy-start.2 = (bf16[1,128,1792]{2,1,0:T(8,128)(2,1)S(1)}, bf16[1,128,1792]{2,1,0:T(8,128)(2,1)}, u32[]{:S(2)}) copy-start(bf16[1,128,1792]{2,1,0:T(8,128)(2,1)} %ko.5) | copy-start | bytes 1376260
  29.4 1.0 %copy-start.4 = (bf16[1,128,1792]{2,1,0:T(8,128)(2,1)S(1)}, bf16[1,128,1792]{2,1,0:T(8,128)(2,1)}, u32[]{:S(2)}) copy-start(bf16[1,128,1792]{2,1,0:T(8,128)(2,1)} %vo.5) | copy-start | bytes 1376260
  32.7 3.9 %collective-permute-start.6 = (f32[48,128]{1,0:T(8,128)S(1)}, f32[48,128]{1,0:T(8,128)S(1)}, u32[]{:S(2)}, u32[]{:S(2)}) collective-permute-start(f32[48,128]{1,0:T(8,128)S(1)} %shard_map.76.mine.first_ref), channel_id=1, source_target_pairs={{0,4},{4,0},{8,12},{12,8},{16,20},{20,16},{24,28},{28,24},{1,5},{5... | collective-permute-start | bytes 73736 | tf_op jit(solution)/shard_map/ppermute | solution.py:459
  34.5 13.9 %collective-permute-start.9 = (f32[48,128]{1,0:T(8,128)S(1)}, f32[48,128]{1,0:T(8,128)S(1)}, u32[]{:S(2)}, u32[]{:S(2)}) collective-permute-start(f32[48,128]{1,0:T(8,128)S(1)} %shard_map.76.mine.first_ref), channel_id=1, source_target_pairs={{12,4},{20,12},{28,20},{13,5},{21,13},{29,21},{14,6},{22,14},{30,2... | collective-permute-start | bytes 73736 | tf_op jit(solution)/shard_map/ppermute | solution.py:459
  39.7 10.3 %copy-start.3 = (bf16[1,128,1792]{2,1,0:T(8,128)(2,1)S(1)}, bf16[1,128,1792]{2,1,0:T(8,128)(2,1)}, u32[]{:S(2)}) copy-start(bf16[1,128,1792]{2,1,0:T(8,128)(2,1)} %ko.5) | copy-start | bytes 1376260
  39.8 10.3 %copy-start.5 = (bf16[1,128,1792]{2,1,0:T(8,128)(2,1)S(1)}, bf16[1,128,1792]{2,1,0:T(8,128)(2,1)}, u32[]{:S(2)}) copy-start(bf16[1,128,1792]{2,1,0:T(8,128)(2,1)} %vo.5) | copy-start | bytes 1376260
  40.5 7.9 %collective-permute-start.7 = (f32[24,128]{1,0:T(8,128)S(1)}, f32[24,128]{1,0:T(8,128)S(1)}, u32[]{:S(2)}, u32[]{:S(2)}) collective-permute-start(f32[24,128]{1,0:T(8,128)S(1)} %shard_map.78.third), channel_id=1, source_target_pairs={{4,12},{12,20},{20,28},{5,13},{13,21},{21,29},{6,14},{14,22},{22,3... | collective-permute-start | bytes 36872 | tf_op jit(solution)/shard_map/ppermute | solution.py:459
  41.2 8.9 %collective-permute-start.8 = (f32[24,128]{1,0:T(8,128)S(1)}, f32[24,128]{1,0:T(8,128)S(1)}, u32[]{:S(2)}, u32[]{:S(2)}) collective-permute-start(f32[24,128]{1,0:T(8,128)S(1)} %shard_map.78.third), channel_id=1, source_target_pairs={{4,8},{12,16},{20,24},{8,4},{16,12},{24,20},{5,9},{13,17},{21,25},... | collective-permute-start | bytes 36872 | tf_op jit(solution)/shard_map/ppermute | solution.py:459
  54.2 0.9 %copy-start.6 = (bf16[2,128,1792]{2,1,0:T(8,128)(2,1)}, bf16[2,128,1792]{2,1,0:T(8,128)(2,1)S(1)}, u32[]{:S(2)}) copy-start(bf16[2,128,1792]{2,1,0:T(8,128)(2,1)S(1)} %get-tuple-element.17) | copy-start | bytes 2752516
  55.1 0.8 copy-start.8
  56.7 20.8 %copy-start.7 = (bf16[2,128,1792]{2,1,0:T(8,128)(2,1)S(1)}, bf16[2,128,1792]{2,1,0:T(8,128)(2,1)}, u32[]{:S(2)}) copy-start(bf16[2,128,1792]{2,1,0:T(8,128)(2,1)} %copy-done.6) | copy-start | bytes 2752516
  56.7 20.8 %collective-permute-start.10 = (bf16[2,128,1792]{2,1,0:T(8,128)(2,1)}, bf16[2,128,1792]{2,1,0:T(8,128)(2,1)S(1)}, u32[]{:S(2)}, u32[]{:S(2)}) collective-permute-start(bf16[2,128,1792]{2,1,0:T(8,128)(2,1)} %get-tuple-element.18), channel_id=1, source_target_pairs={{8,0},{12,4},{16,8},{20,12},{24,16},{28,20},{9,1},{13,5},{17,9},{2... | collective-permute-start | bytes 2752520 | tf_op jit(solution)/shard_map/ppermute | solution.py:459
  59.2 19.5 %collective-permute-start.11 = (bf16[1,128,1792]{2,1,0:T(8,128)(2,1)S(1)}, bf16[1,128,1792]{2,1,0:T(8,128)(2,1)S(1)}, u32[]{:S(2)}, u32[]{:S(2)}) collective-permute-start(bf16[1,128,1792]{2,1,0:T(8,128)(2,1)S(1)} %get-tuple-element.13.after), channel_id=1, source_target_pairs={{0,4},{8,12},{16,20},{24,28},{1,5},{9,13},{17,21},{25,29},{2,6},{1... | collective-permute-start | bytes 1376264 | tf_op jit(solution)/shard_map/ppermute | solution.py:459
  63.9 19.9 %collective-permute-start.12 = (bf16[1,128,1792]{2,1,0:T(8,128)(2,1)}, bf16[1,128,1792]{2,1,0:T(8,128)(2,1)S(1)}, u32[]{:S(2)}, u32[]{:S(2)}) collective-permute-start(bf16[1,128,1792]{2,1,0:T(8,128)(2,1)} %copy-done.8), channel_id=1, source_target_pairs={{4,0},{12,8},{20,16},{28,24},{5,1},{13,9},{21,17},{29,25},{6,2},{1... | collective-permute-start | bytes 1376264 | tf_op jit(solution)/shard_map/ppermute | solution.py:459
  65.2 18.6 %collective-permute-start.13 = (bf16[1,128,1792]{2,1,0:T(8,128)(2,1)}, bf16[1,128,1792]{2,1,0:T(8,128)(2,1)S(1)}, u32[]{:S(2)}, u32[]{:S(2)}) collective-permute-start(bf16[1,128,1792]{2,1,0:T(8,128)(2,1)} %copy-done.10), channel_id=1, source_target_pairs={{4,8},{12,16},{20,24},{5,9},{13,17},{21,25},{6,10},{14,18},{22,26}... | collective-permute-start | bytes 1376264 | tf_op jit(solution)/shard_map/ppermute | solution.py:459
  (1 other events, 0.8 us)

commit v5 on v0

--- a/solution.py
+++ b/solution.py
@@ -1,9 +1,15 @@
+import functools
+import math
 import jax
 import jax.numpy as jnp
 from jax import lax
+from jax.experimental import pallas as pl
+from jax.experimental.pallas import tpu as pltpu
 from jax.sharding import PartitionSpec as P
 
 HEAD = 224
+LANES = 128
+FLOOR = -1e30
 
 
 def pick_slot(stacked, slot):
@@ -14,7 +20,7 @@
     return lax.dynamic_update_index_in_dim(stacked, update, slot, 0)
 
 
-def shards(queries, key_vectors, value_vectors, out_grad, doc_lengths):
+def spread_shards(queries, key_vectors, value_vectors, out_grad, doc_lengths):
     local_rows = queries.shape[1]
     local_width = queries.shape[2]
     head_count = local_width // HEAD
@@ -158,6 +164,385 @@
     return (query_out, settle(key_back), settle(value_back))
 
 
+NT = ((1,), (1,))
+NN = ((1,), (0,))
+TN = ((0,), (0,))
+GROUP = 8
+
+
+def head_span(head):
+    low = head * HEAD // LANES * LANES
+    high = -(-(head + 1) * HEAD // LANES) * LANES
+    return low, high
+
+
+def head_mask(head):
+    low, high = head_span(head)
+    lane = lax.broadcasted_iota(jnp.int32, (1, high - low), 1) + low
+    inside = (lane >= head * HEAD) & (lane < (head + 1) * HEAD)
+    return inside.astype(jnp.float32).astype(jnp.bfloat16)
+
+
+def matmul(left, right, dims):
+    return lax.dot_general(left, right, (dims, ((), ())), preferred_element_type=jnp.float32)
+
+
+def stack(values, axis):
+    return values[0] if len(values) == 1 else jnp.concatenate(values, axis=axis)
+
+
+def allowed(lengths_ref, rows, query_block, key_block):
+    shape = (rows, rows)
+    position = query_block * rows + lax.broadcasted_iota(jnp.int32, shape, 1)
+    keys = key_block * rows + lax.broadcasted_iota(jnp.int32, shape, 0)
+    start = jnp.zeros_like(position)
+    bound = jnp.int32(0)
+    for doc in range(lengths_ref.shape[0]):
+        bound = bound + lengths_ref[doc]
+        start = jnp.where(position >= bound, bound, start)
+    return (keys >= start) & (keys <= position)
+
+
+def make_tile(lengths_ref, rows, queries, keys):
+    mask = stack(
+        [stack([allowed(lengths_ref, rows, q, k) for _, q in queries], 1) for _, k in keys], 0
+    )
+    return [slot for slot, _ in queries], [slot for slot, _ in keys], mask
+
+
+def tile_values(plan, head, queries, keys, products):
+    low, high = head_span(head)
+    keep = head_mask(head)
+
+    def gather(refs, number, slots):
+        return stack([refs[slot][number][0, :, low:high] for slot in slots], 0)
+
+    out = []
+    for query_slots, key_slots, _ in plan:
+        q = [gather(queries, number, query_slots) for number in range(products)]
+        k = [gather(keys, number, key_slots) * keep for number in range(products)]
+        out.append((q, k, [matmul(b, a, NT) for a, b in zip(q, k)]))
+    return out, keep
+
+
+def tiles_ahead(heads, plan, queries, keys, products):
+    ready = tile_values(plan, 0, queries, keys, products)
+    for head in range(heads):
+        now = ready
+        if head + 1 < heads:
+            ready = tile_values(plan, head + 1, queries, keys, products)
+        yield head, now
+
+
+def plans(third, lengths_ref, rows, me):
+    def even():
+        return [make_tile(lengths_ref, rows, ((0, me), (1, me + 1)), ((0, me), (1, me - 2)))]
+
+    def odd():
+        met = ((0, me), (1, me - 1)) + (((2, me + 1),) if third else ())
+        return [
+            make_tile(lengths_ref, rows, ((0, me),), ((0, me),)),
+            make_tile(lengths_ref, rows, met, ((1, me - 2),)),
+        ]
+
+    return even, odd
+
+
+def by_parity(me, even, odd):
+    pl.when(lax.rem(me, 2) == 0)(even)
+    pl.when(lax.rem(me, 2) == 1)(odd)
+
+
+def at_start(step, refs):
+    @pl.when(step == 0)
+    def _():
+        for ref in refs:
+            ref[...] = jnp.zeros_like(ref)
+
+
+def lane_cut(value, number, rows):
+    return value[:, number * rows : (number + 1) * rows]
+
+
+def row_of(group, kinds, kind, head):
+    return pl.ds((group * kinds + kind) * GROUP + head, 1)
+
+
+def per_query(slots, kinds, kind, head, ref):
+    return stack([ref[row_of(slot, kinds, kind, head), :] for slot in slots], 1)
+
+
+def stats_kernel(third, heads, power, place_ref, lengths_ref, *refs):
+    count = 3 if third else 2
+    query_refs, (k_own, k_back, o_own, v_own) = refs[:count], refs[count : count + 4]
+    o_copy, v_copy, out_ref = refs[count + 4 :]
+    rows, me, step = k_own.shape[1], place_ref[0], pl.program_id(0)
+    at_start(step, [out_ref])
+    o_copy[...], v_copy[...] = o_own[...], v_own[...]
+    queries, keys = [(ref,) for ref in query_refs], ((k_own,), (k_back,))
+
+    def run(plan):
+        for head, (tiles, _) in tiles_ahead(heads, plan, queries, keys, 1):
+            parts = {}
+            for (query_slots, _, mask), (_, _, (raw,)) in zip(plan, tiles):
+                raw = jnp.where(mask, raw, FLOOR)
+                for number, slot in enumerate(query_slots):
+                    parts.setdefault(slot, []).append(lane_cut(raw, number, rows))
+            for slot, pieces in parts.items():
+                top = functools.reduce(
+                    jnp.maximum, [jnp.max(p, axis=0, keepdims=True) for p in pieces]
+                )
+                sums = sum(
+                    jnp.sum(jnp.exp2((p - top) * power), axis=0, keepdims=True) for p in pieces
+                )
+                out_ref[row_of(slot, 2, 0, step * heads + head), :] = top
+                out_ref[row_of(slot, 2, 1, step * heads + head), :] = sums
+
+    even, odd = plans(third, lengths_ref, rows, me)
+    by_parity(me, lambda: run(even()), lambda: run(odd()))
+
+
+def group_parts(third, odd, kinds, mine, messages):
+    size = kinds * GROUP
+
+    def group(ref, number):
+        return ref[number * size : (number + 1) * size, :]
+
+    own = [group(mine, 0), group(messages[0], 1)]
+    mate = [group(mine, 1), group(messages[0], 0)]
+    if not third:
+        return [own, mate]
+    _, zig, up, down = messages
+    if odd:
+        return [own, mate + [group(up, 2)], [group(mine, 2), group(zig, 0), group(down, 1)]]
+    return [own + [group(zig, 2)], mate]
+
+
+def merge_stats(scaling, parts):
+    split = [(jnp.where(p[GROUP:] > 0, p[:GROUP], FLOOR), p[GROUP:]) for p in parts]
+    top = functools.reduce(jnp.maximum, [s[0] for s in split])
+    total = sum(jnp.exp((s[0] - top) * scaling) * s[1] for s in split)
+    return top + jnp.log(jnp.where(total > 0, total, 1.0)) / scaling
+
+
+class Emitter:
+    def __init__(self, outs):
+        self.outs, self.carry = outs, {}
+
+    def emit(self, head, name, value):
+        ref = self.outs[name]
+        low, high = head_span(head)
+        first, last = head * HEAD % LANES == 0, (head + 1) * HEAD % LANES == 0
+        start, stop = low, high
+        if not first:
+            shared = value[:, :LANES] + self.carry.pop(name)
+            ref[0, :, low : low + LANES] = shared.astype(jnp.bfloat16)
+            start = low + LANES
+        if not last:
+            self.carry[name] = value[:, high - LANES - low :]
+            stop = high - LANES
+        if stop > start:
+            ref[0, :, start:stop] = value[:, start - low : stop - low].astype(jnp.bfloat16)
+
+
+def add_rows(sums, kind, slots, value, rows):
+    for number, slot in enumerate(slots):
+        piece = value[number * rows : (number + 1) * rows]
+        name = (kind, slot)
+        sums[name] = sums[name] + piece if name in sums else piece
+
+
+def add_lanes(sums, slots, value, rows):
+    for number, slot in enumerate(slots):
+        piece = lane_cut(value, number, rows)
+        sums[slot] = sums[slot] + piece if slot in sums else piece
+
+
+def split_refs(third, refs):
+    count = 3 if third else 2
+    queries = [(refs[2 * n], refs[2 * n + 1]) for n in range(count)]
+    keys = [(refs[2 * n], refs[2 * n + 1]) for n in range(count, count + 2)]
+    return queries, keys, refs[2 * count + 4 :]
+
+
+def values_kernel(third, heads, scaling, power, place_ref, lengths_ref, *refs):
+    queries, keys, refs = split_refs(third, refs)
+    messages = 4 if third else 1
+    mine, others = refs[0], refs[1 : 1 + messages]
+    value_own, value_back, shift_ref, dots_ref = refs[1 + messages :]
+    rows, me, step = keys[0][0].shape[1], place_ref[0], pl.program_id(0)
+    at_start(step, [dots_ref])
+
+    def run(odd, plan):
+        groups = group_parts(third, odd, 2, mine, others)
+        for number, parts in enumerate(groups):
+            shift_ref[number * GROUP : (number + 1) * GROUP, :] = merge_stats(scaling, parts)
+        out = Emitter({("v", 0): value_own, ("v", 1): value_back})
+        for head, (tiles, keep) in tiles_ahead(heads, plan, queries, keys, 2):
+            at = step * heads + head
+            sums, dots = {}, {}
+            for (query_slots, key_slots, mask), ((_, o), _, (raw, grads)) in zip(plan, tiles):
+                shift = per_query(query_slots, 1, 0, at, shift_ref)
+                weight = jnp.where(mask, jnp.exp2((raw - shift) * power), 0.0)
+                add_lanes(dots, query_slots, jnp.sum(weight * grads, axis=0, keepdims=True), rows)
+                add_rows(
+                    sums, "v", key_slots, matmul(weight.astype(jnp.bfloat16), o * keep, NN), rows
+                )
+            for slot, value in dots.items():
+                dots_ref[row_of(slot, 1, 0, at), :] = value
+            for name, value in sums.items():
+                out.emit(head, name, value)
+
+    even, odd = plans(third, lengths_ref, rows, me)
+    by_parity(me, lambda: run(False, even()), lambda: run(True, odd()))
+
+
+def keys_kernel(third, heads, scaling, power, place_ref, lengths_ref, *refs):
+    queries, keys, refs = split_refs(third, refs)
+    messages = 4 if third else 1
+    shift_ref, mine, others = refs[0], refs[1], refs[2 : 2 + messages]
+    key_own, key_back, *query_refs, total_ref = refs[2 + messages :]
+    rows, me, step = keys[0][0].shape[1], place_ref[0], pl.program_id(0)
+
+    def run(odd, plan):
+        for number, parts in enumerate(group_parts(third, odd, 1, mine, others)):
+            total_ref[number * GROUP : (number + 1) * GROUP, :] = sum(parts)
+        outs = {("k", 0): key_own, ("k", 1): key_back}
+        outs.update({("q", slot): ref for slot, ref in enumerate(query_refs)})
+        out = Emitter(outs)
+        if third and not odd:
+            query_refs[2][...] = jnp.zeros_like(query_refs[2])
+        for head, (tiles, keep) in tiles_ahead(heads, plan, queries, keys, 2):
+            at = step * heads + head
+            sums = {}
+            for (query_slots, key_slots, mask), ((q, _), (k, _), (raw, grads)) in zip(plan, tiles):
+                shift = per_query(query_slots, 1, 0, at, shift_ref)
+                dots = per_query(query_slots, 1, 0, at, total_ref)
+                weight = jnp.where(mask, jnp.exp2((raw - shift) * power), 0.0)
+                slope = (weight * (grads - dots) * scaling).astype(jnp.bfloat16)
+                add_rows(sums, "k", key_slots, matmul(slope, q * keep, NN), rows)
+                add_rows(sums, "q", query_slots, matmul(slope, k, TN), rows)
+            for name, value in sums.items():
+                out.emit(head, name, value)
+
+    even, odd = plans(third, lengths_ref, rows, me)
+    by_parity(me, lambda: run(False, even()), lambda: run(True, odd()))
+
+
+def halo_program(third, queries, key_vectors, value_vectors, out_grad, doc_lengths):
+    _, rows, width = queries.shape
+    seq_size = lax.axis_size("seq")
+    me = lax.axis_index("seq").astype(jnp.int32)
+    scaling = HEAD ** (-0.5)
+    power = scaling * math.log2(math.e)
+    steps = width // HEAD // 4
+    part = width // steps
+    heads = part // HEAD
+    count = 3 if third else 2
+    devices = range(seq_size)
+    odds = [s for s in devices if s % 2]
+    mates = [(s, s ^ 1) for s in devices]
+    ahead = [(s, s + 2) for s in devices if s + 2 < seq_size]
+    behind = [(s, s - 2) for s in devices if s >= 2]
+    odd_ahead = [(s, s + 2) for s in odds if s + 2 < seq_size]
+    odd_behind = [(s, s - 2) for s in odds if s >= 2]
+    odd_next = [(s, s + 1) for s in odds if s + 1 < seq_size]
+    zigzag = odd_next + [(t, s) for s, t in odd_next]
+
+    def send(value, pairs):
+        return lax.ppermute(value, "seq", pairs)
+
+    def exchange(value):
+        return [send(value, pairs) for pairs in ((mates, zigzag, odd_ahead, odd_behind) if third else (mates,))]
+
+    smem = pl.BlockSpec(memory_space=pltpu.SMEM)
+    wide = pl.BlockSpec((1, rows, part), lambda step: (0, 0, step))
+    wide_shape = jax.ShapeDtypeStruct((1, rows, width), jnp.bfloat16)
+
+    def slim(kinds):
+        return pl.BlockSpec((count * kinds * GROUP, rows), lambda step: (0, 0))
+
+    def slim_shape(kinds):
+        return jax.ShapeDtypeStruct((count * kinds * GROUP, rows), jnp.float32)
+
+    def call(kernel, products, wides, slims, outs, slim_outs, scratch=()):
+        flops = 2 * products * 4 * rows * rows * width * 3 // 2
+        return pl.pallas_call(
+            kernel,
+            grid=(steps,),
+            in_specs=[smem, smem] + [wide] * len(wides) + [slim(kinds) for kinds, _ in slims],
+            out_specs=[wide] * outs + [slim(kinds) for kinds in slim_outs],
+            out_shape=[wide_shape] * outs + [slim_shape(kinds) for kinds in slim_outs],
+            scratch_shapes=scratch,
+            compiler_params=pltpu.CompilerParams(vmem_limit_bytes=20 * 1024 * 1024),
+            cost_estimate=pl.CostEstimate(
+                flops=flops, bytes_accessed=20 * rows * width, transcendentals=0
+            ),
+        )(me[None], doc_lengths, *wides, *[value for _, value in slims])
+
+    query_mate = send(queries, mates)
+    key_back = send(key_vectors, ahead)
+    grad_mate = send(out_grad, mates)
+    value_back = send(value_vectors, ahead)
+    query_rows = [queries, query_mate] + ([send(query_mate, odd_behind)] if third else [])
+    grad_own, value_own, stats = call(
+        functools.partial(stats_kernel, third, heads, power), 1,
+        [*query_rows, key_vectors, key_back, out_grad, value_vectors], [], 2, [2],
+    )
+    grad_rows = [grad_own, grad_mate] + ([send(grad_mate, odd_behind)] if third else [])
+    tensors = [t for two in zip(query_rows, grad_rows) for t in two]
+    tensors += [key_vectors, value_own, key_back, value_back]
+    value_part, value_sent, shift, dots = call(
+        functools.partial(values_kernel, third, heads, scaling, power), 3, tensors,
+        [(2, value) for value in [stats] + exchange(stats)], 2, [1, 1],
+    )
+    value_received = send(value_sent, behind)
+    key_part, key_sent, query_part, *query_sent = call(
+        functools.partial(keys_kernel, third, heads, scaling, power), 4, tensors,
+        [(1, value) for value in [shift, dots] + exchange(dots)], 2 + count, [],
+        [pltpu.VMEM((count * GROUP, rows), jnp.float32)],
+    )
+    key_received = send(key_sent, behind)
+    query_received = [send(value, pairs) for value, pairs in zip(query_sent, (mates, odd_next))]
+
+    def total(*terms):
+        return sum(term.astype(jnp.float32) for term in terms).astype(jnp.bfloat16)
+
+    return (
+        total(query_part, *query_received),
+        total(key_part, key_received),
+        total(value_part, value_received),
+    )
+
+
+def needs_third(rows, doc_lengths):
+    count = doc_lengths.shape[0]
+    index = jnp.arange(count)
+    ends = jnp.sum(jnp.where(index[None, :] <= index[:, None], doc_lengths[None, :], 0), axis=1)
+    first, last = (ends - doc_lengths) // rows, (ends - 1) // rows
+    return jnp.any((last - first >= 3) & (last % 2 == 0))
+
+
+def halo_shards(*arguments):
+    rows, doc_lengths = arguments[0].shape[1], arguments[-1]
+    return lax.cond(
+        needs_third(rows, doc_lengths),
+        functools.partial(halo_program, True),
+        functools.partial(halo_program, False),
+        *arguments,
+    )
+
+
+def shards(queries, key_vectors, value_vectors, out_grad, doc_lengths):
+    _, rows, width = queries.shape
+    seq_size = lax.axis_size("seq")
+    longest = rows * seq_size * 3 // 8
+    fits = longest <= 3 * rows and seq_size % 2 == 0 and rows == LANES
+    heads = width // HEAD
+    plan = halo_shards if fits and heads % 4 == 0 and heads <= GROUP else spread_shards
+    return plan(queries, key_vectors, value_vectors, out_grad, doc_lengths)
+
+
 def solution(mesh):
     return jax.shard_map(
         shards,

time: 137 us -> 57 us (0.42)
  waiting for transfers between devices: 74.7 us -> 26.7 us
  local copies, waits for them, and re-layouts: 22.1 us -> 0.01 us
  starting transfers between devices: 29.9 us -> 16 us
  Pallas kernels: 0 us -> 8.45 us
  matrix products: 6.32 us -> 0 us
  other arithmetic: 2.27 us -> 4.14 us
    all_to_all x7 -> x0, waiting for transfers between devices: 74.7 us -> none  [the longest x1 12.4 us: shards(): lax.all_to_all(spread(out_grad), 'seq', split_axis=1, concat_axis=0, tile...]
    all_to_all x7 -> x0, starting transfers between devices: 29.9 us -> none  [the longest x1 7.38 us: shards(): lax.all_to_all(spread(queries), 'seq', split_axis=1, concat_axis=0, tiled...]
    ppermute x0 -> x9, waiting for transfers between devices: none -> 26.7 us  [send(): return lax.ppermute(value, 'seq', pairs)]
    ppermute x0 -> x9, starting transfers between devices: none -> 16 us  [send(): return lax.ppermute(value, 'seq', pairs)]
    unnamed x39 -> x6, local copies, waits for them, and re-layouts: 15.2 us -> 0.01 us
    pallas_call x0 -> x3, Pallas kernels: none -> 8.45 us  [call(): pl.pallas_call(kernel, grid=(steps,), in_specs=[smem, smem] + [wide] * le...]
    dot_general x18 -> x0, matrix products: 6.32 us -> none  [the longest x3 1.3 us: score_tile(): jnp.dot(query_rows, key_rows.T, preferred_element_type=jnp.float32)]
    gather x2 -> x0, local copies, waits for them, and re-layouts: 4.54 us -> none  [shards(): doc_stack = jnp.take(doc_index, pos_stack)]
  transfers between devices with their start and end apart: 7 -> 9, of which waited for: 7 -> 7; matrix products, arithmetic and copies ran while one was open for 11% -> 3% of each run, Pallas kernels for 0% -> 10%
where the time goes in v5:
time: 57 us; the launch traced here: 56.7 us
  waiting for transfers between devices  26.7 us (47%)
  starting transfers between devices  16 us (28%)
  Pallas kernels  8.45 us (15%)
  other arithmetic  4.14 us (7%)
  between operations  1.29 us (2%)
    ppermute x9, waiting for transfers between devices, send(): return lax.ppermute(value, 'seq', pairs)  26.7 us
    ppermute x9, starting transfers between devices, send(): return lax.ppermute(value, 'seq', pairs)  16 us
    pallas_call x3, Pallas kernels, call(): pl.pallas_call(kernel, grid=(steps,), in_specs=[smem, smem] + [wide] * le...  8.45 us
    add x3, other arithmetic, total(): sum((term.astype(jnp.float32) for term in terms)).astype(jnp.bfloat16)  2.65 us
  transfers between devices with their start and end apart: 9, of which 7 were waited for; matrix products, arithmetic and copies ran while one was open for 3% of the time, Pallas kernels for 10%

profile of v5, /device:TPU:0, one launch (start us, length us, event | category | flops | bytes accessed | tf_op | source)
XLA Modules:
  0.0 56.7 jit_solution(7281960028694646743)
XLA Ops:
  0.6 0.8 %select_reduce_fusion = s32[8]{0:T(128)S(1)} fusion(s32[8]{0:T(128)} %param.11), kind=kLoop, calls=%fused_computation.6 | loop fusion | flops 184 | bytes 64 | tf_op jit(solution)/shard_map/reduce_sum | solution.py:521
  1.5 0.7 %and_reduce_fusion = pred[]{:T(512)} fusion(s32[8]{0:T(128)S(1)} %select_reduce_fusion, s32[8]{0:T(128)S(1)} %copy-done.4), kind=kLoop, calls=%fused_computation.10 | loop fusion | flops 383 | bytes 65 | tf_op jit(solution)/shard_map/reduce_or | solution.py:523
  2.8 53.9 %conditional.4 = (bf16[1,128,1792]{2,1,0:T(8,128)(2,1)}, bf16[1,128,1792]{2,1,0:T(8,128)(2,1)}, bf16[1,128,1792]{2,1,0:T(8,128)(2,1)}) conditional(s32[]{:T(128)} %convert_element_type.78, (bf16[1,128,1792]{2,1,0:T(8,128)(2,1)}, bf16[1,128,1792]{2,1,0:T(8,128)(2,1)}, s32[8]{0:T(128)S(1)}, bf16[1,128,1792]{2,1,0:T(8,128)(2,1)}, ...), branch_computations={%region_2.3_spmd, %region_3.4_spmd} | conditional | flops 2821783552 | bytes 40960832
  2.8 3.0 %collective-permute-start = (bf16[1,128,1792]{2,1,0:T(8,128)(2,1)}, bf16[1,128,1792]{2,1,0:T(8,128)(2,1)S(1)}, u32[]{:S(2)}, u32[]{:S(2)}) collective-permute-start(bf16[1,128,1792]{2,1,0:T(8,128)(2,1)} %get-tuple-element.39.refs_0_), channel_id=1, source_target_pairs={{0,4},{4,0},{8,12},{12,8},{16,20},{20,16},{24,28},{28,24},{1,5},{5... | collective-permute-start | bytes 1376264 | tf_op jit(solution)/shard_map/cond/branch_0_fun/ppermute | solution.py:453
  5.8 3.5 %collective-permute-start.1 = (bf16[1,128,1792]{2,1,0:T(8,128)(2,1)}, bf16[1,128,1792]{2,1,0:T(8,128)(2,1)S(1)}, u32[]{:S(2)}, u32[]{:S(2)}) collective-permute-start(bf16[1,128,1792]{2,1,0:T(8,128)(2,1)} %get-tuple-element.40.refs_2_.refs_4_), channel_id=1, source_target_pairs={{0,8},{4,12},{8,16},{12,20},{16,24},{20,28},{1,9},{5,13},{9,17},{1... | collective-permute-start | bytes 1376264 | tf_op jit(solution)/shard_map/cond/branch_0_fun/ppermute | solution.py:453
  9.3 0.6 %collective-permute-start.2 = (bf16[1,128,1792]{2,1,0:T(8,128)(2,1)}, bf16[1,128,1792]{2,1,0:T(8,128)(2,1)S(1)}, u32[]{:S(2)}, u32[]{:S(2)}) collective-permute-start(bf16[1,128,1792]{2,1,0:T(8,128)(2,1)} %get-tuple-element.41.refs_4_), channel_id=1, source_target_pairs={{0,4},{4,0},{8,12},{12,8},{16,20},{20,16},{24,28},{28,24},{1,5},{5... | collective-permute-start | bytes 1376264 | tf_op jit(solution)/shard_map/cond/branch_0_fun/ppermute | solution.py:453
  9.9 3.5 %collective-permute-start.3 = (bf16[1,128,1792]{2,1,0:T(8,128)(2,1)}, bf16[1,128,1792]{2,1,0:T(8,128)(2,1)S(1)}, u32[]{:S(2)}, u32[]{:S(2)}) collective-permute-start(bf16[1,128,1792]{2,1,0:T(8,128)(2,1)} %get-tuple-element.42.refs_5_), channel_id=1, source_target_pairs={{0,8},{4,12},{8,16},{12,20},{16,24},{20,28},{1,9},{5,13},{9,17},{1... | collective-permute-start | bytes 1376264 | tf_op jit(solution)/shard_map/cond/branch_0_fun/ppermute | solution.py:453
  13.4 4.0 %collective-permute-done.refs_1_.refs_2_ = bf16[1,128,1792]{2,1,0:T(8,128)(2,1)S(1)} collective-permute-done((bf16[1,128,1792]{2,1,0:T(8,128)(2,1)}, bf16[1,128,1792]{2,1,0:T(8,128)(2,1)S(1)}, u32[]{:S(2)}, u32[]{:S(2)}) %collective-permute-start) | collective-permute-done | bytes 458784 | tf_op jit(solution)/shard_map/cond/branch_0_fun/ppermute | solution.py:453
  17.4 3.2 %collective-permute-done.1.refs_3_.refs_6_ = bf16[1,128,1792]{2,1,0:T(8,128)(2,1)S(1)} collective-permute-done((bf16[1,128,1792]{2,1,0:T(8,128)(2,1)}, bf16[1,128,1792]{2,1,0:T(8,128)(2,1)S(1)}, u32[]{:S(2)}, u32[]{:S(2)}) %collective-permute-start.1) | collective-permute-done | bytes 458784 | tf_op jit(solution)/shard_map/cond/branch_0_fun/ppermute | solution.py:453
  20.5 2.6 %branch_0_fun.3 = (bf16[1,128,1792]{2,1,0:T(8,128)(2,1)S(1)}, bf16[1,128,1792]{2,1,0:T(8,128)(2,1)S(1)}, f32[32,128]{1,0:T(8,128)S(1)}) custom-call(s32[1]{0:T(128)} %bitcast.place_ref, s32[8]{0:T(128)S(1)} %get-tuple-element.38.lengths_ref, bf16[1,128,1792]{2,1,0:T(8,128)(2,1)} %get-tuple-element.39.refs_0_, ...), custom_call_target="tpu_custom_call" | custom-call | flops 352321536 | bytes 4587520 | tf_op jit(solution)/shard_map/cond/branch_0_fun/pallas_call | solution.py:470
  23.8 2.8 %collective-permute-done.2.refs_3_ = bf16[1,128,1792]{2,1,0:T(8,128)(2,1)S(1)} collective-permute-done((bf16[1,128,1792]{2,1,0:T(8,128)(2,1)}, bf16[1,128,1792]{2,1,0:T(8,128)(2,1)S(1)}, u32[]{:S(2)}, u32[]{:S(2)}) %collective-permute-start.2) | collective-permute-done | bytes 458784 | tf_op jit(solution)/shard_map/cond/branch_0_fun/ppermute | solution.py:453
  26.5 2.4 %collective-permute-done.3.refs_7_ = bf16[1,128,1792]{2,1,0:T(8,128)(2,1)S(1)} collective-permute-done((bf16[1,128,1792]{2,1,0:T(8,128)(2,1)}, bf16[1,128,1792]{2,1,0:T(8,128)(2,1)S(1)}, u32[]{:S(2)}, u32[]{:S(2)}) %collective-permute-start.3) | collective-permute-done | bytes 458784 | tf_op jit(solution)/shard_map/cond/branch_0_fun/ppermute | solution.py:453
  28.9 2.6 %branch_0_fun.4 = (bf16[1,128,1792]{2,1,0:T(8,128)(2,1)S(1)}, bf16[1,128,1792]{2,1,0:T(8,128)(2,1)S(1)}, f32[16,128]{1,0:T(8,128)S(1)}, f32[16,128]{1,0:T(8,128)S(1)}) custom-call(s32[1]{0:T(128)} %bitcast.place_ref, s32[8]{0:T(128)S(1)} %get-tuple-element.38.lengths_ref, bf16[1,128,1792]{2,1,0:T(8,128)(2,1)S(1)} %copy-done, ...), custom_call_target="tpu_custom_call" | custom-call | flops 1056964608 | bytes 4587520 | tf_op jit(solution)/shard_map/cond/branch_0_fun/pallas_call | solution.py:470
  31.5 1.3 %collective-permute-start.8 = (bf16[1,128,1792]{2,1,0:T(8,128)(2,1)S(1)}, bf16[1,128,1792]{2,1,0:T(8,128)(2,1)S(1)}, u32[]{:S(2)}, u32[]{:S(2)}) collective-permute-start(bf16[1,128,1792]{2,1,0:T(8,128)(2,1)S(1)} %get-tuple-element.53), channel_id=1, source_target_pairs={{8,0},{12,4},{16,8},{20,12},{24,16},{28,20},{9,1},{13,5},{17,9},{2... | collective-permute-start | bytes 1376264 | tf_op jit(solution)/shard_map/cond/branch_0_fun/ppermute | solution.py:453
  32.8 0.9 %collective-permute-start.5 = (f32[16,128]{1,0:T(8,128)S(1)}, f32[16,128]{1,0:T(8,128)S(1)}, u32[]{:S(2)}, u32[]{:S(2)}) collective-permute-start(f32[16,128]{1,0:T(8,128)S(1)} %get-tuple-element.47.refs_9_), channel_id=1, source_target_pairs={{0,4},{4,0},{8,12},{12,8},{16,20},{20,16},{24,28},{28,24},{1,5},{5... | collective-permute-start | bytes 24584 | tf_op jit(solution)/shard_map/cond/branch_0_fun/ppermute | solution.py:453
  33.8 2.8 %collective-permute-done.5.refs_10_ = f32[16,128]{1,0:T(8,128)S(1)} collective-permute-done((f32[16,128]{1,0:T(8,128)S(1)}, f32[16,128]{1,0:T(8,128)S(1)}, u32[]{:S(2)}, u32[]{:S(2)}) %collective-permute-start.5) | collective-permute-done | bytes 8224 | tf_op jit(solution)/shard_map/cond/branch_0_fun/ppermute | solution.py:453
  36.5 3.2 %branch_0_fun.5 = (bf16[1,128,1792]{2,1,0:T(8,128)(2,1)S(1)}, bf16[1,128,1792]{2,1,0:T(8,128)(2,1)S(1)}, bf16[1,128,1792]{2,1,0:T(8,128)(2,1)S(1)}, bf16[1,128,1792]{2,1,0:T(8,128)(2,1)S(1)}) custom-call(s32[1]{0:T(128)} %bitcast.place_ref, s32[8]{0:T(128)S(1)} %get-tuple-element.38.lengths_ref, bf16[1,128,1792]{2,1,0:T(8,128)(2,1)S(1)} %copy-done, ...), custom_call_target="tpu_custom_call" | custom-call | flops 1409286144 | bytes 4587520 | tf_op jit(solution)/shard_map/cond/branch_0_fun/pallas_call | solution.py:470
  39.8 1.3 %collective-permute-start.7 = (bf16[1,128,1792]{2,1,0:T(8,128)(2,1)S(1)}, bf16[1,128,1792]{2,1,0:T(8,128)(2,1)S(1)}, u32[]{:S(2)}, u32[]{:S(2)}) collective-permute-start(bf16[1,128,1792]{2,1,0:T(8,128)(2,1)S(1)} %get-tuple-element.51), channel_id=1, source_target_pairs={{8,0},{12,4},{16,8},{20,12},{24,16},{28,20},{9,1},{13,5},{17,9},{2... | collective-permute-start | bytes 1376264 | tf_op jit(solution)/shard_map/cond/branch_0_fun/ppermute | solution.py:453
  41.1 1.3 %collective-permute-start.6 = (bf16[1,128,1792]{2,1,0:T(8,128)(2,1)S(1)}, bf16[1,128,1792]{2,1,0:T(8,128)(2,1)S(1)}, u32[]{:S(2)}, u32[]{:S(2)}) collective-permute-start(bf16[1,128,1792]{2,1,0:T(8,128)(2,1)S(1)} %get-tuple-element.49), channel_id=1, source_target_pairs={{0,4},{4,0},{8,12},{12,8},{16,20},{20,16},{24,28},{28,24},{1,5},{5... | collective-permute-start | bytes 1376264 | tf_op jit(solution)/shard_map/cond/branch_0_fun/ppermute | solution.py:453
  42.4 4.9 %collective-permute-done.8 = bf16[1,128,1792]{2,1,0:T(8,128)(2,1)S(1)} collective-permute-done((bf16[1,128,1792]{2,1,0:T(8,128)(2,1)S(1)}, bf16[1,128,1792]{2,1,0:T(8,128)(2,1)S(1)}, u32[]{:S(2)}, u32[]{:S(2)}) %collective-permute-start.8) | collective-permute-done | bytes 458784 | tf_op jit(solution)/shard_map/cond/branch_0_fun/ppermute | solution.py:453
  47.2 0.9 %convert_add_fusion = bf16[1,128,1792]{2,1,0:T(8,128)(2,1)} fusion(bf16[1,128,1792]{2,1,0:T(8,128)(2,1)S(1)} %collective-permute-done.8, bf16[1,128,1792]{2,1,0:T(8,128)(2,1)S(1)} %get-tuple-element.52), kind=kLoop, calls=%fused_computation | loop fusion | flops 917504 | bytes 1376256 | tf_op jit(solution)/shard_map/cond/branch_0_fun/add | solution.py:509
  48.1 6.8 %collective-permute-done.7 = bf16[1,128,1792]{2,1,0:T(8,128)(2,1)S(1)} collective-permute-done((bf16[1,128,1792]{2,1,0:T(8,128)(2,1)S(1)}, bf16[1,128,1792]{2,1,0:T(8,128)(2,1)S(1)}, u32[]{:S(2)}, u32[]{:S(2)}) %collective-permute-start.7) | collective-permute-done | bytes 458784 | tf_op jit(solution)/shard_map/cond/branch_0_fun/ppermute | solution.py:453
  55.0 0.9 %convert_add_fusion.1 = bf16[1,128,1792]{2,1,0:T(8,128)(2,1)} fusion(bf16[1,128,1792]{2,1,0:T(8,128)(2,1)S(1)} %collective-permute-done.7, bf16[1,128,1792]{2,1,0:T(8,128)(2,1)S(1)} %get-tuple-element.50), kind=kLoop, calls=%fused_computation.1 | loop fusion | flops 917504 | bytes 1376256 | tf_op jit(solution)/shard_map/cond/branch_0_fun/add | solution.py:509
  55.8 0.9 %convert_add_fusion.2 = bf16[1,128,1792]{2,1,0:T(8,128)(2,1)} fusion(bf16[1,128,1792]{2,1,0:T(8,128)(2,1)S(1)} %collective-permute-done.6, bf16[1,128,1792]{2,1,0:T(8,128)(2,1)S(1)} %get-tuple-element.48), kind=kLoop, calls=%fused_computation.2 | loop fusion | flops 917504 | bytes 1376256 | tf_op jit(solution)/shard_map/cond/branch_0_fun/add | solution.py:509
  (9 shorter events, 0.6 us)
Async XLA Ops:
  0.6 0.8 %copy-start.4 = (s32[8]{0:T(128)S(1)}, s32[8]{0:T(128)}, u32[]{:S(2)}) copy-start(s32[8]{0:T(128)} %param.11) | copy-start | bytes 100
  2.8 14.6 %collective-permute-start = (bf16[1,128,1792]{2,1,0:T(8,128)(2,1)}, bf16[1,128,1792]{2,1,0:T(8,128)(2,1)S(1)}, u32[]{:S(2)}, u32[]{:S(2)}) collective-permute-start(bf16[1,128,1792]{2,1,0:T(8,128)(2,1)} %get-tuple-element.39.refs_0_), channel_id=1, source_target_pairs={{0,4},{4,0},{8,12},{12,8},{16,20},{20,16},{24,28},{28,24},{1,5},{5... | collective-permute-start | bytes 1376264 | tf_op jit(solution)/shard_map/cond/branch_0_fun/ppermute | solution.py:453
  5.8 14.7 %collective-permute-start.1 = (bf16[1,128,1792]{2,1,0:T(8,128)(2,1)}, bf16[1,128,1792]{2,1,0:T(8,128)(2,1)S(1)}, u32[]{:S(2)}, u32[]{:S(2)}) collective-permute-start(bf16[1,128,1792]{2,1,0:T(8,128)(2,1)} %get-tuple-element.40.refs_2_.refs_4_), channel_id=1, source_target_pairs={{0,8},{4,12},{8,16},{12,20},{16,24},{20,28},{1,9},{5,13},{9,17},{1... | collective-permute-start | bytes 1376264 | tf_op jit(solution)/shard_map/cond/branch_0_fun/ppermute | solution.py:453
  9.3 17.2 %collective-permute-start.2 = (bf16[1,128,1792]{2,1,0:T(8,128)(2,1)}, bf16[1,128,1792]{2,1,0:T(8,128)(2,1)S(1)}, u32[]{:S(2)}, u32[]{:S(2)}) collective-permute-start(bf16[1,128,1792]{2,1,0:T(8,128)(2,1)} %get-tuple-element.41.refs_4_), channel_id=1, source_target_pairs={{0,4},{4,0},{8,12},{12,8},{16,20},{20,16},{24,28},{28,24},{1,5},{5... | collective-permute-start | bytes 1376264 | tf_op jit(solution)/shard_map/cond/branch_0_fun/ppermute | solution.py:453
  9.9 19.0 %collective-permute-start.3 = (bf16[1,128,1792]{2,1,0:T(8,128)(2,1)}, bf16[1,128,1792]{2,1,0:T(8,128)(2,1)S(1)}, u32[]{:S(2)}, u32[]{:S(2)}) collective-permute-start(bf16[1,128,1792]{2,1,0:T(8,128)(2,1)} %get-tuple-element.42.refs_5_), channel_id=1, source_target_pairs={{0,8},{4,12},{8,16},{12,20},{16,24},{20,28},{1,9},{5,13},{9,17},{1... | collective-permute-start | bytes 1376264 | tf_op jit(solution)/shard_map/cond/branch_0_fun/ppermute | solution.py:453
  20.5 8.4 %copy-start = (bf16[1,128,1792]{2,1,0:T(8,128)(2,1)S(1)}, bf16[1,128,1792]{2,1,0:T(8,128)(2,1)}, u32[]{:S(2)}) copy-start(bf16[1,128,1792]{2,1,0:T(8,128)(2,1)} %get-tuple-element.39.refs_0_) | copy-start | bytes 1376260
  20.5 8.4 %copy-start.2 = (bf16[1,128,1792]{2,1,0:T(8,128)(2,1)S(1)}, bf16[1,128,1792]{2,1,0:T(8,128)(2,1)}, u32[]{:S(2)}) copy-start(bf16[1,128,1792]{2,1,0:T(8,128)(2,1)} %get-tuple-element.40.refs_2_.refs_4_) | copy-start | bytes 1376260
  23.2 5.7 %collective-permute-start.4 = (f32[32,128]{1,0:T(8,128)S(1)}, f32[32,128]{1,0:T(8,128)S(1)}, u32[]{:S(2)}, u32[]{:S(2)}) collective-permute-start(f32[32,128]{1,0:T(8,128)S(1)} %get-tuple-element.45.refs_8_), channel_id=1, source_target_pairs={{0,4},{4,0},{8,12},{12,8},{16,20},{20,16},{24,28},{28,24},{1,5},{5... | collective-permute-start | bytes 49160 | tf_op jit(solution)/shard_map/cond/branch_0_fun/ppermute | solution.py:453
  31.5 15.7 %collective-permute-start.8 = (bf16[1,128,1792]{2,1,0:T(8,128)(2,1)S(1)}, bf16[1,128,1792]{2,1,0:T(8,128)(2,1)S(1)}, u32[]{:S(2)}, u32[]{:S(2)}) collective-permute-start(bf16[1,128,1792]{2,1,0:T(8,128)(2,1)S(1)} %get-tuple-element.53), channel_id=1, source_target_pairs={{8,0},{12,4},{16,8},{20,12},{24,16},{28,20},{9,1},{13,5},{17,9},{2... | collective-permute-start | bytes 1376264 | tf_op jit(solution)/shard_map/cond/branch_0_fun/ppermute | solution.py:453
  32.8 3.7 %collective-permute-start.5 = (f32[16,128]{1,0:T(8,128)S(1)}, f32[16,128]{1,0:T(8,128)S(1)}, u32[]{:S(2)}, u32[]{:S(2)}) collective-permute-start(f32[16,128]{1,0:T(8,128)S(1)} %get-tuple-element.47.refs_9_), channel_id=1, source_target_pairs={{0,4},{4,0},{8,12},{12,8},{16,20},{20,16},{24,28},{28,24},{1,5},{5... | collective-permute-start | bytes 24584 | tf_op jit(solution)/shard_map/cond/branch_0_fun/ppermute | solution.py:453
  39.8 15.2 %collective-permute-start.7 = (bf16[1,128,1792]{2,1,0:T(8,128)(2,1)S(1)}, bf16[1,128,1792]{2,1,0:T(8,128)(2,1)S(1)}, u32[]{:S(2)}, u32[]{:S(2)}) collective-permute-start(bf16[1,128,1792]{2,1,0:T(8,128)(2,1)S(1)} %get-tuple-element.51), channel_id=1, source_target_pairs={{8,0},{12,4},{16,8},{20,12},{24,16},{28,20},{9,1},{13,5},{17,9},{2... | collective-permute-start | bytes 1376264 | tf_op jit(solution)/shard_map/cond/branch_0_fun/ppermute | solution.py:453
  41.1 14.8 %collective-permute-start.6 = (bf16[1,128,1792]{2,1,0:T(8,128)(2,1)S(1)}, bf16[1,128,1792]{2,1,0:T(8,128)(2,1)S(1)}, u32[]{:S(2)}, u32[]{:S(2)}) collective-permute-start(bf16[1,128,1792]{2,1,0:T(8,128)(2,1)S(1)} %get-tuple-element.49), channel_id=1, source_target_pairs={{0,4},{4,0},{8,12},{12,8},{16,20},{20,16},{24,28},{28,24},{1,5},{5... | collective-permute-start | bytes 1376264 | tf_op jit(solution)/shard_map/cond/branch_0_fun/ppermute | solution.py:453
